TPU v7x, 32 devices: a whole 2x2x4 slice. The times are simulated.
32 devices in a mesh: tile: 16 (over z, x, core), mlp: 2 (over y).
Axes of the slice: x: 2, y: 2, z: 4, core: 2. Of those that a mesh axis runs over, the one named last changes fastest.
Arguments:
- features: bfloat16 [16, 512, 2, 2, 256], P('tile', 'mlp'), may hold values from -6 to 6
- w_in: bfloat16 [256, 1024], P(None, 'mlp'), may hold values from -0.375 to 0.375
- w_out: bfloat16 [1024, 256], P('mlp'), may hold values from -0.1875 to 0.1875
- bilinear: bfloat16 [256, 256], replicated, may hold values from -0.375 to 0.375
- partner: int32 [16, 2, 512], replicated, may hold values from 0 to 13823
- counts: int32 [16, 2, 2], replicated, may hold values from 128 to 512
Outputs:
- pair_loss: float32 [], replicated
- grad_in: float32 [256, 1024], P(None, 'mlp')
- grad_out: float32 [1024, 256], P('mlp')
- grad_bilinear: float32 [256, 256], replicated
All inputs are finite; a program needn't handle non-finite values.
Results may differ from a plain program's by a relative error of at most 0.0024.
The roundings to bfloat16 on the way count: a program that leaves them out, or rounds other values in their place, can miss the bound.
Values may be sent and summed in bfloat16 or wider, within the bound.
No kernel may reach another device: no remote copies, remote signals or barrier semaphores. Data moves between devices by JAX's collectives and lax.ppermute only.
A program may use at most 64 MiB of HBM per device.

v0:
```python
import jax
import jax.numpy as jnp
from jax import lax
from jax.sharding import PartitionSpec as P

column_plan = ((-1, 1), (0, 0), (0, 1), (1, 0))


def shifted(array, axis, by):
    peers = lax.axis_size(axis)
    pairs = [(i, i + by) for i in range(peers) if 0 <= i + by < peers]
    return lax.ppermute(array, axis, pairs)


def pair_slope(raw_score, target, weight, heavy_weight, factor):
    chance = jax.nn.sigmoid(raw_score)
    signed = (1.0 - target) * chance - heavy_weight * target * (1.0 - chance)
    return (weight * signed * factor).astype(jnp.bfloat16)


def pair_cost(raw_score, target, weight, heavy_weight):
    missed = heavy_weight * target * jnp.log1p(jnp.exp(-raw_score))
    spurious = (1.0 - target) * jnp.log1p(jnp.exp(raw_score))
    return jnp.sum(weight * (missed + spurious))


def local(features, w_in, w_out, bilinear, partner, counts):
    row_part = features.shape[1]
    feature_width = features.shape[4]
    groups = lax.axis_size("mlp")
    site_rows = row_part * groups
    tile_count = lax.axis_size("tile")
    grid_depth = tile_count // 8
    tile_here = lax.axis_index("tile")
    member = lax.axis_index("mlp")
    block_x = tile_here // (4 * grid_depth)
    block_y = tile_here // grid_depth % 4
    block_z = tile_here % grid_depth
    heavy_weight = 27 * site_rows // 4
    score_scale = feature_width ** (-0.5)
    factor = score_scale / (2 * tile_count * site_rows)
    own_rows = member * row_part + jnp.arange(row_part, dtype=jnp.int32)
    all_rows = jnp.arange(site_rows, dtype=jnp.int32)
    mine_counts = lax.dynamic_index_in_dim(counts, tile_here, 0, keepdims=False)
    mine_partner = lax.dynamic_index_in_dim(partner, tile_here, 0, keepdims=False)
    own_partner = lax.dynamic_slice_in_dim(mine_partner, member * row_part, row_part, 1)
    own_pre_ok = own_rows[None, :] < mine_counts[:, 0:1]
    own_post_ok = own_rows[None, :] < mine_counts[:, 1:2]
    local_x = features.reshape(row_part, 4, feature_width)
    whole_x = lax.all_gather(local_x, "mlp", axis=0, tiled=True)
    hidden_pre = jnp.einsum("rcf,fh->rch", whole_x, w_in, preferred_element_type=jnp.float32)
    active = jax.nn.gelu(hidden_pre).astype(jnp.bfloat16)
    mixed_rows = lax.psum_scatter(
        jnp.einsum("rch,hf->rcf", active, w_out, preferred_element_type=jnp.float32),
        "mlp",
        scatter_dimension=0,
        tiled=True,
    )
    embedded = (local_x.astype(jnp.float32) + mixed_rows).astype(jnp.bfloat16)
    pre_local = embedded[:, 0::2]
    post_local = embedded[:, 1::2]
    query_local = jnp.einsum(
        "ruf,fg->rug", pre_local, bilinear, preferred_element_type=jnp.float32
    ).astype(jnp.bfloat16)

    def pair_code(step_x, step_y, step_z):
        return ((step_x + 1) * 9 + (step_y + 1) * 3 + step_z + 1) * site_rows

    loss_sum = jnp.zeros((), jnp.float32)
    post_grads = [
        jnp.zeros((row_part, feature_width), jnp.float32),
        jnp.zeros((row_part, feature_width), jnp.float32),
    ]
    post_whole, query_whole = (
        lax.all_gather(post_local, "mlp", axis=0, tiled=True),
        lax.all_gather(query_local, "mlp", axis=0, tiled=True),
    )
    query_grads = [
        jnp.zeros((row_part, feature_width), jnp.float32),
        jnp.zeros((row_part, feature_width), jnp.float32),
    ]
    for step_y in (-1, 0, 1):
        for step_z in (-1, 0, 1):
            post_cols, query_cols, post_valid, pre_valid, label_cols = ([], [], [], [], [])
            for position in range(4):
                shift_x, sub_tile = column_plan[position]
                offset = shift_x * 4 * grid_depth + step_y * grid_depth + step_z
                inside = (
                    (block_x + shift_x >= 0)
                    & (block_x + shift_x < 2)
                    & (block_y + step_y >= 0)
                    & (block_y + step_y < 4)
                    & (block_z + step_z >= 0)
                    & (block_z + step_z < grid_depth)
                )
                source = jnp.clip(tile_here + offset, 0, tile_count - 1)
                tile_counts = lax.dynamic_index_in_dim(counts, source, 0, keepdims=False)[sub_tile]
                labels = lax.dynamic_index_in_dim(partner, source, 0, keepdims=False)[sub_tile]
                offset, sub_tile, inside, tile_counts, labels = (
                    offset,
                    sub_tile,
                    inside,
                    tile_counts,
                    labels,
                )
                both_sides = jnp.stack([post_whole[:, sub_tile], query_whole[:, sub_tile]], 0)
                if offset != 0:
                    both_sides = shifted(both_sides, "tile", -offset)
                post_cols.append(both_sides[0])
                query_cols.append(both_sides[1])
                post_valid.append(inside & (all_rows < tile_counts[1]))
                pre_valid.append(inside & (all_rows < tile_counts[0]))
                label_cols.append(labels)
            for pretile in (0, 1):
                chosen = range(pretile, pretile + 3)
                others = jnp.concatenate([post_cols[column_id] for column_id in chosen], 0)
                col_key = jnp.concatenate(
                    [
                        pair_code(column_id - 1 - pretile, step_y, step_z) + all_rows
                        for column_id in chosen
                    ]
                )
                col_ok = jnp.concatenate([post_valid[column_id] for column_id in chosen])
                raw_score = (
                    jnp.einsum(
                        "rf,cf->rc",
                        query_local[:, pretile],
                        others,
                        preferred_element_type=jnp.float32,
                    )
                    * score_scale
                )
                target = (own_partner[pretile][:, None] == col_key[None, :]).astype(jnp.float32)
                weight = (own_pre_ok[pretile][:, None] & col_ok[None, :]).astype(jnp.float32)
                loss_sum = loss_sum + pair_cost(raw_score, target, weight, heavy_weight)
                slope = pair_slope(raw_score, target, weight, heavy_weight, factor)
                query_grads[pretile] = query_grads[pretile] + jnp.dot(
                    slope, others, preferred_element_type=jnp.float32
                )
                senders = jnp.concatenate([query_cols[column_id] for column_id in chosen], 0)
                row_key = jnp.concatenate(
                    [
                        label_cols[column_id] - pair_code(pretile - column_id + 1, -step_y, -step_z)
                        for column_id in chosen
                    ]
                )
                row_ok = jnp.concatenate([pre_valid[column_id] for column_id in chosen])
                back_score = (
                    jnp.einsum(
                        "cf,rf->cr",
                        post_local[:, pretile],
                        senders,
                        preferred_element_type=jnp.float32,
                    )
                    * score_scale
                )
                back_target = (own_rows[:, None] == row_key[None, :]).astype(jnp.float32)
                back_weight = (own_post_ok[pretile][:, None] & row_ok[None, :]).astype(jnp.float32)
                back_slope = pair_slope(back_score, back_target, back_weight, heavy_weight, factor)
                post_grads[pretile] = post_grads[pretile] + jnp.dot(
                    back_slope, senders, preferred_element_type=jnp.float32
                )
    query_total = jnp.stack(query_grads, 1)
    query_back = query_total.astype(jnp.bfloat16)
    post_back = jnp.stack(post_grads, 1)
    bilinear_part = jnp.einsum(
        "ruf,rug->fg", pre_local, query_back, preferred_element_type=jnp.float32
    )
    pre_back = jnp.einsum("rug,fg->ruf", query_back, bilinear, preferred_element_type=jnp.float32)
    embed_grad = jnp.stack(
        [pre_back[:, 0], post_back[:, 0], pre_back[:, 1], post_back[:, 1]], 1
    ).astype(jnp.bfloat16)
    embed_whole = lax.all_gather(embed_grad, "mlp", axis=0, tiled=True)
    active_grad = jnp.einsum("rcf,hf->rch", embed_whole, w_out, preferred_element_type=jnp.float32)
    unused, pullback = jax.vjp(jax.nn.gelu, hidden_pre)
    hidden_grad = pullback(active_grad)[0].astype(jnp.bfloat16)
    in_part = jnp.einsum("rcf,rch->fh", whole_x, hidden_grad, preferred_element_type=jnp.float32)
    out_part = jnp.einsum("rch,rcf->hf", active, embed_whole, preferred_element_type=jnp.float32)
    grad_in, grad_out = lax.psum((in_part, out_part), "tile")
    grad_bilinear, loss_total = lax.psum((bilinear_part, loss_sum), ("tile", "mlp"))
    pair_loss = loss_total / (2.0 * tile_count * site_rows * 27 * site_rows)
    return (pair_loss, grad_in, grad_out, grad_bilinear)


def solution(mesh):
    placed = (P("tile", "mlp", None, None, None), P(None, "mlp"), P("mlp", None), P(), P(), P())
    return jax.shard_map(
        local,
        mesh=mesh,
        in_specs=placed,
        out_specs=(P(), P(None, "mlp"), P("mlp", None), P()),
        check_vma=False,
    )
```

profile of v0, /device:TPU:0, one launch (start us, length us, event | category | flops | bytes accessed | tf_op | source)
XLA Modules:
  0.0 785.0 jit_solution(13970447617277279155)
XLA Ops:
  73.8 20.3 %reduce-scatter.2.cloned.1.call-done = f32[256,4,256]{2,0,1:T(8,128)} async-done(((f32[512,4,256]{2,0,1:T(8,128)}), f32[256,4,256]{2,0,1:T(8,128)}) %reduce-scatter.2.cloned.1.call-update) | async-done | bytes 1048592 | tf_op jit(solution)/shard_map/reduce_scatter | solution.py:53
  95.8 8.7 %all_gather.14 = bf16[512,2,256]{2,0,1:T(8,128)(2,1)S(1)} all-gather(bf16[256,2,256]{2,0,1:T(8,128)(2,1)S(1)} %convolution_convert_fusion.1), channel_id=1, replica_groups=mesh['tile'=16,'mlp'=2] {'mlp'}, dimensions={0}, use_global_device_ids=true | all-gather | bytes 786432 | tf_op jit(solution)/shard_map/all_gather | solution.py:76
  104.5 7.8 all_gather.13
  115.1 6.1 collective-permute-start.8
  123.2 5.2 collective-permute-start.22
  131.0 9.0 %collective-permute-start.4 = (bf16[2,512,256]{2,1,0:T(8,128)(2,1)S(1)}, bf16[2,512,256]{2,1,0:T(8,128)(2,1)S(1)}, u32[]{:S(2)}, u32[]{:S(2)}) collective-permute-start(bf16[2,512,256]{2,1,0:T(8,128)(2,1)S(1)} %pad_maximum_fusion.18), channel_id=1, source_target_pairs={{0,20},{2,22},{4,24},{6,26},{8,28},{10,30},{1,21},{3,23},{5,25},{7... | collective-permute-start | bytes 1572872 | tf_op jit(solution)/shard_map/ppermute | solution.py:12
  141.4 10.2 %collective-permute-done.6 = bf16[2,512,256]{2,1,0:T(8,128)(2,1)S(1)} collective-permute-done((bf16[2,512,256]{2,1,0:T(8,128)(2,1)S(1)}, bf16[2,512,256]{2,1,0:T(8,128)(2,1)S(1)}, u32[]{:S(2)}, u32[]{:S(2)}) %collective-permute-start.6) | collective-permute-done | bytes 524320 | tf_op jit(solution)/shard_map/ppermute | solution.py:12
  157.2 21.1 %collective-permute-start.5 = (bf16[2,512,256]{2,1,0:T(8,128)(2,1)S(1)}, bf16[2,512,256]{2,1,0:T(8,128)(2,1)S(1)}, u32[]{:S(2)}, u32[]{:S(2)}) collective-permute-start(bf16[2,512,256]{2,1,0:T(8,128)(2,1)S(1)} %pad_maximum_fusion.19), channel_id=1, source_target_pairs={{0,4},{2,6},{4,8},{6,10},{8,12},{10,14},{12,16},{14,18},{16,20},{1... | collective-permute-start | bytes 1572872 | tf_op jit(solution)/shard_map/ppermute | solution.py:12
  180.2 26.0 %collective-permute-done.5 = bf16[2,512,256]{2,1,0:T(8,128)(2,1)S(1)} collective-permute-done((bf16[2,512,256]{2,1,0:T(8,128)(2,1)S(1)}, bf16[2,512,256]{2,1,0:T(8,128)(2,1)S(1)}, u32[]{:S(2)}, u32[]{:S(2)}) %collective-permute-start.5) | collective-permute-done | bytes 524320 | tf_op jit(solution)/shard_map/ppermute | solution.py:12
  209.0 24.9 %collective-permute-done.7 = bf16[2,512,256]{2,1,0:T(8,128)(2,1)S(1)} collective-permute-done((bf16[2,512,256]{2,1,0:T(8,128)(2,1)S(1)}, bf16[2,512,256]{2,1,0:T(8,128)(2,1)S(1)}, u32[]{:S(2)}, u32[]{:S(2)}) %collective-permute-start.7) | collective-permute-done | bytes 524320 | tf_op jit(solution)/shard_map/ppermute | solution.py:12
  235.6 9.2 %fusion.72 = (f32[]{:T(128)}, f32[]{:T(128)}, f32[]{:T(128)}, f32[]{:T(128)}, f32[]{:T(128)}, /*index=5*/f32[]{:T(128)}, f32[256,1536]{1,0:T(8,128)S(1)}) fusion(s32[1536]{0:T(1024)S(1)} %pad_add_fusion.1, pred[1536]{0:T(1024)(128)(4,1)S(1)} %get-tuple-element.258, s32[256]{0:T(256)S(1)} %bitcast.374, pred[256]{0:T(512)(128)(4,1)S(1)} %get-tuple-element.50, ...), kind=kOutput, calls=%fused_computation.229 | convolution fusion | flops 229244928 | bytes 7248920 | tf_op jit(solution)/shard_map/rf,cf->rc/dot_general | solution.py:125
  244.8 5.6 collective-permute-start.18
  250.4 6.1 collective-permute-done.17
  261.7 8.9 %collective-permute-start.14 = (bf16[2,512,256]{2,1,0:T(8,128)(2,1)S(1)}, bf16[2,512,256]{2,1,0:T(8,128)(2,1)S(1)}, u32[]{:S(2)}, u32[]{:S(2)}) collective-permute-start(bf16[2,512,256]{2,1,0:T(8,128)(2,1)S(1)} %pad_maximum_fusion.18), channel_id=1, source_target_pairs={{0,14},{2,16},{4,18},{6,20},{8,22},{10,24},{12,26},{14,28},{16,30}... | collective-permute-start | bytes 1572872 | tf_op jit(solution)/shard_map/ppermute | solution.py:12
  272.9 9.0 %collective-permute-done.14 = bf16[2,512,256]{2,1,0:T(8,128)(2,1)S(1)} collective-permute-done((bf16[2,512,256]{2,1,0:T(8,128)(2,1)S(1)}, bf16[2,512,256]{2,1,0:T(8,128)(2,1)S(1)}, u32[]{:S(2)}, u32[]{:S(2)}) %collective-permute-start.14) | collective-permute-done | bytes 524320 | tf_op jit(solution)/shard_map/ppermute | solution.py:12
  289.8 31.0 %collective-permute-start = (bf16[2,512,256]{2,1,0:T(8,128)(2,1)S(1)}, bf16[2,512,256]{2,1,0:T(8,128)(2,1)S(1)}, u32[]{:S(2)}, u32[]{:S(2)}) collective-permute-start(bf16[2,512,256]{2,1,0:T(8,128)(2,1)S(1)} %pad_maximum_fusion.18), channel_id=1, source_target_pairs={{0,22},{2,24},{4,26},{6,28},{8,30},{1,23},{3,25},{5,27},{7,29},{9,... | collective-permute-start | bytes 1572872 | tf_op jit(solution)/shard_map/ppermute | solution.py:12
  321.9 4.4 collective-permute-start.1
  327.4 5.6 collective-permute-done.1
  335.8 12.6 %collective-permute-done.3 = bf16[2,512,256]{2,1,0:T(8,128)(2,1)S(1)} collective-permute-done((bf16[2,512,256]{2,1,0:T(8,128)(2,1)S(1)}, bf16[2,512,256]{2,1,0:T(8,128)(2,1)S(1)}, u32[]{:S(2)}, u32[]{:S(2)}) %collective-permute-start.3) | collective-permute-done | bytes 524320 | tf_op jit(solution)/shard_map/ppermute | solution.py:12
  348.4 10.7 %collective-permute-start.12 = (bf16[2,512,256]{2,1,0:T(8,128)(2,1)S(1)}, bf16[2,512,256]{2,1,0:T(8,128)(2,1)S(1)}, u32[]{:S(2)}, u32[]{:S(2)}) collective-permute-start(bf16[2,512,256]{2,1,0:T(8,128)(2,1)S(1)} %pad_maximum_fusion.18), channel_id=1, source_target_pairs={{0,16},{2,18},{4,20},{6,22},{8,24},{10,26},{12,28},{14,30},{1,17},... | collective-permute-start | bytes 1572872 | tf_op jit(solution)/shard_map/ppermute | solution.py:12
  359.8 9.2 %fusion.66 = (f32[]{:T(128)}, f32[]{:T(128)}, f32[]{:T(128)}, f32[]{:T(128)}, f32[]{:T(128)}, /*index=5*/f32[]{:T(128)}, f32[256,1536]{1,0:T(8,128)S(1)}) fusion(s32[1536]{0:T(1024)S(1)} %pad_add_fusion, pred[1536]{0:T(1024)(128)(4,1)S(1)} %get-tuple-element.264, s32[256]{0:T(256)S(1)} %bitcast.376, pred[256]{0:T(512)(128)(4,1)S(1)} %get-tuple-element.50, ...), kind=kOutput, calls=%fused_computation.223 | convolution fusion | flops 229244928 | bytes 7248920 | tf_op jit(solution)/shard_map/rf,cf->rc/dot_general | solution.py:125
  374.2 24.0 %collective-permute-done.21 = bf16[2,512,256]{2,1,0:T(8,128)(2,1)S(1)} collective-permute-done((bf16[2,512,256]{2,1,0:T(8,128)(2,1)S(1)}, bf16[2,512,256]{2,1,0:T(8,128)(2,1)S(1)}, u32[]{:S(2)}, u32[]{:S(2)}) %collective-permute-start.21) | collective-permute-done | bytes 524320 | tf_op jit(solution)/shard_map/ppermute | solution.py:12
  401.7 12.3 %collective-permute-done.19 = bf16[2,512,256]{2,1,0:T(8,128)(2,1)S(1)} collective-permute-done((bf16[2,512,256]{2,1,0:T(8,128)(2,1)S(1)}, bf16[2,512,256]{2,1,0:T(8,128)(2,1)S(1)}, u32[]{:S(2)}, u32[]{:S(2)}) %collective-permute-start.19) | collective-permute-done | bytes 524320 | tf_op jit(solution)/shard_map/ppermute | solution.py:12
  426.3 20.7 %collective-permute-done.25 = bf16[2,512,256]{2,1,0:T(8,128)(2,1)S(1)} collective-permute-done((bf16[2,512,256]{2,1,0:T(8,128)(2,1)S(1)}, bf16[2,512,256]{2,1,0:T(8,128)(2,1)S(1)}, u32[]{:S(2)}, u32[]{:S(2)}) %collective-permute-start.25) | collective-permute-done | bytes 524320 | tf_op jit(solution)/shard_map/ppermute | solution.py:12
  453.8 8.6 %collective-permute-done.13 = bf16[2,512,256]{2,1,0:T(8,128)(2,1)S(1)} collective-permute-done((bf16[2,512,256]{2,1,0:T(8,128)(2,1)S(1)}, bf16[2,512,256]{2,1,0:T(8,128)(2,1)S(1)}, u32[]{:S(2)}, u32[]{:S(2)}) %collective-permute-start.13) | collective-permute-done | bytes 524320 | tf_op jit(solution)/shard_map/ppermute | solution.py:12
  463.2 12.3 %fusion.90 = (f32[]{:T(128)}, f32[]{:T(128)}, f32[]{:T(128)}, f32[]{:T(128)}, f32[]{:T(128)}, /*index=5*/f32[]{:T(128)}, f32[256,1536]{1,0:T(8,128)S(1)}) fusion(s32[1536]{0:T(1024)S(1)} %copy-done.45, pred[1536]{0:T(1024)(128)(4,1)S(1)} %copy-done.70, s32[256]{0:T(256)S(1)} %bitcast.380, pred[256]{0:T(512)(128)(4,1)S(1)} %copy-done.87, ...), kind=kOutput, calls=%fused_computation.247 | convolution fusion | flops 230031360 | bytes 10394648 | tf_op jit(solution)/shard_map/rf,cf->rc/dot_general | solution.py:125
  519.8 17.6 %all-gather.5.cloned.1.call-done = bf16[512,4,256]{2,0,1:T(8,128)(2,1)} async-done(((bf16[256,4,256]{2,0,1:T(8,128)(2,1)}), bf16[512,4,256]{2,0,1:T(8,128)(2,1)}) %all-gather.5.cloned.1.call-update) | async-done | bytes 1048592 | tf_op jit(solution)/shard_map/all_gather | solution.py:173
  537.5 6.8 fusion.334
  544.3 4.5 convolution_bitcast_fusion
  561.1 39.4 %psum.28 = f32[]{:T(128)} all-reduce(f32[]{:T(128)S(6)} %add.942), channel_id=1, replica_groups=mesh['tile'=16,'mlp'=2] {'tile','mlp'}, use_global_device_ids=true, to_apply=%region_19.20 | all-reduce | flops 1 | bytes 8 | tf_op jit(solution)/shard_map/psum | solution.py:180
  601.1 41.4 %all-reduce.6.cloned.1.call-done = (f32[256,512]{0,1:T(8,128)}, f32[512,256]{1,0:T(8,128)}) async-done(((f32[256,512]{0,1:T(8,128)}, f32[512,256]{1,0:T(8,128)}), (f32[256,512]{0,1:T(8,128)}, f32[512,256]{1,0:T(8,128)})) %all-reduce.6.cloned.1.call-update) | async-done | bytes 1048592 | tf_op jit(solution)/shard_map/psum | solution.py:179
  644.6 129.1 %all-reduce.4.cloned.1.call-done = f32[256,256]{1,0:T(8,128)} async-done(((f32[256,256]{1,0:T(8,128)}), f32[256,256]{1,0:T(8,128)}) %all-reduce.4.cloned.1.call-update) | async-done | bytes 262160 | tf_op jit(solution)/shard_map/psum | solution.py:180
  (461 shorter events, 187.3 us)
Async XLA Ops:
  7.2 45.3 %all-gather.3.cloned.1.call-start = ((), (), s32[]{:S(2)}) async-start(), calls=%async_computation.1 | async-start | bytes 1572864 | tf_op jit(solution)/shard_map/all_gather | solution.py:50
  9.2 85.0 %reduce-scatter.2.cloned.1.call-start = ((), (), s32[]{:S(2)}) async-start(), calls=%async_computation.2 | async-start | bytes 3145728 | tf_op jit(solution)/shard_map/reduce_scatter | solution.py:53
  59.5 478.0 %all-gather.5.cloned.1.call-start = ((), (), s32[]{:S(2)}) async-start(), calls=%async_computation.3 | async-start | bytes 1572864 | tf_op jit(solution)/shard_map/all_gather | solution.py:173
  61.7 361.6 %copy-start.72 = (pred[1536]{0:T(1024)(128)(4,1)}, pred[1536]{0:T(1024)(128)(4,1)S(1)}, u32[]{:S(2)}) copy-start(pred[1536]{0:T(1024)(128)(4,1)S(1)} %get-tuple-element.251) | copy-start | bytes 4612
  112.6 18.4 %collective-permute-start.10 = (bf16[2,512,256]{2,1,0:T(8,128)(2,1)S(1)}, bf16[2,512,256]{2,1,0:T(8,128)(2,1)S(1)}, u32[]{:S(2)}, u32[]{:S(2)}) collective-permute-start(bf16[2,512,256]{2,1,0:T(8,128)(2,1)S(1)} %pad_maximum_fusion.18), channel_id=1, source_target_pairs={{0,2},{2,4},{4,6},{6,8},{8,10},{10,12},{12,14},{14,16},{16,18},{18... | collective-permute-start | bytes 1572872 | tf_op jit(solution)/shard_map/ppermute | solution.py:12
  115.1 25.0 %collective-permute-start.8 = (bf16[2,512,256]{2,1,0:T(8,128)(2,1)S(1)}, bf16[2,512,256]{2,1,0:T(8,128)(2,1)S(1)}, u32[]{:S(2)}, u32[]{:S(2)}) collective-permute-start(bf16[2,512,256]{2,1,0:T(8,128)(2,1)S(1)} %pad_maximum_fusion.18), channel_id=1, source_target_pairs={{0,18},{2,20},{4,22},{6,24},{8,26},{10,28},{12,30},{1,19},{3,21},{... | collective-permute-start | bytes 1572872 | tf_op jit(solution)/shard_map/ppermute | solution.py:12
  121.9 302.6 %collective-permute-start.24 = (bf16[2,512,256]{2,1,0:T(8,128)(2,1)S(1)}, bf16[2,512,256]{2,1,0:T(8,128)(2,1)S(1)}, u32[]{:S(2)}, u32[]{:S(2)}) collective-permute-start(bf16[2,512,256]{2,1,0:T(8,128)(2,1)S(1)} %pad_maximum_fusion.18), channel_id=1, source_target_pairs={{6,0},{8,2},{10,4},{12,6},{14,8},{16,10},{18,12},{20,14},{22,16},{... | collective-permute-start | bytes 1572872 | tf_op jit(solution)/shard_map/ppermute | solution.py:12
  123.2 328.1 %collective-permute-start.22 = (bf16[2,512,256]{2,1,0:T(8,128)(2,1)S(1)}, bf16[2,512,256]{2,1,0:T(8,128)(2,1)S(1)}, u32[]{:S(2)}, u32[]{:S(2)}) collective-permute-start(bf16[2,512,256]{2,1,0:T(8,128)(2,1)S(1)} %pad_maximum_fusion.18), channel_id=1, source_target_pairs={{0,10},{2,12},{4,14},{6,16},{8,18},{10,20},{12,22},{14,24},{16,26}... | collective-permute-start | bytes 1572872 | tf_op jit(solution)/shard_map/ppermute | solution.py:12
  128.4 23.2 %collective-permute-start.6 = (bf16[2,512,256]{2,1,0:T(8,128)(2,1)S(1)}, bf16[2,512,256]{2,1,0:T(8,128)(2,1)S(1)}, u32[]{:S(2)}, u32[]{:S(2)}) collective-permute-start(bf16[2,512,256]{2,1,0:T(8,128)(2,1)S(1)} %pad_maximum_fusion.18), channel_id=1, source_target_pairs={{0,4},{2,6},{4,8},{6,10},{8,12},{10,14},{12,16},{14,18},{16,20},{1... | collective-permute-start | bytes 1572872 | tf_op jit(solution)/shard_map/ppermute | solution.py:12
  131.0 24.2 %collective-permute-start.4 = (bf16[2,512,256]{2,1,0:T(8,128)(2,1)S(1)}, bf16[2,512,256]{2,1,0:T(8,128)(2,1)S(1)}, u32[]{:S(2)}, u32[]{:S(2)}) collective-permute-start(bf16[2,512,256]{2,1,0:T(8,128)(2,1)S(1)} %pad_maximum_fusion.18), channel_id=1, source_target_pairs={{0,20},{2,22},{4,24},{6,26},{8,28},{10,30},{1,21},{3,23},{5,25},{7... | collective-permute-start | bytes 1572872 | tf_op jit(solution)/shard_map/ppermute | solution.py:12
  140.1 17.2 %collective-permute-start.11 = (bf16[2,512,256]{2,1,0:T(8,128)(2,1)S(1)}, bf16[2,512,256]{2,1,0:T(8,128)(2,1)S(1)}, u32[]{:S(2)}, u32[]{:S(2)}) collective-permute-start(bf16[2,512,256]{2,1,0:T(8,128)(2,1)S(1)} %pad_maximum_fusion.19), channel_id=1, source_target_pairs={{14,0},{16,2},{18,4},{20,6},{22,8},{24,10},{26,12},{28,14},{30,16}... | collective-permute-start | bytes 1572872 | tf_op jit(solution)/shard_map/ppermute | solution.py:12
  151.6 26.8 %collective-permute-start.9 = (bf16[2,512,256]{2,1,0:T(8,128)(2,1)S(1)}, bf16[2,512,256]{2,1,0:T(8,128)(2,1)S(1)}, u32[]{:S(2)}, u32[]{:S(2)}) collective-permute-start(bf16[2,512,256]{2,1,0:T(8,128)(2,1)S(1)} %pad_maximum_fusion.19), channel_id=1, source_target_pairs={{0,2},{2,4},{4,6},{6,8},{8,10},{10,12},{12,14},{14,16},{16,18},{18... | collective-permute-start | bytes 1572872 | tf_op jit(solution)/shard_map/ppermute | solution.py:12
  155.2 216.7 %collective-permute-start.20 = (bf16[2,512,256]{2,1,0:T(8,128)(2,1)S(1)}, bf16[2,512,256]{2,1,0:T(8,128)(2,1)S(1)}, u32[]{:S(2)}, u32[]{:S(2)}) collective-permute-start(bf16[2,512,256]{2,1,0:T(8,128)(2,1)S(1)} %pad_maximum_fusion.18), channel_id=1, source_target_pairs={{4,0},{6,2},{8,4},{10,6},{12,8},{14,10},{16,12},{18,14},{20,16},{2... | collective-permute-start | bytes 1572872 | tf_op jit(solution)/shard_map/ppermute | solution.py:12
  157.2 48.9 %collective-permute-start.5 = (bf16[2,512,256]{2,1,0:T(8,128)(2,1)S(1)}, bf16[2,512,256]{2,1,0:T(8,128)(2,1)S(1)}, u32[]{:S(2)}, u32[]{:S(2)}) collective-permute-start(bf16[2,512,256]{2,1,0:T(8,128)(2,1)S(1)} %pad_maximum_fusion.19), channel_id=1, source_target_pairs={{0,4},{2,6},{4,8},{6,10},{8,12},{10,14},{12,16},{14,18},{16,20},{1... | collective-permute-start | bytes 1572872 | tf_op jit(solution)/shard_map/ppermute | solution.py:12
  178.5 66.4 %collective-permute-start.16 = (bf16[2,512,256]{2,1,0:T(8,128)(2,1)S(1)}, bf16[2,512,256]{2,1,0:T(8,128)(2,1)S(1)}, u32[]{:S(2)}, u32[]{:S(2)}) collective-permute-start(bf16[2,512,256]{2,1,0:T(8,128)(2,1)S(1)} %pad_maximum_fusion.18), channel_id=1, source_target_pairs={{2,0},{4,2},{6,4},{8,6},{10,8},{12,10},{14,12},{16,14},{18,16},{20... | collective-permute-start | bytes 1572872 | tf_op jit(solution)/shard_map/ppermute | solution.py:12
  206.2 27.7 %collective-permute-start.7 = (bf16[2,512,256]{2,1,0:T(8,128)(2,1)S(1)}, bf16[2,512,256]{2,1,0:T(8,128)(2,1)S(1)}, u32[]{:S(2)}, u32[]{:S(2)}) collective-permute-start(bf16[2,512,256]{2,1,0:T(8,128)(2,1)S(1)} %pad_maximum_fusion.19), channel_id=1, source_target_pairs={{12,0},{14,2},{16,4},{18,6},{20,8},{22,10},{24,12},{26,14},{28,16}... | collective-permute-start | bytes 1572872 | tf_op jit(solution)/shard_map/ppermute | solution.py:12
  233.9 22.6 %collective-permute-start.17 = (bf16[2,512,256]{2,1,0:T(8,128)(2,1)S(1)}, bf16[2,512,256]{2,1,0:T(8,128)(2,1)S(1)}, u32[]{:S(2)}, u32[]{:S(2)}) collective-permute-start(bf16[2,512,256]{2,1,0:T(8,128)(2,1)S(1)} %pad_maximum_fusion.19), channel_id=1, source_target_pairs={{18,0},{20,2},{22,4},{24,6},{26,8},{28,10},{30,12},{19,1},{21,3},{... | collective-permute-start | bytes 1572872 | tf_op jit(solution)/shard_map/ppermute | solution.py:12
  244.8 172.6 %collective-permute-start.18 = (bf16[2,512,256]{2,1,0:T(8,128)(2,1)S(1)}, bf16[2,512,256]{2,1,0:T(8,128)(2,1)S(1)}, u32[]{:S(2)}, u32[]{:S(2)}) collective-permute-start(bf16[2,512,256]{2,1,0:T(8,128)(2,1)S(1)} %pad_maximum_fusion.18), channel_id=1, source_target_pairs={{0,12},{2,14},{4,16},{6,18},{8,20},{10,22},{12,24},{14,26},{16,28}... | collective-permute-start | bytes 1572872 | tf_op jit(solution)/shard_map/ppermute | solution.py:12
  256.6 5.2 collective-permute-start.15
  261.7 20.1 %collective-permute-start.14 = (bf16[2,512,256]{2,1,0:T(8,128)(2,1)S(1)}, bf16[2,512,256]{2,1,0:T(8,128)(2,1)S(1)}, u32[]{:S(2)}, u32[]{:S(2)}) collective-permute-start(bf16[2,512,256]{2,1,0:T(8,128)(2,1)S(1)} %pad_maximum_fusion.18), channel_id=1, source_target_pairs={{0,14},{2,16},{4,18},{6,20},{8,22},{10,24},{12,26},{14,28},{16,30}... | collective-permute-start | bytes 1572872 | tf_op jit(solution)/shard_map/ppermute | solution.py:12
  281.9 8.0 %collective-permute-start.2 = (bf16[2,512,256]{2,1,0:T(8,128)(2,1)S(1)}, bf16[2,512,256]{2,1,0:T(8,128)(2,1)S(1)}, u32[]{:S(2)}, u32[]{:S(2)}) collective-permute-start(bf16[2,512,256]{2,1,0:T(8,128)(2,1)S(1)} %pad_maximum_fusion.18), channel_id=1, source_target_pairs={{0,6},{2,8},{4,10},{6,12},{8,14},{10,16},{12,18},{14,20},{16,22},{... | collective-permute-start | bytes 1572872 | tf_op jit(solution)/shard_map/ppermute | solution.py:12
  289.8 32.1 %collective-permute-start = (bf16[2,512,256]{2,1,0:T(8,128)(2,1)S(1)}, bf16[2,512,256]{2,1,0:T(8,128)(2,1)S(1)}, u32[]{:S(2)}, u32[]{:S(2)}) collective-permute-start(bf16[2,512,256]{2,1,0:T(8,128)(2,1)S(1)} %pad_maximum_fusion.18), channel_id=1, source_target_pairs={{0,22},{2,24},{4,26},{6,28},{8,30},{1,23},{3,25},{5,27},{7,29},{9,... | collective-permute-start | bytes 1572872 | tf_op jit(solution)/shard_map/ppermute | solution.py:12
  321.9 11.1 %collective-permute-start.1 = (bf16[2,512,256]{2,1,0:T(8,128)(2,1)S(1)}, bf16[2,512,256]{2,1,0:T(8,128)(2,1)S(1)}, u32[]{:S(2)}, u32[]{:S(2)}) collective-permute-start(bf16[2,512,256]{2,1,0:T(8,128)(2,1)S(1)} %pad_maximum_fusion.19), channel_id=1, source_target_pairs={{0,6},{2,8},{4,10},{6,12},{8,14},{10,16},{12,18},{14,20},{16,22},{... | collective-permute-start | bytes 1572872 | tf_op jit(solution)/shard_map/ppermute | solution.py:12
  333.0 15.4 %collective-permute-start.3 = (bf16[2,512,256]{2,1,0:T(8,128)(2,1)S(1)}, bf16[2,512,256]{2,1,0:T(8,128)(2,1)S(1)}, u32[]{:S(2)}, u32[]{:S(2)}) collective-permute-start(bf16[2,512,256]{2,1,0:T(8,128)(2,1)S(1)} %pad_maximum_fusion.19), channel_id=1, source_target_pairs={{10,0},{12,2},{14,4},{16,6},{18,8},{20,10},{22,12},{24,14},{26,16}... | collective-permute-start | bytes 1572872 | tf_op jit(solution)/shard_map/ppermute | solution.py:12
  348.4 72.6 %collective-permute-start.12 = (bf16[2,512,256]{2,1,0:T(8,128)(2,1)S(1)}, bf16[2,512,256]{2,1,0:T(8,128)(2,1)S(1)}, u32[]{:S(2)}, u32[]{:S(2)}) collective-permute-start(bf16[2,512,256]{2,1,0:T(8,128)(2,1)S(1)} %pad_maximum_fusion.18), channel_id=1, source_target_pairs={{0,16},{2,18},{4,20},{6,22},{8,24},{10,26},{12,28},{14,30},{1,17},... | collective-permute-start | bytes 1572872 | tf_op jit(solution)/shard_map/ppermute | solution.py:12
  371.9 26.3 %collective-permute-start.21 = (bf16[2,512,256]{2,1,0:T(8,128)(2,1)S(1)}, bf16[2,512,256]{2,1,0:T(8,128)(2,1)S(1)}, u32[]{:S(2)}, u32[]{:S(2)}) collective-permute-start(bf16[2,512,256]{2,1,0:T(8,128)(2,1)S(1)} %pad_maximum_fusion.19), channel_id=1, source_target_pairs={{20,0},{22,2},{24,4},{26,6},{28,8},{30,10},{21,1},{23,3},{25,5},{2... | collective-permute-start | bytes 1572872 | tf_op jit(solution)/shard_map/ppermute | solution.py:12
  398.2 15.7 %collective-permute-start.19 = (bf16[2,512,256]{2,1,0:T(8,128)(2,1)S(1)}, bf16[2,512,256]{2,1,0:T(8,128)(2,1)S(1)}, u32[]{:S(2)}, u32[]{:S(2)}) collective-permute-start(bf16[2,512,256]{2,1,0:T(8,128)(2,1)S(1)} %pad_maximum_fusion.19), channel_id=1, source_target_pairs={{4,0},{6,2},{8,4},{10,6},{12,8},{14,10},{16,12},{18,14},{20,16},{2... | collective-permute-start | bytes 1572872 | tf_op jit(solution)/shard_map/ppermute | solution.py:12
  413.9 33.1 %collective-permute-start.25 = (bf16[2,512,256]{2,1,0:T(8,128)(2,1)S(1)}, bf16[2,512,256]{2,1,0:T(8,128)(2,1)S(1)}, u32[]{:S(2)}, u32[]{:S(2)}) collective-permute-start(bf16[2,512,256]{2,1,0:T(8,128)(2,1)S(1)} %pad_maximum_fusion.19), channel_id=1, source_target_pairs={{22,0},{24,2},{26,4},{28,6},{30,8},{23,1},{25,3},{27,5},{29,7},{31... | collective-permute-start | bytes 1572872 | tf_op jit(solution)/shard_map/ppermute | solution.py:12
  417.4 31.4 %collective-permute-start.23 = (bf16[2,512,256]{2,1,0:T(8,128)(2,1)S(1)}, bf16[2,512,256]{2,1,0:T(8,128)(2,1)S(1)}, u32[]{:S(2)}, u32[]{:S(2)}) collective-permute-start(bf16[2,512,256]{2,1,0:T(8,128)(2,1)S(1)} %pad_maximum_fusion.19), channel_id=1, source_target_pairs={{6,0},{8,2},{10,4},{12,6},{14,8},{16,10},{18,12},{20,14},{22,16},{... | collective-permute-start | bytes 1572872 | tf_op jit(solution)/shard_map/ppermute | solution.py:12
  420.9 41.4 %collective-permute-start.13 = (bf16[2,512,256]{2,1,0:T(8,128)(2,1)S(1)}, bf16[2,512,256]{2,1,0:T(8,128)(2,1)S(1)}, u32[]{:S(2)}, u32[]{:S(2)}) collective-permute-start(bf16[2,512,256]{2,1,0:T(8,128)(2,1)S(1)} %pad_maximum_fusion.19), channel_id=1, source_target_pairs={{16,0},{18,2},{20,4},{22,6},{24,8},{26,10},{28,12},{30,14},{17,1},... | collective-permute-start | bytes 1572872 | tf_op jit(solution)/shard_map/ppermute | solution.py:12
  519.8 122.7 %all-reduce.6.cloned.1.call-start = ((), (), s32[]{:S(2)}) async-start(), calls=%async_computation.5 | async-start | bytes 2097152 | tf_op jit(solution)/shard_map/psum | solution.py:179
  548.9 224.8 %all-reduce.4.cloned.1.call-start = ((), (), s32[]{:S(2)}) async-start(), calls=%async_computation.4 | async-start | bytes 524288 | tf_op jit(solution)/shard_map/psum | solution.py:180
  (108 other events, 4141.0 us)
Sparse Core Ops, SparseCore 0:
  10.1 23.9 all-gather.2
  59.6 34.5 reduce-scatter.1
  519.9 17.5 all-gather.4
  549.0 93.5 all-reduce.5
  649.4 124.2 all-reduce.3
where the time goes:
time: 793 us; the launch traced here: 785 us
  waiting for transfers between devices  376 us (47%)
  starting transfers between devices  127 us (16%)
  matrix products  114 us (14%)
  other arithmetic  57.9 us (7%)
  blocking collectives  55.9 us (7%)
  between operations  29.4 us (4%)
  local copies, waits for them, and re-layouts  25.4 us (3%)
    ppermute x26, waiting for transfers between devices, shifted(): return lax.ppermute(array, axis, pairs)  167 us
    psum x1, waiting for transfers between devices, local(): lax.psum((bilinear_part, loss_sum), ('tile', 'mlp'))  129 us
    ppermute x26, starting transfers between devices, shifted(): return lax.ppermute(array, axis, pairs)  126 us
    psum x1, waiting for transfers between devices, local(): grad_in, grad_out = lax.psum((in_part, out_part), 'tile')  41.4 us
    psum x1, blocking collectives, local(): lax.psum((bilinear_part, loss_sum), ('tile', 'mlp'))  39.4 us
    dot_general x14, matrix products, local(): jnp.einsum('rf,cf->rc', query_local[:, pretile], others, preferred_elemen...  35.2 us
    dot_general x18, matrix products, local(): jnp.dot(back_slope, senders, preferred_element_type=jnp.float32)  34.8 us
    and x23, other arithmetic, local(): post_valid.append(inside & (all_rows < tile_counts[1]))  24.5 us
  transfers between devices with their start and end apart: 31, of which 18 were waited for; matrix products, arithmetic and copies ran while one was open for 15% of the time, Pallas kernels for 0%

commit v1 on v0

v1 whole, which is shorter than its diff:
```python
import functools

import jax
import jax.numpy as jnp
from jax import lax
from jax.experimental import pallas as pl
from jax.experimental.pallas import tpu as pltpu
from jax.sharding import PartitionSpec as P

f32 = jnp.float32
bf16 = jnp.bfloat16
OFF = -1e30
VMEM = pl.BlockSpec(memory_space=pltpu.VMEM)
SMEM = pl.BlockSpec(memory_space=pltpu.SMEM)


def dot(a, b):
    return lax.dot_general(a, b, (((1,), (0,)), ((), ())), preferred_element_type=f32)


def moved(array, axis, target):
    peers = lax.axis_size(axis)
    pairs = [(i, target(i)) for i in range(peers) if target(i) is not None]
    return lax.ppermute(array, axis, pairs)


def over_mlp(array):
    groups = lax.axis_size("mlp")
    if groups == 2:
        return [array, moved(array, "mlp", lambda i: 1 - i)]
    gathered = lax.all_gather(array, "mlp", axis=0)
    member = lax.axis_index("mlp")
    order = [lax.rem(member + step, groups) for step in range(groups)]
    return [lax.dynamic_index_in_dim(gathered, g, 0, keepdims=False) for g in order]


def owner(meta, step, groups):
    return lax.rem(meta[1] + step, groups)


def call(kernel, name, outs, operands, flops=0, scratch=(), aliases=None):
    specs = [SMEM if o.dtype == jnp.int32 and o.ndim == 1 else VMEM for o in operands]
    size = sum(o.size * o.dtype.itemsize for o in operands)
    return pl.pallas_call(
        kernel,
        out_shape=[jax.ShapeDtypeStruct(shape, kind) for shape, kind in outs],
        in_specs=specs,
        out_specs=[VMEM] * len(outs),
        scratch_shapes=list(scratch),
        input_output_aliases=aliases or {},
        compiler_params=pltpu.CompilerParams(vmem_limit_bytes=40 * 1024 * 1024),
        cost_estimate=pl.CostEstimate(flops=flops, bytes_accessed=size, transcendentals=0),
        name=name,
    )(*operands)


def summed(arrays, places, kind, name):
    def kernel(*refs):
        for (first, count), out in zip(places, refs[len(arrays) :], strict=True):
            for t in range(count):
                total = None
                for ref in refs[: len(arrays)]:
                    if first + t < ref.shape[0]:
                        part = ref[first + t].astype(f32)
                        total = part if total is None else total + part
                out[t] = total.astype(kind)

    shape = arrays[0].shape[1:]
    return call(kernel, name, [((count, *shape), kind) for unused, count in places], arrays)


def sub_tile(xb, t):
    return 1 - xb if t == 0 else xb


def gelu_parts(h):
    c = 0.7978845608028654
    square = h * h
    bend = jnp.tanh(c * (h + 0.044715 * (square * h)))
    whole = 0.5 * (1.0 + bend)
    slope = whole + 0.5 * h * (1.0 - bend * bend) * (c * (1.0 + 3 * 0.044715 * square))
    return h * whole, slope


def mlp_kernel(kinds, ready, near, groups, *refs):
    refs = list(refs)
    meta, x_ref = refs[:2]
    del refs[:2]
    near_ref = refs.pop() if near else None
    out_ref = refs.pop()
    start_ref = refs.pop(0) if ready else None
    xb = meta[2]
    for place, kind in enumerate(kinds):
        for t in range(2):
            x = x_ref[kind, sub_tile(xb, t)]
            total = start_ref[kind, t] if ready else x.astype(f32)
            for g in range(groups):
                hidden = dot(x, refs[2 * g][...])
                active = gelu_parts(hidden)[0].astype(bf16)
                total = total + dot(active, refs[2 * g + 1][...])
            if len(kinds) == 1:
                out_ref[t] = total.astype(out_ref.dtype)
                if near and t == 0:
                    near_ref[0] = total.astype(out_ref.dtype)
            else:
                out_ref[place, t] = total.astype(out_ref.dtype)


def hidden_kernel(groups, meta, w_in_ref, *refs):
    w_t = w_in_ref[...].T
    outs = refs[groups:]
    for kind in range(2):
        for g in range(groups):
            for u in range(2):
                active, slope = gelu_parts(dot(w_t, refs[g][kind, u].T))
                outs[2 * kind][g, u] = active.astype(bf16)
                outs[2 * kind + 1][g, u] = slope


def weight_part(back, x, active_t, slope_t, w_out, sums):
    active_grad = dot(w_out, back.T)
    hidden_grad = (active_grad * slope_t).astype(bf16)
    return sums[0] + dot(hidden_grad, x), sums[1] + dot(active_t, back)


def pre_kernel(groups, meta, w_out_ref, bil_ref, active_ref, slope_ref, *refs):
    query_refs, pre_refs, x_refs = refs[:groups], refs[groups : 2 * groups], refs[2 * groups : 3 * groups]
    in_ref, out_ref, bil_grad_ref, loss_ref, pre_all, back_all = refs[3 * groups :]
    rows = pre_refs[0].shape[1]
    site_rows = rows * groups
    xb = meta[2]
    bil_t = bil_ref[...].T
    bil_grad = jnp.zeros(bil_grad_ref.shape, f32)
    sums = (jnp.zeros(in_ref.shape, f32), jnp.zeros(out_ref.shape, f32))
    for a in range(2):
        total = query_refs[0][a * site_rows : (a + 1) * site_rows]
        for ref in query_refs[1:]:
            total = total + ref[a * site_rows : (a + 1) * site_rows]
        query_back = total.astype(bf16)
        for g in range(groups):
            place = pl.ds(pl.multiple_of(owner(meta, g, groups) * rows, rows), rows)
            pre_all[a, place, :] = pre_refs[g][a]
        for g in range(groups):
            place = slice(g * rows, (g + 1) * rows)
            bil_grad = bil_grad + dot(pre_all[a, place, :].T, query_back[place])
        back_all[a] = dot(query_back, bil_t).astype(bf16)
        u = sub_tile(xb, a)
        for g in range(groups):
            place = pl.ds(pl.multiple_of(owner(meta, g, groups) * rows, rows), rows)
            back = back_all[a, place, :]
            sums = weight_part(back, x_refs[g][0, u], active_ref[g, u], slope_ref[g, u], w_out_ref[...], sums)
    in_ref[...], out_ref[...] = sums
    bil_grad_ref[...] = bil_grad
    loss = query_refs[0][2 * site_rows :]
    for ref in query_refs[1:]:
        loss = loss + ref[2 * site_rows :]
    loss_ref[...] = loss


def post_kernel(groups, meta, w_out_ref, active_ref, slope_ref, in0, out0, bil0, loss0, *refs):
    near_refs, far_refs, x_refs = refs[:groups], refs[groups : 2 * groups], refs[2 * groups : 3 * groups]
    mine_ref, other_ref, whole = refs[3 * groups :]
    xb = meta[2]
    core = lax.rem(meta[0], 2)
    sums = (in0[...], out0[...])
    for t in range(2):
        u = sub_tile(xb, t)
        for g in range(groups):
            back = (near_refs, far_refs)[t][g][0]
            sums = weight_part(back, x_refs[g][1, u], active_ref[g, u], slope_ref[g, u], w_out_ref[...], sums)
    hid = in0.shape[0]
    half = mine_ref.shape[0]
    whole[:hid] = sums[0]
    whole[hid : 2 * hid] = sums[1]
    whole[2 * hid :] = bil0[...]
    mine_ref[...] = whole[pl.ds(pl.multiple_of(core * half, 16), half), :]
    other_ref[:half] = whole[pl.ds(pl.multiple_of((1 - core) * half, 16), half), :]
    other_ref[half:] = loss0[...]


def halves_kernel(meta, mine_ref, other_ref, loss0, sent_ref, kept_ref, whole):
    rows = kept_ref.shape[0] - 8
    half = mine_ref.shape[0]
    whole[...] = mine_ref[...] + other_ref[:half]
    sent_ref[...] = whole[...].astype(sent_ref.dtype)
    kept_ref[rows:] = loss0[...] + other_ref[half:]
    kept_ref[:rows] = whole[pl.ds(pl.multiple_of(meta[0] // 2 * rows, 16), rows), :]


def total_kernel(meta, got_ref, kept_ref, out_ref):
    rows = kept_ref.shape[0] - 8
    chips = got_ref.shape[0] // rows
    total = kept_ref[:rows]
    for n in range(chips):
        piece = got_ref[n * rows : (n + 1) * rows, :].astype(f32)
        total = total + jnp.where(n == meta[0] // 2, 0.0, piece)
    for n in range(chips):
        first = n * (rows + 8)
        out_ref[first : first + rows, :] = total
        out_ref[first + rows : first + rows + 8, :] = kept_ref[rows:]


def last_kernel(chips, share, meta, mine_ref, other_ref, in_ref, out_ref, bil_ref, loss_ref, whole):
    core = lax.rem(meta[0], 2)
    half = whole.shape[0] // 2
    rows = half // chips
    loss = jnp.zeros((8, 128), f32)
    for n in range(chips):
        first = n * (rows + 8)
        for ref, side in ((mine_ref, core), (other_ref, 1 - core)):
            place = side * half + n * rows
            whole[pl.ds(pl.multiple_of(place, 8), rows), :] = ref[first : first + rows, :]
        loss = loss + mine_ref[first + rows : first + rows + 8, :128]
    hid = out_ref.shape[0]
    in_ref[...] = whole[:hid].T
    out_ref[...] = whole[hid : 2 * hid]
    bil_ref[...] = whole[2 * hid :]
    loss_ref[...] = loss * share


def pair_kernel(slots, foreign, first, last, groups, site_rows, depth, heavy, out_scale, *refs):
    refs = list(refs)

    def take(count):
        taken = refs[:count]
        del refs[:count]
        return taken

    meta, counts, label_ref = take(3)
    if first:
        bil_ref = take(1)[0]
        pre_refs = take(groups)
    else:
        q_ref, qt_ref, acc_in, loss_in, hit_in, found_in = take(6)
    post_refs = take(len(slots))
    z_list = list(dict.fromkeys(z for unused, z in slots))
    grad_refs = dict(zip(z_list, take(len(z_list)), strict=True))
    if first:
        q_ref, qt_ref = take(2)
    if last:
        out_ref, acc, loss_ref, hit_ref, found_ref = refs
    else:
        acc, loss_ref, hit_ref, found_ref = refs
    tile_here, member, xb = meta[0], meta[1], meta[2]
    yg = lax.rem(tile_here // depth, 4)
    zg = lax.rem(tile_here, depth)
    toward = 1 - 2 * xb
    rows = post_refs[0].shape[1]
    width = post_refs[0].shape[2]
    if first:
        scale = jnp.asarray(width ** (-0.5), bf16)
        for a in range(2):
            for g in range(groups):
                part = dot(pre_refs[g][a], bil_ref[...]).astype(bf16)
                place = pl.ds(pl.multiple_of(owner(meta, g, groups) * rows, rows), rows)
                q_ref[a, place, :] = part
            qt_ref[a] = (q_ref[a] * scale).T
        acc[...] = jnp.zeros_like(acc)
        loss_ref[...] = jnp.zeros_like(loss_ref)
        hit_ref[...] = jnp.zeros_like(hit_ref)
        found_ref[...] = jnp.zeros_like(found_ref)
    elif last:
        acc[...] = acc_in[...]
        loss_ref[...] = loss_in[...]
        hit_ref[...] = hit_in[...]
        found_ref[...] = found_in[...]
    j_own = lax.broadcasted_iota(jnp.int32, (rows, site_rows), 0)
    j_col = lax.broadcasted_iota(jnp.int32, (rows, 128), 0)
    i_row = lax.broadcasted_iota(jnp.int32, (1, site_rows), 1)
    step = rows // (8 if rows >= 128 else 4)
    i_ok = [i_row < counts[tile_here * 4 + sub_tile(xb, a) * 2] for a in (0, 1)]
    i_bias = [jnp.where(ok, 0.0, OFF).astype(f32) for ok in i_ok]
    if foreign:
        nz = sum(1 for dy, unused in slots if dy == 0)
        chunks = [[(n, 0) for n in range(k, k + nz)] for k in range(0, len(slots), nz)]
    else:
        chunks = [[(n, 0), (n, 1)] for n in range(len(slots))]
    for chunk in chunks:
        post = jnp.concatenate([post_refs[n][t] for n, t in chunk], 0)
        post_t = post.T
        places = []
        for n, t in chunk:
            dy, z_slot = slots[n]
            if depth == 2:
                z_other = zg if z_slot == 0 else 1 - zg
            else:
                z_other = zg + z_slot
            x_other = 1 - xb if foreign else xb
            y_other = yg + dy
            inside = (y_other >= 0) & (y_other < 4) & (z_other >= 0) & (z_other < depth)
            source = jnp.where(inside, x_other * 4 * depth + y_other * depth + z_other, tile_here)
            valid = jnp.clip(counts[source * 4 + sub_tile(x_other, t) * 2 + 1] - member * rows, 0, rows)
            places.append((t, dy, z_other - zg, jnp.where(inside, valid, 0)))
        j_bias = jnp.concatenate([jnp.where(j_col < place[3], 0.0, OFF).astype(f32) for place in places], 0)
        j_bias = jnp.concatenate([j_bias] * (site_rows // 128), 1)
        total = None
        for a in (0,) if foreign else (0, 1):
            targets = []
            for t, dy, dz, valid in places:
                dx = toward if foreign else 0 if t == a else -toward if a == 0 else toward
                base = ((dx + 1) * 9 + (dy + 1) * 3 + dz + 1) * site_rows + member * rows
                key = label_ref[sub_tile(xb, a)] - base
                key = jnp.where(i_ok[a] & (key < valid), key, -1)
                found_ref[a] += jnp.where(key >= 0, 1.0, 0.0)
                targets.append(j_own == key)
            target = jnp.concatenate(targets, 0)
            s = dot(post, qt_ref[a]) + j_bias + i_bias[a]
            e = jnp.exp(-jnp.abs(s))
            w = 1.0 + e
            r = pl.reciprocal(w, approx=True)
            chance = jnp.where(s >= 0.0, r, e * r)
            slope = jnp.where(target, (chance - 1.0) * heavy, chance).astype(bf16)
            part = dot(slope, q_ref[a])
            total = part if total is None else total + part
            acc[a] += dot(post_t, slope)
            piece = hit = None
            for k in range(len(chunk)):
                product = small = above = None
                for g in range(k * rows, (k + 1) * rows, step):
                    here = slice(g, g + step)
                    more = jnp.maximum(s[here], 0.0)
                    found = jnp.where(target[here], s[here], 0.0)
                    product = w[here] if product is None else product * w[here]
                    small = e[here] if small is None else small + e[here]
                    above = more if above is None else above + more
                    hit = found if hit is None else hit + found
                loss = above + jnp.where(small < 1e-3, small, jnp.log(product))
                piece = loss if piece is None else piece + loss
            loss_ref[...] += jnp.sum(piece.reshape(step // 8, 8, site_rows), 0)
            hit_ref[a] += jnp.sum(hit.reshape(step // 8, 8, site_rows), 0)
        for k, (n, t) in enumerate(chunk):
            dy, z_slot = slots[n]
            place = [other for other, z in slots if z == z_slot].index(dy) * post_refs[n].shape[0] + t
            grad_refs[z_slot][place] = total[k * rows : (k + 1) * rows] * out_scale
    if last:
        total = jnp.sum(loss_ref[...])
        for a in range(2):
            out_ref[a * site_rows : (a + 1) * site_rows] = (acc[a] * out_scale).T
            score = jnp.sum(hit_ref[a], 0, keepdims=True)
            soft = jnp.log1p(jnp.exp(-jnp.abs(score)))
            missed = heavy * (jnp.maximum(-score, 0.0) + soft) - (jnp.maximum(score, 0.0) + soft)
            total = total + jnp.sum(jnp.where(found_ref[a] > 0.0, missed, 0.0))
        out_ref[2 * site_rows :] = jnp.full((8, width), total, f32)


def pair_call(name, slots, foreign, first, last, operands, posts, sizes):
    tiles, rows, width = posts[0].shape
    groups, site_rows = sizes[0], sizes[1]
    kernel = functools.partial(pair_kernel, slots, foreign, first, last, *sizes)
    state = [
        ((2, width, site_rows), f32),
        ((8, site_rows), f32),
        ((2, 8, site_rows), f32),
        ((2, 1, site_rows), f32),
    ]
    z_count = len(set(z for unused, z in slots))
    outs = [((tiles * len(slots) // z_count, rows, width), f32)] * z_count
    if first:
        outs += [((2, site_rows, width), bf16), ((2, width, site_rows), bf16)]
    if last:
        outs += [((2 * site_rows + 8, width), f32)]
    else:
        outs += state
    pairs = len(slots) * (1 if foreign else 4)
    aliases = {} if first or last else {5 + n: z_count + n for n in range(4)}
    results = call(
        kernel,
        name,
        outs,
        operands + posts,
        flops=pairs * rows * site_rows * width * 40,
        scratch=[pltpu.VMEM(shape, kind) for shape, kind in state] if last else (),
        aliases=aliases,
    )
    return list(results[:z_count]), list(results[z_count:])


def after(array, *others):
    return lax.optimization_barrier((array, *others))[0]


def local(features, w_in, w_out, bilinear, partner, counts):
    row_part = features.shape[1]
    width = features.shape[4]
    hid = w_in.shape[1]
    groups = lax.axis_size("mlp")
    site_rows = row_part * groups
    tile_count = lax.axis_size("tile")
    depth = tile_count // 8
    tile_here = lax.axis_index("tile")
    member = lax.axis_index("mlp")
    xb = tile_here // (4 * depth)
    heavy = float(27 * site_rows // 4)
    out_scale = width ** (-0.5) / (2 * tile_count * site_rows)
    half = tile_count // 2

    def side(i):
        return i ^ half

    def along_y(step):
        return lambda i: i + step * depth if 0 <= i // depth % 4 + step < 4 else None

    def both(step):
        return lambda i: None if along_y(step)(i) is None else along_y(step)(i) ^ half

    z_slots = (0, 1) if depth == 2 else (0, -1, 1)

    def along_z(slot):
        if depth == 2:
            return lambda i: i ^ 1
        return lambda i: i - slot if 0 <= i % depth - slot < depth else None

    def back_z(slot):
        return along_z(slot if depth == 2 else -slot)

    def from_z(array):
        return [moved(array, "tile", along_z(slot)) for slot in z_slots[1:]]

    w_ins, w_outs = over_mlp(w_in), over_mlp(w_out)
    meta = jnp.stack([tile_here, member, xb]).astype(jnp.int32)
    x = jnp.transpose(features[0], (2, 1, 0, 3))
    labels = lax.dynamic_index_in_dim(partner, tile_here, 0, keepdims=False)[:, None, :]
    flat_counts = counts.reshape(-1)
    rows4 = (2, 2, row_part, width)
    rows3 = (2, row_part, width)
    flops = 4 * row_part * width * hid * 4
    begun = call(
        functools.partial(mlp_kernel, (0, 1), False, False, 1), "mlp_own", [(rows4, f32)], [meta, x, w_in, w_out], flops
    )[0]
    pairs_w = [w for pair in zip(w_ins[1:], w_outs[1:], strict=True) for w in pair]
    results = []
    for kind, name in ((1, "mlp_post"), (0, "mlp_pre")):
        near = kind == 1
        results += call(
            functools.partial(mlp_kernel, (kind,), True, near, groups - 1),
            name,
            [(rows3, bf16)] + [((1, row_part, width), bf16)] * near,
            [meta, x, begun, *pairs_w],
            flops * (groups - 1) // 2,
        )
    post, post_near, pre = results

    near = {dy: moved(post, "tile", along_y(-dy)) for dy in (-1, 1)}
    pres = over_mlp(pre)
    far = {0: moved(post_near, "tile", side)}
    for dy in (-1, 1):
        far[dy] = moved(after(post_near, pres[-1]), "tile", both(-dy))
    sizes = (groups, site_rows, depth, heavy, out_scale)
    fixed = [meta, flat_counts, labels]
    grads_own, (query, query_t, *state) = pair_call(
        "pairs_own", [(0, z) for z in z_slots], False, True, False, fixed + [bilinear, *pres], [post] + from_z(post), sizes
    )
    queries = [query, query_t]
    xs = over_mlp(after(x, pres[-1]))
    near = {dy: after(near[dy], state[1]) for dy in (-1, 1)}
    near_z = {dy: from_z(near[dy]) for dy in (-1, 1)}
    grads_near, state = pair_call(
        "pairs_near", [(dy, 0) for dy in (-1, 1)], False, False, False, fixed + queries + state, [near[-1], near[1]], sizes
    )
    far = {dy: after(far[dy], state[1]) for dy in (-1, 0, 1)}
    far_z = {dy: from_z(far[dy]) for dy in (-1, 0, 1)}
    grads_near_z, state = pair_call(
        "pairs_near_z",
        [(dy, z) for dy in (-1, 1) for z in z_slots[1:]],
        False, False, False,
        fixed + queries + state,
        near_z[-1] + near_z[1],
        sizes,
    )
    grads_far, (query_part,) = pair_call(
        "pairs_far",
        [(dy, z) for dy in (-1, 0, 1) for z in z_slots],
        True, False, True,
        fixed + queries + state,
        [one for dy in (-1, 0, 1) for one in [far[dy]] + far_z[dy]],
        sizes,
    )

    def back_from_z(grads):
        return [moved(g, "tile", back_z(slot)) for slot, g in zip(z_slots[1:], grads, strict=True)]

    own_parts = grads_own[:1] + back_from_z(grads_own[1:])
    near_sums = summed(grads_near + back_from_z(grads_near_z), [(0, 2), (2, 2)], bf16, "near_sums")
    near_back = [moved(total, "tile", along_y(dy)) for total, dy in zip(near_sums, (-1, 1), strict=True)]
    query_parts = over_mlp(query_part)
    far_sums = summed(grads_far[:1] + back_from_z(grads_far[1:]), [(0, 1), (1, 1), (2, 1)], bf16, "far_sums")
    far_back = [
        moved(total, "tile", target) for total, target in zip(far_sums, (both(-1), side, both(1)), strict=True)
    ]
    part_t = (groups, 2, hid, row_part)
    active_0, slope_0, active_1, slope_1 = call(
        functools.partial(hidden_kernel, groups),
        "hidden",
        [(part_t, bf16), (part_t, f32)] * 2,
        [meta, w_in, *xs],
        flops * groups // 2,
    )
    in_0, out_0, bil_0, loss = call(
        functools.partial(pre_kernel, groups),
        "pre_grads",
        [((hid, width), f32)] * 2 + [((width, width), f32), ((8, width), f32)],
        [meta, w_out, bilinear, active_0, slope_0, *query_parts, *pres, *xs],
        flops * groups,
        [pltpu.VMEM((2, site_rows, width), bf16)] * 2,
    )
    near_post, far_post = summed(own_parts + near_back, [(0, 1), (1, 1)], f32, "post_sums")
    far_post = over_mlp(far_post.astype(bf16))
    near_post = over_mlp(summed([near_post] + far_back, [(0, 1)], bf16, "near_post")[0])
    half_rows = (2 * hid + width) // 2
    mine, other = call(
        functools.partial(post_kernel, groups),
        "post_grads",
        [((half_rows, width), f32), ((half_rows + 8, width), f32)],
        [meta, w_out, active_1, slope_1, in_0, out_0, bil_0, loss, *near_post, *far_post, *xs],
        flops * groups,
        [pltpu.VMEM((2 * half_rows, width), f32)],
    )

    chips = tile_count // 2
    swap = lambda i: i ^ 1
    same_core = [[core + 2 * chip for chip in range(chips)] for core in range(2)]

    def to_chips(array):
        return lax.all_to_all(array, "tile", 0, 0, tiled=True, axis_index_groups=same_core)

    half_shape, piece = (half_rows, width), (half_rows // chips + 8, width)
    sent, kept = call(
        halves_kernel,
        "halves",
        [(half_shape, bf16), (piece, f32)],
        [meta, mine, moved(other, "tile", swap), loss],
        scratch=[pltpu.VMEM(half_shape, f32)],
    )
    joined_shape = (half_rows + 8 * chips, width)
    total = call(total_kernel, "total", [(joined_shape, f32)], [meta, to_chips(sent), kept])[0]
    joined = to_chips(total)
    share = 1.0 / (2.0 * tile_count * site_rows * 27 * site_rows)
    grad_in, grad_out, grad_bilinear, pair_loss = call(
        functools.partial(last_kernel, chips, share),
        "last",
        [((width, hid), f32), ((hid, width), f32), ((width, width), f32), ((8, 128), f32)],
        [meta, joined, moved(joined, "tile", swap)],
        scratch=[pltpu.VMEM((2 * half_rows, width), f32)],
    )
    return (pair_loss[0, 0], grad_in, grad_out, grad_bilinear)


def solution(mesh):
    placed = (P("tile", "mlp", None, None, None), P(None, "mlp"), P("mlp", None), P(), P(), P())
    return jax.shard_map(
        local,
        mesh=mesh,
        in_specs=placed,
        out_specs=(P(), P(None, "mlp"), P("mlp", None), P()),
        check_vma=False,
    )
```

time: 793 us -> 149 us (0.19)
  waiting for transfers between devices: 376 us -> 29.2 us
  matrix products: 114 us -> 0 us
  starting transfers between devices: 127 us -> 42.7 us
  other arithmetic: 57.9 us -> 0.09 us
  Pallas kernels: 0 us -> 33.5 us
  between operations: 29.4 us -> 1.05 us
  local copies, waits for them, and re-layouts: 25.4 us -> 3.78 us
  blocking collectives: 55.9 us -> 38.5 us
    psum x2 -> x0, waiting for transfers between devices: 171 us -> none  [the longest x1 129 us: local(): lax.psum((bilinear_part, loss_sum), ('tile', 'mlp'))]
    ppermute x26 -> x28, waiting for transfers between devices: 167 us -> 29.2 us  [moved(): return lax.ppermute(array, axis, pairs)]
    dot_general x61 -> x0, matrix products: 114 us -> none  [the longest x14 35.2 us: local(): jnp.einsum('rf,cf->rc', query_local[:, pretile], others, preferred_elemen...]
    ppermute x26 -> x28, starting transfers between devices: 126 us -> 42.7 us  [moved(): return lax.ppermute(array, axis, pairs)]
    psum x1 -> x0, blocking collectives: 39.4 us -> none  [local(): lax.psum((bilinear_part, loss_sum), ('tile', 'mlp'))]
    and x36 -> x0, other arithmetic: 38.9 us -> none  [the longest x23 24.5 us: local(): post_valid.append(inside & (all_rows < tile_counts[1]))]
    all_to_all x0 -> x2, blocking collectives: none -> 38.5 us  [to_chips(): lax.all_to_all(array, 'tile', 0, 0, tiled=True, axis_index_groups=same_core)]
    pallas_call x0 -> x17, Pallas kernels: none -> 33.5 us  [call(): pl.pallas_call(kernel, out_shape=[jax.ShapeDtypeStruct(shape, kind) for s...]
  transfers between devices with their start and end apart: 31 -> 28, of which waited for: 18 -> 8; matrix products, arithmetic and copies ran while one was open for 15% -> 1% of each run, Pallas kernels for 0% -> 18%
where the time goes in v1:
time: 149 us
  starting transfers between devices  42.7 us (29%)
  blocking collectives  38.5 us (26%)
  Pallas kernels  33.5 us (22%)
  waiting for transfers between devices  29.2 us (20%)
  local copies, waits for them, and re-layouts  3.78 us (3%)
    ppermute x28, starting transfers between devices, moved(): return lax.ppermute(array, axis, pairs)  42.7 us
    all_to_all x2, blocking collectives, to_chips(): lax.all_to_all(array, 'tile', 0, 0, tiled=True, axis_index_groups=same_core)  38.5 us
    pallas_call x17, Pallas kernels, call(): pl.pallas_call(kernel, out_shape=[jax.ShapeDtypeStruct(shape, kind) for s...  33.5 us
    ppermute x28, waiting for transfers between devices, moved(): return lax.ppermute(array, axis, pairs)  29.2 us
    unnamed x16, local copies, waits for them, and re-layouts  3.14 us
  transfers between devices with their start and end apart: 28, of which 8 were waited for; matrix products, arithmetic and copies ran while one was open for 1% of the time, Pallas kernels for 18%

profile of v1, /device:TPU:0, one launch (start us, length us, event | category | flops | bytes accessed | tf_op | source)
XLA Modules:
  0.0 148.8 jit_solution(7192473933828589189)
XLA Ops:
  0.6 3.0 %collective-permute-start = (bf16[256,512]{1,0:T(8,128)(2,1)}, bf16[256,512]{1,0:T(8,128)(2,1)S(1)}, u32[]{:S(2)}, u32[]{:S(2)}) collective-permute-start(bf16[256,512]{1,0:T(8,128)(2,1)} %w_in_ref.1), channel_id=1, source_target_pairs={{0,1},{1,0},{2,3},{3,2},{4,5},{5,4},{6,7},{7,6},{8,9},{9,8},{10,11... | collective-permute-start | bytes 786440 | tf_op jit(solution)/shard_map/ppermute | solution.py:24
  6.9 1.6 %mlp_own.1.refs_2_ = f32[2,2,256,256]{3,2,1,0:T(8,128)S(1)} custom-call(s32[3]{0:T(128)S(1)} %pad_add_fusion.refs_0_.meta, bf16[2,2,256,256]{3,2,1,0:T(8,128)(2,1)S(1)} %bitcast.13, bf16[256,512]{1,0:T(8,128)(2,1)S(1)} %copy-done.3, bf16[512,256]{1,0:T(8,128)(2,1)S(1)} %copy-done.1), custom_call_target="tpu_custom_call" | custom-call | flops 536870912 | bytes 1048588 | tf_op jit(solution)/shard_map/mlp_own/pallas_call | solution.py:44
  8.5 2.6 %collective-permute-done.refs_3_ = bf16[256,512]{1,0:T(8,128)(2,1)S(1)} collective-permute-done((bf16[256,512]{1,0:T(8,128)(2,1)}, bf16[256,512]{1,0:T(8,128)(2,1)S(1)}, u32[]{:S(2)}, u32[]{:S(2)}) %collective-permute-start) | collective-permute-done | bytes 262176 | tf_op jit(solution)/shard_map/ppermute | solution.py:24
  11.0 4.8 %collective-permute-done.1.refs_4_ = bf16[512,256]{1,0:T(8,128)(2,1)S(1)} collective-permute-done((bf16[512,256]{1,0:T(8,128)(2,1)}, bf16[512,256]{1,0:T(8,128)(2,1)S(1)}, u32[]{:S(2)}, u32[]{:S(2)}) %collective-permute-start.1) | collective-permute-done | bytes 262176 | tf_op jit(solution)/shard_map/ppermute | solution.py:24
  17.0 1.8 %collective-permute-start.2 = (bf16[2,256,256]{2,1,0:T(8,128)(2,1)S(1)}, bf16[2,256,256]{2,1,0:T(8,128)(2,1)S(1)}, u32[]{:S(2)}, u32[]{:S(2)}) collective-permute-start(bf16[2,256,256]{2,1,0:T(8,128)(2,1)S(1)} %mlp_pre.1.refs_4_.refs_2_), channel_id=1, source_target_pairs={{0,1},{1,0},{2,3},{3,2},{4,5},{5,4},{6,7},{7,6},{8,9},{9,8},{10,11... | collective-permute-start | bytes 786440 | tf_op jit(solution)/shard_map/ppermute | solution.py:24
  20.3 1.3 collective-permute-start.6
  21.6 4.6 %collective-permute-start.5 = (bf16[2,256,256]{2,1,0:T(8,128)(2,1)S(1)}, bf16[2,256,256]{2,1,0:T(8,128)(2,1)S(1)}, u32[]{:S(2)}, u32[]{:S(2)}) collective-permute-start(bf16[2,256,256]{2,1,0:T(8,128)(2,1)S(1)} %get-tuple-element.62.refs_6_), channel_id=1, source_target_pairs={{0,4},{2,6},{4,8},{6,10},{8,12},{10,14},{16,20},{18,22},{20,24},{2... | collective-permute-start | bytes 786440 | tf_op jit(solution)/shard_map/ppermute | solution.py:24
  26.2 2.7 %collective-permute-start.11 = (bf16[1,256,256]{2,1,0:T(8,128)(2,1)S(1)}, bf16[1,256,256]{2,1,0:T(8,128)(2,1)S(1)}, u32[]{:S(2)}, u32[]{:S(2)}) collective-permute-start(bf16[1,256,256]{2,1,0:T(8,128)(2,1)S(1)} %get-tuple-element.80), channel_id=1, source_target_pairs={{0,16},{2,18},{4,20},{6,22},{8,24},{10,26},{12,28},{14,30},{16,0},... | collective-permute-start | bytes 393224 | tf_op jit(solution)/shard_map/ppermute | solution.py:24
  28.8 1.3 collective-permute-start.13
  30.1 6.5 %collective-permute-start.9 = (bf16[1,256,256]{2,1,0:T(8,128)(2,1)S(1)}, bf16[1,256,256]{2,1,0:T(8,128)(2,1)S(1)}, u32[]{:S(2)}, u32[]{:S(2)}) collective-permute-start(bf16[1,256,256]{2,1,0:T(8,128)(2,1)S(1)} %get-tuple-element.80), channel_id=1, source_target_pairs={{0,20},{2,22},{4,24},{6,26},{8,28},{10,30},{16,4},{18,6},{20,8},{2... | collective-permute-start | bytes 393224 | tf_op jit(solution)/shard_map/ppermute | solution.py:24
  36.7 5.1 %pairs_own.1 = (f32[2,256,256]{2,1,0:T(8,128)S(1)}, f32[2,256,256]{2,1,0:T(8,128)S(1)}, bf16[2,512,256]{2,1,0:T(8,128)(2,1)S(1)}, bf16[2,256,512]{2,1,0:T(8,128)...) custom-call(s32[3]{0:T(128)S(1)} %pad_add_fusion.refs_0_.meta, ...), custom_call_target="tpu_custom_call" | custom-call | flops 10737418240 | bytes 1184012 | tf_op jit(solution)/shard_map/pairs_own/pallas_call | solution.py:44
  42.4 4.7 %pairs_near.1 = (f32[4,256,256]{2,1,0:T(8,128)S(1)}, f32[2,256,512]{2,1,0:T(8,128)S(1)}, f32[8,512]{1,0:T(8,128)S(1)}, f32[2,8,512]{2,1,0:T(8,128)S(1)}, f32[2,1,512]{2,1,0:T(1,128)S(1)}) custom-call(s32[3]{0:T(128)S(1)} %pad_add_fusion.refs_0_.meta, ...), custom_call_target="tpu_custom_call", output_to_operand_aliasing={{1}: (5, {}), {2}: (6, {}), {3}: (7, {}), {4}: (8, {})} | custom-call | flops 10737418240 | bytes 2679052 | tf_op jit(solution)/shard_map/pairs_near/pallas_call | solution.py:44
  47.8 4.9 %pairs_near_z.1 = (f32[4,256,256]{2,1,0:T(8,128)S(1)}, f32[2,256,512]{2,1,0:T(8,128)S(1)}, f32[8,512]{1,0:T(8,128)S(1)}, f32[2,8,512]{2,1,0:T(8,128)S(1)}, f32[2,1,512]{2,1,0:T(1,128)S(1)}) custom-call(s32[3]{0:T(128)S(1)} %pad_add_fusion.refs_0_.meta, ...), custom_call_target="tpu_custom_call", output_to_operand_aliasing={{1}: (5, {}), {2}: (6, {}), {3}: (7, {}), {4}: (8, {})} | custom-call | flops 10737418240 | bytes 2679052 | tf_op jit(solution)/shard_map/pairs_near_z/pallas_call | solution.py:44
  53.1 3.9 %pairs_far.1 = (f32[3,256,256]{2,1,0:T(8,128)S(1)}, f32[3,256,256]{2,1,0:T(8,128)S(1)}, f32[1032,256]{1,0:T(8,128)S(1)}) custom-call(s32[3]{0:T(128)S(1)} %pad_add_fusion.refs_0_.meta, s32[64]{0:T(128)S(1)} %reshape.16.refs_1_, s32[2,1,512]{2,1,0:T(1,128)S(1)} %broadcast_in_dim.3.refs_2_, bf16[2,512,256]{2,1,0:T(8,128)(2,1)S(1)} %get-tuple-element.63.refs_3_, ...), custom_call_target="tpu_custom_call" | custom-call | flops 8053063680 | bytes 2941196 | tf_op jit(solution)/shard_map/pairs_far/pallas_call | solution.py:44
  57.9 1.5 %collective-permute-start.3 = (bf16[2,2,256,256]{3,2,1,0:T(8,128)(2,1)S(1)}, bf16[2,2,256,256]{3,2,1,0:T(8,128)(2,1)S(1)}, u32[]{:S(2)}, u32[]{:S(2)}) collective-permute-start(bf16[2,2,256,256]{3,2,1,0:T(8,128)(2,1)S(1)} %bitcast.16), channel_id=1, source_target_pairs={{0,1},{1,0},{2,3},{3,2},{4,5},{5,4},{6,7},{7,6},{8,9},{9,8},{10,11... | collective-permute-start | bytes 1572872 | tf_op jit(solution)/shard_map/ppermute | solution.py:24
  59.5 1.3 collective-permute-start.18
  60.9 5.8 %collective-permute-start.19 = (bf16[2,256,256]{2,1,0:T(8,128)(2,1)S(1)}, bf16[2,256,256]{2,1,0:T(8,128)(2,1)S(1)}, u32[]{:S(2)}, u32[]{:S(2)}) collective-permute-start(bf16[2,256,256]{2,1,0:T(8,128)(2,1)S(1)} %get-tuple-element.94), channel_id=1, source_target_pairs={{0,4},{2,6},{4,8},{6,10},{8,12},{10,14},{16,20},{18,22},{20,24},{2... | collective-permute-start | bytes 786440 | tf_op jit(solution)/shard_map/ppermute | solution.py:24
  66.8 1.3 collective-permute-start.21
  68.1 3.2 %collective-permute-done.18.refs_2_ = bf16[2,256,256]{2,1,0:T(8,128)(2,1)S(1)} collective-permute-done((bf16[2,256,256]{2,1,0:T(8,128)(2,1)S(1)}, bf16[2,256,256]{2,1,0:T(8,128)(2,1)S(1)}, u32[]{:S(2)}, u32[]{:S(2)}) %collective-permute-start.18) | collective-permute-done | bytes 262176 | tf_op jit(solution)/shard_map/ppermute | solution.py:24
  71.3 1.9 %collective-permute-start.22 = (bf16[1,256,256]{2,1,0:T(8,128)(2,1)S(1)}, bf16[1,256,256]{2,1,0:T(8,128)(2,1)S(1)}, u32[]{:S(2)}, u32[]{:S(2)}) collective-permute-start(bf16[1,256,256]{2,1,0:T(8,128)(2,1)S(1)} %get-tuple-element.99), channel_id=1, source_target_pairs={{0,16},{2,18},{4,20},{6,22},{8,24},{10,26},{12,28},{14,30},{16,0},... | collective-permute-start | bytes 393224 | tf_op jit(solution)/shard_map/ppermute | solution.py:24
  73.2 6.6 %collective-permute-done.19.refs_3_ = bf16[2,256,256]{2,1,0:T(8,128)(2,1)S(1)} collective-permute-done((bf16[2,256,256]{2,1,0:T(8,128)(2,1)S(1)}, bf16[2,256,256]{2,1,0:T(8,128)(2,1)S(1)}, u32[]{:S(2)}, u32[]{:S(2)}) %collective-permute-start.19) | collective-permute-done | bytes 262176 | tf_op jit(solution)/shard_map/ppermute | solution.py:24
  79.8 5.8 %collective-permute-start.23 = (bf16[1,256,256]{2,1,0:T(8,128)(2,1)S(1)}, bf16[1,256,256]{2,1,0:T(8,128)(2,1)S(1)}, u32[]{:S(2)}, u32[]{:S(2)}) collective-permute-start(bf16[1,256,256]{2,1,0:T(8,128)(2,1)S(1)} %get-tuple-element.100), channel_id=1, source_target_pairs={{0,20},{2,22},{4,24},{6,26},{8,28},{10,30},{16,4},{18,6},{20,8},{2... | collective-permute-start | bytes 393224 | tf_op jit(solution)/shard_map/ppermute | solution.py:24
  86.3 2.2 %collective-permute-done.23.refs_3_ = bf16[1,256,256]{2,1,0:T(8,128)(2,1)S(1)} collective-permute-done((bf16[1,256,256]{2,1,0:T(8,128)(2,1)S(1)}, bf16[1,256,256]{2,1,0:T(8,128)(2,1)S(1)}, u32[]{:S(2)}, u32[]{:S(2)}) %collective-permute-start.23) | collective-permute-done | bytes 131104 | tf_op jit(solution)/shard_map/ppermute | solution.py:24
  89.2 5.5 %collective-permute-done.3.refs_1_.refs_5_ = bf16[2,2,256,256]{3,2,1,0:T(8,128)(2,1)S(1)} collective-permute-done((bf16[2,2,256,256]{3,2,1,0:T(8,128)(2,1)S(1)}, bf16[2,2,256,256]{3,2,1,0:T(8,128)(2,1)S(1)}, u32[]{:S(2)}, u32[]{:S(2)}) %collective-permute-start.3) | collective-permute-done | bytes 524320 | tf_op jit(solution)/shard_map/ppermute | solution.py:24
  94.6 3.3 %hidden.1 = (bf16[2,2,512,256]{3,2,1,0:T(8,128)(2,1)S(1)}, f32[2,2,512,256]{3,2,1,0:T(8,128)S(1)}, bf16[2,2,512,256]{3,2,1,0:T(8,128)(2,1)S(1)}, f32[2,2,512,256]{3,2,1,0:T(8,128)S(1)}) custom-call(s32[3]{0:T(128)S(1)} %pad_add_fusion.refs_0_.meta, bf16[256,512]{1,0:T(8,128)(2,1)S(1)} %copy-done.4, bf16[2,2,256,256]{3,2,1,0:T(8,128)(2,1)S(1)} %bitcast.17, ...), custom_call_target="tpu_custom_call" | custom-call | flops 536870912 | bytes 1310732 | tf_op jit(solution)/shard_map/hidden/pallas_call | solution.py:44
  98.0 2.2 %pre_grads.1 = (f32[512,256]{1,0:T(8,128)S(1)}, f32[512,256]{1,0:T(8,128)S(1)}, f32[256,256]{1,0:T(8,128)S(1)}, f32[8,256]{1,0:T(8,128)S(1)}) custom-call(s32[3]{0:T(128)S(1)} %pad_add_fusion.refs_0_.meta, bf16[512,256]{1,0:T(8,128)(2,1)S(1)} %copy-done.2, bf16[256,256]{1,0:T(8,128)(2,1)S(1)} %copy-done.5, ...), custom_call_target="tpu_custom_call" | custom-call | flops 1073741824 | bytes 7225356 | tf_op jit(solution)/shard_map/pre_grads/pallas_call | solution.py:44
  100.3 2.1 %post_grads.1 = (f32[640,256]{1,0:T(8,128)S(1)}, f32[648,256]{1,0:T(8,128)S(1)}) custom-call(s32[3]{0:T(128)S(1)} %pad_add_fusion.refs_0_.meta, bf16[512,256]{1,0:T(8,128)(2,1)S(1)} %copy-done.2, bf16[2,2,512,256]{3,2,1,0:T(8,128)(2,1)S(1)} %get-tuple-element.58.active_ref, f32[2,2,512,256]{3,2,1,0:T(8,128)S(1)} %get-tuple-element.59.slope_ref, ...), custom_call_target="tpu_custom_call" | custom-call | flops 1073741824 | bytes 6299660 | tf_op jit(solution)/shard_map/post_grads/pallas_call | solution.py:44
  102.4 2.1 %collective-permute-done.26.other_ref = f32[648,256]{1,0:T(8,128)S(1)} collective-permute-done((f32[648,256]{1,0:T(8,128)S(1)}, f32[648,256]{1,0:T(8,128)S(1)}, u32[]{:S(2)}, u32[]{:S(2)}) %collective-permute-start.26) | collective-permute-done | bytes 663584 | tf_op jit(solution)/shard_map/ppermute | solution.py:24
  105.1 16.9 %all_to_all.22 = bf16[8,80,256]{2,1,0:T(8,128)(2,1)S(1)} all-to-all(bf16[8,80,256]{2,1,0:T(8,128)(2,1)S(1)} %bitcast.24), channel_id=1, replica_groups={{0,4,8,12,16,20,24,28},{2,6,10,14,18,22,26,30},{1,5,9,13,17,21,25,29},{..., dimensions={0} | all-to-all | bytes 655360 | tf_op jit(solution)/shard_map/all_to_all | solution.py:524
  122.7 21.6 %all_to_all.23 = f32[8,88,256]{2,1,0:T(8,128)S(1)} all-to-all(f32[8,88,256]{2,1,0:T(8,128)S(1)} %bitcast.20), channel_id=1, replica_groups={{0,4,8,12,16,20,24,28},{2,6,10,14,18,22,26,30},{1,5,9,13,17,21,25,29},{..., dimensions={0} | all-to-all | bytes 1441792 | tf_op jit(solution)/shard_map/all_to_all | solution.py:524
  144.3 2.2 %collective-permute-done.27.other_ref = f32[704,256]{1,0:T(8,128)S(1)} collective-permute-done((f32[704,256]{1,0:T(8,128)S(1)}, f32[704,256]{1,0:T(8,128)S(1)}, u32[]{:S(2)}, u32[]{:S(2)}) %collective-permute-start.27) | collective-permute-done | bytes 720928 | tf_op jit(solution)/shard_map/ppermute | solution.py:24
  146.5 1.9 %last.1 = (f32[256,512]{1,0:T(8,128)}, f32[512,256]{1,0:T(8,128)}, f32[256,256]{1,0:T(8,128)}, f32[8,128]{1,0:T(8,128)S(1)}) custom-call(s32[3]{0:T(128)S(1)} %pad_add_fusion.refs_0_.meta, f32[704,256]{1,0:T(8,128)S(1)} %bitcast.22, f32[704,256]{1,0:T(8,128)S(1)} %collective-permute-done.27.other_ref), custom_call_target="tpu_custom_call" | custom-call | bytes 1441804 | tf_op jit(solution)/shard_map/last/pallas_call | solution.py:44
  (65 shorter events, 11.7 us)
Async XLA Ops:
  0.6 19.4 %copy-start = (s32[16,2,512]{2,1,0:T(2,128)S(1)}, s32[16,2,512]{2,1,0:T(2,128)}, u32[]{:S(2)}) copy-start(s32[16,2,512]{2,1,0:T(2,128)} %param.10) | copy-start | bytes 196612
  0.6 10.4 %collective-permute-start = (bf16[256,512]{1,0:T(8,128)(2,1)}, bf16[256,512]{1,0:T(8,128)(2,1)S(1)}, u32[]{:S(2)}, u32[]{:S(2)}) collective-permute-start(bf16[256,512]{1,0:T(8,128)(2,1)} %w_in_ref.1), channel_id=1, source_target_pairs={{0,1},{1,0},{2,3},{3,2},{4,5},{5,4},{6,7},{7,6},{8,9},{9,8},{10,11... | collective-permute-start | bytes 786440 | tf_op jit(solution)/shard_map/ppermute | solution.py:24
  3.7 12.1 %collective-permute-start.1 = (bf16[512,256]{1,0:T(8,128)(2,1)}, bf16[512,256]{1,0:T(8,128)(2,1)S(1)}, u32[]{:S(2)}, u32[]{:S(2)}) collective-permute-start(bf16[512,256]{1,0:T(8,128)(2,1)} %w_out_ref.3), channel_id=1, source_target_pairs={{0,1},{1,0},{2,3},{3,2},{4,5},{5,4},{6,7},{7,6},{8,9},{9,8},{10,11... | collective-permute-start | bytes 786440 | tf_op jit(solution)/shard_map/ppermute | solution.py:24
  8.5 28.2 %copy-start.5 = (bf16[256,256]{1,0:T(8,128)(2,1)S(1)}, bf16[256,256]{1,0:T(8,128)(2,1)}, u32[]{:S(2)}) copy-start(bf16[256,256]{1,0:T(8,128)(2,1)} %bil_ref.1) | copy-start | bytes 393220
  17.0 11.8 %collective-permute-start.2 = (bf16[2,256,256]{2,1,0:T(8,128)(2,1)S(1)}, bf16[2,256,256]{2,1,0:T(8,128)(2,1)S(1)}, u32[]{:S(2)}, u32[]{:S(2)}) collective-permute-start(bf16[2,256,256]{2,1,0:T(8,128)(2,1)S(1)} %mlp_pre.1.refs_4_.refs_2_), channel_id=1, source_target_pairs={{0,1},{1,0},{2,3},{3,2},{4,5},{5,4},{6,7},{7,6},{8,9},{9,8},{10,11... | collective-permute-start | bytes 786440 | tf_op jit(solution)/shard_map/ppermute | solution.py:24
  19.9 10.2 %collective-permute-start.4 = (bf16[2,256,256]{2,1,0:T(8,128)(2,1)S(1)}, bf16[2,256,256]{2,1,0:T(8,128)(2,1)S(1)}, u32[]{:S(2)}, u32[]{:S(2)}) collective-permute-start(bf16[2,256,256]{2,1,0:T(8,128)(2,1)S(1)} %get-tuple-element.62.refs_6_), channel_id=1, source_target_pairs={{0,2},{2,0},{4,6},{6,4},{8,10},{10,8},{12,14},{14,12},{16,18},{18,... | collective-permute-start | bytes 786440 | tf_op jit(solution)/shard_map/ppermute | solution.py:24
  20.3 21.5 %collective-permute-start.6 = (bf16[2,256,256]{2,1,0:T(8,128)(2,1)S(1)}, bf16[2,256,256]{2,1,0:T(8,128)(2,1)S(1)}, u32[]{:S(2)}, u32[]{:S(2)}) collective-permute-start(bf16[2,256,256]{2,1,0:T(8,128)(2,1)S(1)} %get-tuple-element.62.refs_6_), channel_id=1, source_target_pairs={{4,0},{6,2},{8,4},{10,6},{12,8},{14,10},{20,16},{22,18},{24,20},{2... | collective-permute-start | bytes 786440 | tf_op jit(solution)/shard_map/ppermute | solution.py:24
  21.6 20.2 %collective-permute-start.5 = (bf16[2,256,256]{2,1,0:T(8,128)(2,1)S(1)}, bf16[2,256,256]{2,1,0:T(8,128)(2,1)S(1)}, u32[]{:S(2)}, u32[]{:S(2)}) collective-permute-start(bf16[2,256,256]{2,1,0:T(8,128)(2,1)S(1)} %get-tuple-element.62.refs_6_), channel_id=1, source_target_pairs={{0,4},{2,6},{4,8},{6,10},{8,12},{10,14},{16,20},{18,22},{20,24},{2... | collective-permute-start | bytes 786440 | tf_op jit(solution)/shard_map/ppermute | solution.py:24
  26.2 20.9 %collective-permute-start.11 = (bf16[1,256,256]{2,1,0:T(8,128)(2,1)S(1)}, bf16[1,256,256]{2,1,0:T(8,128)(2,1)S(1)}, u32[]{:S(2)}, u32[]{:S(2)}) collective-permute-start(bf16[1,256,256]{2,1,0:T(8,128)(2,1)S(1)} %get-tuple-element.80), channel_id=1, source_target_pairs={{0,16},{2,18},{4,20},{6,22},{8,24},{10,26},{12,28},{14,30},{16,0},... | collective-permute-start | bytes 393224 | tf_op jit(solution)/shard_map/ppermute | solution.py:24
  28.8 18.4 %collective-permute-start.13 = (bf16[1,256,256]{2,1,0:T(8,128)(2,1)S(1)}, bf16[1,256,256]{2,1,0:T(8,128)(2,1)S(1)}, u32[]{:S(2)}, u32[]{:S(2)}) collective-permute-start(bf16[1,256,256]{2,1,0:T(8,128)(2,1)S(1)} %get-tuple-element.80), channel_id=1, source_target_pairs={{4,16},{6,18},{8,20},{10,22},{12,24},{14,26},{20,0},{22,2},{24,4},... | collective-permute-start | bytes 393224 | tf_op jit(solution)/shard_map/ppermute | solution.py:24
  30.1 17.1 %collective-permute-start.9 = (bf16[1,256,256]{2,1,0:T(8,128)(2,1)S(1)}, bf16[1,256,256]{2,1,0:T(8,128)(2,1)S(1)}, u32[]{:S(2)}, u32[]{:S(2)}) collective-permute-start(bf16[1,256,256]{2,1,0:T(8,128)(2,1)S(1)} %get-tuple-element.80), channel_id=1, source_target_pairs={{0,20},{2,22},{4,24},{6,26},{8,28},{10,30},{16,4},{18,6},{20,8},{2... | collective-permute-start | bytes 393224 | tf_op jit(solution)/shard_map/ppermute | solution.py:24
  41.8 6.0 %collective-permute-start.7 = (bf16[2,256,256]{2,1,0:T(8,128)(2,1)S(1)}, bf16[2,256,256]{2,1,0:T(8,128)(2,1)S(1)}, u32[]{:S(2)}, u32[]{:S(2)}) collective-permute-start(bf16[2,256,256]{2,1,0:T(8,128)(2,1)S(1)} %collective-permute-done.5.refs_9_), channel_id=1, source_target_pairs={{0,2},{2,0},{4,6},{6,4},{8,10},{10,8},{12,14},{14,12},{16,18},{18,... | collective-permute-start | bytes 786440 | tf_op jit(solution)/shard_map/ppermute | solution.py:24
  41.9 5.9 %collective-permute-start.8 = (bf16[2,256,256]{2,1,0:T(8,128)(2,1)S(1)}, bf16[2,256,256]{2,1,0:T(8,128)(2,1)S(1)}, u32[]{:S(2)}, u32[]{:S(2)}) collective-permute-start(bf16[2,256,256]{2,1,0:T(8,128)(2,1)S(1)} %collective-permute-done.6.refs_10_), channel_id=1, source_target_pairs={{0,2},{2,0},{4,6},{6,4},{8,10},{10,8},{12,14},{14,12},{16,18},{18,... | collective-permute-start | bytes 786440 | tf_op jit(solution)/shard_map/ppermute | solution.py:24
  47.1 6.1 %collective-permute-start.12 = (bf16[1,256,256]{2,1,0:T(8,128)(2,1)S(1)}, bf16[1,256,256]{2,1,0:T(8,128)(2,1)S(1)}, u32[]{:S(2)}, u32[]{:S(2)}) collective-permute-start(bf16[1,256,256]{2,1,0:T(8,128)(2,1)S(1)} %collective-permute-done.11.refs_11_), channel_id=1, source_target_pairs={{0,2},{2,0},{4,6},{6,4},{8,10},{10,8},{12,14},{14,12},{16,18},{18,... | collective-permute-start | bytes 393224 | tf_op jit(solution)/shard_map/ppermute | solution.py:24
  47.2 5.9 %collective-permute-start.10 = (bf16[1,256,256]{2,1,0:T(8,128)(2,1)S(1)}, bf16[1,256,256]{2,1,0:T(8,128)(2,1)S(1)}, u32[]{:S(2)}, u32[]{:S(2)}) collective-permute-start(bf16[1,256,256]{2,1,0:T(8,128)(2,1)S(1)} %collective-permute-done.9.refs_9_), channel_id=1, source_target_pairs={{0,2},{2,0},{4,6},{6,4},{8,10},{10,8},{12,14},{14,12},{16,18},{18,... | collective-permute-start | bytes 393224 | tf_op jit(solution)/shard_map/ppermute | solution.py:24
  47.7 5.5 %collective-permute-start.14 = (bf16[1,256,256]{2,1,0:T(8,128)(2,1)S(1)}, bf16[1,256,256]{2,1,0:T(8,128)(2,1)S(1)}, u32[]{:S(2)}, u32[]{:S(2)}) collective-permute-start(bf16[1,256,256]{2,1,0:T(8,128)(2,1)S(1)} %collective-permute-done.13.refs_13_), channel_id=1, source_target_pairs={{0,2},{2,0},{4,6},{6,4},{8,10},{10,8},{12,14},{14,12},{16,18},{18,... | collective-permute-start | bytes 393224 | tf_op jit(solution)/shard_map/ppermute | solution.py:24
  52.7 6.8 %collective-permute-start.17 = (f32[4,256,256]{2,1,0:T(8,128)S(1)}, f32[4,256,256]{2,1,0:T(8,128)S(1)}, u32[]{:S(2)}, u32[]{:S(2)}) collective-permute-start(f32[4,256,256]{2,1,0:T(8,128)S(1)} %get-tuple-element.92), channel_id=1, source_target_pairs={{0,2},{2,0},{4,6},{6,4},{8,10},{10,8},{12,14},{14,12},{16,18},{18,... | collective-permute-start | bytes 3145736 | tf_op jit(solution)/shard_map/ppermute | solution.py:24
  57.1 3.8 %collective-permute-start.20 = (f32[3,256,256]{2,1,0:T(8,128)S(1)}, f32[3,256,256]{2,1,0:T(8,128)S(1)}, u32[]{:S(2)}, u32[]{:S(2)}) collective-permute-start(f32[3,256,256]{2,1,0:T(8,128)S(1)} %get-tuple-element.97), channel_id=1, source_target_pairs={{0,2},{2,0},{4,6},{6,4},{8,10},{10,8},{12,14},{14,12},{16,18},{18,... | collective-permute-start | bytes 2359304 | tf_op jit(solution)/shard_map/ppermute | solution.py:24
  57.3 40.7 %collective-permute-start.15 = (f32[1032,256]{1,0:T(8,128)S(1)}, f32[1032,256]{1,0:T(8,128)S(1)}, u32[]{:S(2)}, u32[]{:S(2)}) collective-permute-start(f32[1032,256]{1,0:T(8,128)S(1)} %get-tuple-element.84.refs_0_), channel_id=1, source_target_pairs={{0,1},{1,0},{2,3},{3,2},{4,5},{5,4},{6,7},{7,6},{8,9},{9,8},{10,11... | collective-permute-start | bytes 3170312 | tf_op jit(solution)/shard_map/ppermute | solution.py:24
  57.8 9.0 %collective-permute-start.16 = (f32[2,256,256]{2,1,0:T(8,128)S(1)}, f32[2,256,256]{2,1,0:T(8,128)S(1)}, u32[]{:S(2)}, u32[]{:S(2)}) collective-permute-start(f32[2,256,256]{2,1,0:T(8,128)S(1)} %get-tuple-element.90), channel_id=1, source_target_pairs={{0,2},{2,0},{4,6},{6,4},{8,10},{10,8},{12,14},{14,12},{16,18},{18,... | collective-permute-start | bytes 1572872 | tf_op jit(solution)/shard_map/ppermute | solution.py:24
  57.9 36.7 %collective-permute-start.3 = (bf16[2,2,256,256]{3,2,1,0:T(8,128)(2,1)S(1)}, bf16[2,2,256,256]{3,2,1,0:T(8,128)(2,1)S(1)}, u32[]{:S(2)}, u32[]{:S(2)}) collective-permute-start(bf16[2,2,256,256]{3,2,1,0:T(8,128)(2,1)S(1)} %bitcast.16), channel_id=1, source_target_pairs={{0,1},{1,0},{2,3},{3,2},{4,5},{5,4},{6,7},{7,6},{8,9},{9,8},{10,11... | collective-permute-start | bytes 1572872 | tf_op jit(solution)/shard_map/ppermute | solution.py:24
  59.5 11.7 %collective-permute-start.18 = (bf16[2,256,256]{2,1,0:T(8,128)(2,1)S(1)}, bf16[2,256,256]{2,1,0:T(8,128)(2,1)S(1)}, u32[]{:S(2)}, u32[]{:S(2)}) collective-permute-start(bf16[2,256,256]{2,1,0:T(8,128)(2,1)S(1)} %get-tuple-element.93), channel_id=1, source_target_pairs={{4,0},{6,2},{8,4},{10,6},{12,8},{14,10},{20,16},{22,18},{24,20},{2... | collective-permute-start | bytes 786440 | tf_op jit(solution)/shard_map/ppermute | solution.py:24
  60.9 19.0 %collective-permute-start.19 = (bf16[2,256,256]{2,1,0:T(8,128)(2,1)S(1)}, bf16[2,256,256]{2,1,0:T(8,128)(2,1)S(1)}, u32[]{:S(2)}, u32[]{:S(2)}) collective-permute-start(bf16[2,256,256]{2,1,0:T(8,128)(2,1)S(1)} %get-tuple-element.94), channel_id=1, source_target_pairs={{0,4},{2,6},{4,8},{6,10},{8,12},{10,14},{16,20},{18,22},{20,24},{2... | collective-permute-start | bytes 786440 | tf_op jit(solution)/shard_map/ppermute | solution.py:24
  66.7 27.9 %copy-start.4 = (bf16[256,512]{1,0:T(8,128)(2,1)S(1)}, bf16[256,512]{1,0:T(8,128)(2,1)}, u32[]{:S(2)}) copy-start(bf16[256,512]{1,0:T(8,128)(2,1)} %w_in_ref.1) | copy-start | bytes 786436
  66.8 19.0 %collective-permute-start.21 = (bf16[1,256,256]{2,1,0:T(8,128)(2,1)S(1)}, bf16[1,256,256]{2,1,0:T(8,128)(2,1)S(1)}, u32[]{:S(2)}, u32[]{:S(2)}) collective-permute-start(bf16[1,256,256]{2,1,0:T(8,128)(2,1)S(1)} %get-tuple-element.98), channel_id=1, source_target_pairs={{4,16},{6,18},{8,20},{10,22},{12,24},{14,26},{20,0},{22,2},{24,4},... | collective-permute-start | bytes 393224 | tf_op jit(solution)/shard_map/ppermute | solution.py:24
  71.3 15.1 %collective-permute-start.22 = (bf16[1,256,256]{2,1,0:T(8,128)(2,1)S(1)}, bf16[1,256,256]{2,1,0:T(8,128)(2,1)S(1)}, u32[]{:S(2)}, u32[]{:S(2)}) collective-permute-start(bf16[1,256,256]{2,1,0:T(8,128)(2,1)S(1)} %get-tuple-element.99), channel_id=1, source_target_pairs={{0,16},{2,18},{4,20},{6,22},{8,24},{10,26},{12,28},{14,30},{16,0},... | collective-permute-start | bytes 393224 | tf_op jit(solution)/shard_map/ppermute | solution.py:24
  79.8 8.7 %collective-permute-start.23 = (bf16[1,256,256]{2,1,0:T(8,128)(2,1)S(1)}, bf16[1,256,256]{2,1,0:T(8,128)(2,1)S(1)}, u32[]{:S(2)}, u32[]{:S(2)}) collective-permute-start(bf16[1,256,256]{2,1,0:T(8,128)(2,1)S(1)} %get-tuple-element.100), channel_id=1, source_target_pairs={{0,20},{2,22},{4,24},{6,26},{8,28},{10,30},{16,4},{18,6},{20,8},{2... | collective-permute-start | bytes 393224 | tf_op jit(solution)/shard_map/ppermute | solution.py:24
  85.6 12.4 %copy-start.2 = (bf16[512,256]{1,0:T(8,128)(2,1)S(1)}, bf16[512,256]{1,0:T(8,128)(2,1)}, u32[]{:S(2)}) copy-start(bf16[512,256]{1,0:T(8,128)(2,1)} %w_out_ref.3) | copy-start | bytes 786436
  85.8 14.5 %collective-permute-start.25 = (bf16[1,256,256]{2,1,0:T(8,128)(2,1)S(1)}, bf16[1,256,256]{2,1,0:T(8,128)(2,1)S(1)}, u32[]{:S(2)}, u32[]{:S(2)}) collective-permute-start(bf16[1,256,256]{2,1,0:T(8,128)(2,1)S(1)} %convert_element_type.3.refs_2_), channel_id=1, source_target_pairs={{0,1},{1,0},{2,3},{3,2},{4,5},{5,4},{6,7},{7,6},{8,9},{9,8},{10,11... | collective-permute-start | bytes 393224 | tf_op jit(solution)/shard_map/ppermute | solution.py:24
  88.6 11.7 %collective-permute-start.24 = (bf16[1,256,256]{2,1,0:T(8,128)(2,1)S(1)}, bf16[1,256,256]{2,1,0:T(8,128)(2,1)S(1)}, u32[]{:S(2)}, u32[]{:S(2)}) collective-permute-start(bf16[1,256,256]{2,1,0:T(8,128)(2,1)S(1)} %near_post.1.refs_0_), channel_id=1, source_target_pairs={{0,1},{1,0},{2,3},{3,2},{4,5},{5,4},{6,7},{7,6},{8,9},{9,8},{10,11... | collective-permute-start | bytes 393224 | tf_op jit(solution)/shard_map/ppermute | solution.py:24
  102.3 2.2 %collective-permute-start.26 = (f32[648,256]{1,0:T(8,128)S(1)}, f32[648,256]{1,0:T(8,128)S(1)}, u32[]{:S(2)}, u32[]{:S(2)}) collective-permute-start(f32[648,256]{1,0:T(8,128)S(1)} %get-tuple-element.103), channel_id=1, source_target_pairs={{0,2},{2,0},{4,6},{6,4},{8,10},{10,8},{12,14},{14,12},{16,18},{18,... | collective-permute-start | bytes 1990664 | tf_op jit(solution)/shard_map/ppermute | solution.py:24
  144.3 2.2 %collective-permute-start.27 = (f32[704,256]{1,0:T(8,128)S(1)}, f32[704,256]{1,0:T(8,128)S(1)}, u32[]{:S(2)}, u32[]{:S(2)}) collective-permute-start(f32[704,256]{1,0:T(8,128)S(1)} %bitcast.21), channel_id=1, source_target_pairs={{0,2},{2,0},{4,6},{6,4},{8,10},{10,8},{12,14},{14,12},{16,18},{18,... | collective-permute-start | bytes 2162696 | tf_op jit(solution)/shard_map/ppermute | solution.py:24
  (3 other events, 13.5 us)

commit v2 on v1

--- a/solution.py
+++ b/solution.py
@@ -82,37 +82,37 @@
     return h * whole, slope
 
 
-def mlp_kernel(kinds, ready, near, groups, *refs):
+def mlp_own_kernel(meta, x0_ref, x1_ref, w_in_ref, w_out_ref, sum0_ref, sum1_ref):
+    for x_ref, out_ref in ((x1_ref, sum1_ref), (x0_ref, sum0_ref)):
+        for t in range(2):
+            hidden = dot(x_ref[sub_tile(meta[2], t)], w_in_ref[...])
+            out_ref[t] = dot(gelu_parts(hidden)[0].astype(bf16), w_out_ref[...])
+
+
+def mlp_kernel(begun, groups, meta, x_ref, *refs):
     refs = list(refs)
-    meta, x_ref = refs[:2]
-    del refs[:2]
-    near_ref = refs.pop() if near else None
-    out_ref = refs.pop()
-    start_ref = refs.pop(0) if ready else None
-    xb = meta[2]
-    for place, kind in enumerate(kinds):
-        for t in range(2):
-            x = x_ref[kind, sub_tile(xb, t)]
-            total = start_ref[kind, t] if ready else x.astype(f32)
-            for g in range(groups):
-                hidden = dot(x, refs[2 * g][...])
-                active = gelu_parts(hidden)[0].astype(bf16)
-                total = total + dot(active, refs[2 * g + 1][...])
-            if len(kinds) == 1:
-                out_ref[t] = total.astype(out_ref.dtype)
-                if near and t == 0:
-                    near_ref[0] = total.astype(out_ref.dtype)
-            else:
-                out_ref[place, t] = total.astype(out_ref.dtype)
+    start_ref = refs.pop(0) if begun else None
+    outs = refs[2 * groups :]
+    for t in range(2):
+        x = x_ref[sub_tile(meta[2], t)]
+        total = start_ref[t] if begun else None
+        for g in range(groups):
+            hidden = dot(x, refs[2 * g][...])
+            part = dot(gelu_parts(hidden)[0].astype(bf16), refs[2 * g + 1][...])
+            total = part if total is None else total + part
+        embedded = (x.astype(f32) + total).astype(bf16)
+        outs[0][t] = embedded
+        if t == 0 and len(outs) == 2:
+            outs[1][0] = embedded
 
 
 def hidden_kernel(groups, meta, w_in_ref, *refs):
     w_t = w_in_ref[...].T
-    outs = refs[groups:]
+    outs = refs[2 * groups :]
     for kind in range(2):
         for g in range(groups):
             for u in range(2):
-                active, slope = gelu_parts(dot(w_t, refs[g][kind, u].T))
+                active, slope = gelu_parts(dot(w_t, refs[kind * groups + g][u].T))
                 outs[2 * kind][g, u] = active.astype(bf16)
                 outs[2 * kind + 1][g, u] = slope
 
@@ -148,7 +148,7 @@
         for g in range(groups):
             place = pl.ds(pl.multiple_of(owner(meta, g, groups) * rows, rows), rows)
             back = back_all[a, place, :]
-            sums = weight_part(back, x_refs[g][0, u], active_ref[g, u], slope_ref[g, u], w_out_ref[...], sums)
+            sums = weight_part(back, x_refs[g][u], active_ref[g, u], slope_ref[g, u], w_out_ref[...], sums)
     in_ref[...], out_ref[...] = sums
     bil_grad_ref[...] = bil_grad
     loss = query_refs[0][2 * site_rows :]
@@ -167,7 +167,7 @@
         u = sub_tile(xb, t)
         for g in range(groups):
             back = (near_refs, far_refs)[t][g][0]
-            sums = weight_part(back, x_refs[g][1, u], active_ref[g, u], slope_ref[g, u], w_out_ref[...], sums)
+            sums = weight_part(back, x_refs[g][u], active_ref[g, u], slope_ref[g, u], w_out_ref[...], sums)
     hid = in0.shape[0]
     half = mine_ref.shape[0]
     whole[:hid] = sums[0]
@@ -187,35 +187,58 @@
     kept_ref[:rows] = whole[pl.ds(pl.multiple_of(meta[0] // 2 * rows, 16), rows), :]
 
 
-def total_kernel(meta, got_ref, kept_ref, out_ref):
+def exponent(largest):
+    return 14.0 - jnp.ceil(jnp.log2(jnp.maximum(largest, 1e-30)))
+
+
+def total_kernel(meta, got_ref, kept_ref, out_ref, coded):
     rows = kept_ref.shape[0] - 8
     chips = got_ref.shape[0] // rows
     total = kept_ref[:rows]
     for n in range(chips):
         piece = got_ref[n * rows : (n + 1) * rows, :].astype(f32)
         total = total + jnp.where(n == meta[0] // 2, 0.0, piece)
+    width = total.shape[1]
+    line = lax.broadcasted_iota(jnp.int32, (16, width), 0)
+    notes = jnp.zeros((16, width), f32)
+    for k in range(rows // 16):
+        part = total[k * 16 : (k + 1) * 16]
+        power = exponent(jnp.max(jnp.max(jnp.abs(part), 0, keepdims=True), 1, keepdims=True))
+        coded[k * 16 : (k + 1) * 16, :] = jnp.round(part * jnp.exp2(power)).astype(jnp.int32).astype(jnp.int16)
+        notes = jnp.where(line == k, power, notes)
+    loss = kept_ref[rows : rows + 1]
+    power = exponent(jnp.max(loss, 1, keepdims=True))
+    scaled = loss * jnp.exp2(power)
+    high = jnp.floor(scaled)
+    low = jnp.floor((scaled - high) * 16384.0)
+    for k, note in ((13, power), (14, high), (15, low)):
+        notes = jnp.where(line == k, note, notes)
+    coded[rows:, :] = notes.astype(jnp.int32).astype(jnp.int16)
     for n in range(chips):
-        first = n * (rows + 8)
-        out_ref[first : first + rows, :] = total
-        out_ref[first + rows : first + rows + 8, :] = kept_ref[rows:]
+        out_ref[n * (rows + 16) : (n + 1) * (rows + 16), :] = coded[...]
 
 
 def last_kernel(chips, share, meta, mine_ref, other_ref, in_ref, out_ref, bil_ref, loss_ref, whole):
     core = lax.rem(meta[0], 2)
     half = whole.shape[0] // 2
     rows = half // chips
-    loss = jnp.zeros((8, 128), f32)
+    loss = jnp.zeros((1, 128), f32)
     for n in range(chips):
-        first = n * (rows + 8)
+        first = n * (rows + 16)
         for ref, side in ((mine_ref, core), (other_ref, 1 - core)):
-            place = side * half + n * rows
-            whole[pl.ds(pl.multiple_of(place, 8), rows), :] = ref[first : first + rows, :]
-        loss = loss + mine_ref[first + rows : first + rows + 8, :128]
+            piece = ref[first : first + rows + 16, :].astype(jnp.int32).astype(f32)
+            notes = piece[rows:]
+            for k in range(rows // 16):
+                place = side * half + n * rows + k * 16
+                part = piece[k * 16 : (k + 1) * 16] * jnp.exp2(-notes[k : k + 1])
+                whole[pl.ds(pl.multiple_of(place, 16), 16), :] = part
+            if ref is mine_ref:
+                loss = loss + (notes[14:15] + notes[15:16] / 16384.0)[:, :128] * jnp.exp2(-notes[13:14, :128])
     hid = out_ref.shape[0]
     in_ref[...] = whole[:hid].T
     out_ref[...] = whole[hid : 2 * hid]
     bil_ref[...] = whole[2 * hid :]
-    loss_ref[...] = loss * share
+    loss_ref[...] = jnp.broadcast_to(loss * share, loss_ref.shape)
 
 
 def pair_kernel(slots, foreign, first, last, groups, site_rows, depth, heavy, out_scale, *refs):
@@ -280,7 +303,8 @@
         post_t = post.T
         places = []
         for n, t in chunk:
-            dy, z_slot = slots[n]
+            sign, z_slot = slots[n]
+            dy = sign * (1 - 2 * lax.rem(yg, 2))
             if depth == 2:
                 z_other = zg if z_slot == 0 else 1 - zg
             else:
@@ -397,11 +421,16 @@
     def side(i):
         return i ^ half
 
-    def along_y(step):
-        return lambda i: i + step * depth if 0 <= i // depth % 4 + step < 4 else None
-
-    def both(step):
-        return lambda i: None if along_y(step)(i) is None else along_y(step)(i) ^ half
+    def along_y(sign):
+        def target(i):
+            y = i // depth % 4
+            step = sign * (1 - 2 * (y % 2))
+            return i + step * depth if 0 <= y + step < 4 else None
+
+        return target
+
+    def both(sign):
+        return lambda i: None if along_y(sign)(i) is None else along_y(sign)(i) ^ half
 
     z_slots = (0, 1) if depth == 2 else (0, -1, 1)
 
@@ -418,41 +447,37 @@
 
     w_ins, w_outs = over_mlp(w_in), over_mlp(w_out)
     meta = jnp.stack([tile_here, member, xb]).astype(jnp.int32)
-    x = jnp.transpose(features[0], (2, 1, 0, 3))
+    x0, x1 = [jnp.transpose(features[0, :, :, kind], (1, 0, 2)) for kind in (0, 1)]
+    x0s, x1s = over_mlp(x0), over_mlp(x1)
     labels = lax.dynamic_index_in_dim(partner, tile_here, 0, keepdims=False)[:, None, :]
     flat_counts = counts.reshape(-1)
-    rows4 = (2, 2, row_part, width)
     rows3 = (2, row_part, width)
     flops = 4 * row_part * width * hid * 4
-    begun = call(
-        functools.partial(mlp_kernel, (0, 1), False, False, 1), "mlp_own", [(rows4, f32)], [meta, x, w_in, w_out], flops
-    )[0]
+    begun = call(mlp_own_kernel, "mlp_own", [(rows3, f32)] * 2, [meta, x0, x1, w_in, w_out], flops)
     pairs_w = [w for pair in zip(w_ins[1:], w_outs[1:], strict=True) for w in pair]
-    results = []
-    for kind, name in ((1, "mlp_post"), (0, "mlp_pre")):
-        near = kind == 1
-        results += call(
-            functools.partial(mlp_kernel, (kind,), True, near, groups - 1),
-            name,
-            [(rows3, bf16)] + [((1, row_part, width), bf16)] * near,
-            [meta, x, begun, *pairs_w],
-            flops * (groups - 1) // 2,
-        )
-    post, post_near, pre = results
-
-    near = {dy: moved(post, "tile", along_y(-dy)) for dy in (-1, 1)}
-    pres = over_mlp(pre)
+    more = functools.partial(mlp_kernel, True, groups - 1)
+    near_shape = (1, row_part, width)
+    post, post_near = call(
+        more, "mlp_post", [(rows3, bf16), (near_shape, bf16)], [meta, x1, begun[1], *pairs_w], flops * (groups - 1) // 2
+    )
+    pre = call(more, "mlp_pre", [(rows3, bf16)], [meta, x0, begun[0], *pairs_w], flops * (groups - 1) // 2)[0]
+    if groups == 2:
+        full = functools.partial(mlp_kernel, False, 2)
+        pres = [pre, call(full, "mlp_pre_other", [(rows3, bf16)], [meta, x0s[1], w_in, w_out, *pairs_w], flops)[0]]
+    else:
+        pres = over_mlp(pre)
+
+    near = {dy: moved(post, "tile", along_y(dy)) for dy in (-1, 1)}
     far = {0: moved(post_near, "tile", side)}
-    for dy in (-1, 1):
-        far[dy] = moved(after(post_near, pres[-1]), "tile", both(-dy))
     sizes = (groups, site_rows, depth, heavy, out_scale)
     fixed = [meta, flat_counts, labels]
     grads_own, (query, query_t, *state) = pair_call(
         "pairs_own", [(0, z) for z in z_slots], False, True, False, fixed + [bilinear, *pres], [post] + from_z(post), sizes
     )
     queries = [query, query_t]
-    xs = over_mlp(after(x, pres[-1]))
-    near = {dy: after(near[dy], state[1]) for dy in (-1, 1)}
+    for dy in (-1, 1):
+        far[dy] = moved(after(post_near, state[1]), "tile", both(dy))
+    near = {dy: after(near[dy], state[1], x1s[-1]) for dy in (-1, 1)}
     near_z = {dy: from_z(near[dy]) for dy in (-1, 1)}
     grads_near, state = pair_call(
         "pairs_near", [(dy, 0) for dy in (-1, 1)], False, False, False, fixed + queries + state, [near[-1], near[1]], sizes
@@ -484,22 +509,21 @@
     near_back = [moved(total, "tile", along_y(dy)) for total, dy in zip(near_sums, (-1, 1), strict=True)]
     query_parts = over_mlp(query_part)
     far_sums = summed(grads_far[:1] + back_from_z(grads_far[1:]), [(0, 1), (1, 1), (2, 1)], bf16, "far_sums")
-    far_back = [
-        moved(total, "tile", target) for total, target in zip(far_sums, (both(-1), side, both(1)), strict=True)
-    ]
+    far_back = [moved(far_sums[0], "tile", both(-1)), moved(far_sums[2], "tile", both(1))]
+    far_back.append(moved(after(far_sums[1], near_back[0]), "tile", side))
     part_t = (groups, 2, hid, row_part)
     active_0, slope_0, active_1, slope_1 = call(
         functools.partial(hidden_kernel, groups),
         "hidden",
         [(part_t, bf16), (part_t, f32)] * 2,
-        [meta, w_in, *xs],
+        [meta, w_in, *x0s, *x1s],
         flops * groups // 2,
     )
     in_0, out_0, bil_0, loss = call(
         functools.partial(pre_kernel, groups),
         "pre_grads",
         [((hid, width), f32)] * 2 + [((width, width), f32), ((8, width), f32)],
-        [meta, w_out, bilinear, active_0, slope_0, *query_parts, *pres, *xs],
+        [meta, w_out, bilinear, active_0, slope_0, *query_parts, *pres, *x0s],
         flops * groups,
         [pltpu.VMEM((2, site_rows, width), bf16)] * 2,
     )
@@ -511,7 +535,7 @@
         functools.partial(post_kernel, groups),
         "post_grads",
         [((half_rows, width), f32), ((half_rows + 8, width), f32)],
-        [meta, w_out, active_1, slope_1, in_0, out_0, bil_0, loss, *near_post, *far_post, *xs],
+        [meta, w_out, active_1, slope_1, in_0, out_0, bil_0, loss, *near_post, *far_post, *x1s],
         flops * groups,
         [pltpu.VMEM((2 * half_rows, width), f32)],
     )
@@ -531,8 +555,14 @@
         [meta, mine, moved(other, "tile", swap), loss],
         scratch=[pltpu.VMEM(half_shape, f32)],
     )
-    joined_shape = (half_rows + 8 * chips, width)
-    total = call(total_kernel, "total", [(joined_shape, f32)], [meta, to_chips(sent), kept])[0]
+    coded = (half_rows // chips + 16, width)
+    total = call(
+        total_kernel,
+        "total",
+        [((chips * coded[0], width), jnp.int16)],
+        [meta, to_chips(sent), kept],
+        scratch=[pltpu.VMEM(coded, jnp.int16)],
+    )[0]
     joined = to_chips(total)
     share = 1.0 / (2.0 * tile_count * site_rows * 27 * site_rows)
     grad_in, grad_out, grad_bilinear, pair_loss = call(

time: 149 us -> 129 us (0.87)
  waiting for transfers between devices: 29.2 us -> 19.2 us
  blocking collectives: 38.5 us -> 29.4 us
  starting transfers between devices: 42.7 us -> 40.4 us
  Pallas kernels: 33.5 us -> 35.3 us
    ppermute x28, waiting for transfers between devices: 29.2 us -> 19.2 us  [moved(): return lax.ppermute(array, axis, pairs)]
    all_to_all x2, blocking collectives: 38.5 us -> 29.4 us  [to_chips(): lax.all_to_all(array, 'tile', 0, 0, tiled=True, axis_index_groups=same_core)]
    unnamed x16 -> x13, local copies, waits for them, and re-layouts: 3.14 us -> 0.21 us
    ppermute x28, starting transfers between devices: 42.7 us -> 40.4 us  [moved(): return lax.ppermute(array, axis, pairs)]
    slice x0 -> x1, local copies, waits for them, and re-layouts: none -> 2.1 us  [local(): features[0, :, :, kind]]
    pallas_call x17 -> x18, Pallas kernels: 33.5 us -> 35.3 us  [call(): pl.pallas_call(kernel, out_shape=[jax.ShapeDtypeStruct(shape, kind) for s...]
  transfers between devices with their start and end apart: 28 -> 28, of which waited for: 8 -> 7; matrix products, arithmetic and copies ran while one was open for 1% -> 2% of each run, Pallas kernels for 18% -> 23%
where the time goes in v2:
time: 129 us; the launch traced here: 128 us
  starting transfers between devices  40.4 us (31%)
  Pallas kernels  35.3 us (27%)
  blocking collectives  29.4 us (23%)
  waiting for transfers between devices  19.2 us (15%)
  local copies, waits for them, and re-layouts  2.94 us (2%)
    ppermute x28, starting transfers between devices, moved(): return lax.ppermute(array, axis, pairs)  40.4 us
    pallas_call x18, Pallas kernels, call(): pl.pallas_call(kernel, out_shape=[jax.ShapeDtypeStruct(shape, kind) for s...  35.3 us
    all_to_all x2, blocking collectives, to_chips(): lax.all_to_all(array, 'tile', 0, 0, tiled=True, axis_index_groups=same_core)  29.4 us
    ppermute x28, waiting for transfers between devices, moved(): return lax.ppermute(array, axis, pairs)  19.2 us
  transfers between devices with their start and end apart: 28, of which 7 were waited for; matrix products, arithmetic and copies ran while one was open for 2% of the time, Pallas kernels for 23%

profile of v2, /device:TPU:0, one launch (start us, length us, event | category | flops | bytes accessed | tf_op | source)
XLA Modules:
  0.0 128.3 jit_solution(14782540402029519026)
XLA Ops:
  0.7 3.0 %collective-permute-start.2 = (bf16[256,512]{1,0:T(8,128)(2,1)}, bf16[256,512]{1,0:T(8,128)(2,1)S(1)}, u32[]{:S(2)}, u32[]{:S(2)}) collective-permute-start(bf16[256,512]{1,0:T(8,128)(2,1)} %refs_0_.1), channel_id=1, source_target_pairs={{0,1},{1,0},{2,3},{3,2},{4,5},{5,4},{6,7},{7,6},{8,9},{9,8},{10,11... | collective-permute-start | bytes 786440 | tf_op jit(solution)/shard_map/ppermute | solution.py:24
  3.8 2.1 %fusion = (bf16[1,256,2,1,256]{4,3,2,1,0:T(2,128)(2,1)S(1)}, bf16[1,256,2,1,256]{4,3,2,1,0:T(2,128)(2,1)S(1)}) fusion(bf16[1,256,2,2,256]{4,3,2,1,0:T(2,128)(2,1)} %param.6), kind=kLoop, calls=%fused_computation.4 | loop fusion | bytes 1048576 | tf_op jit(solution)/shard_map/slice | solution.py:450
  5.9 2.0 %collective-permute-start = (bf16[2,256,256]{2,1,0:T(8,128)(2,1)S(1)}, bf16[2,256,256]{2,1,0:T(8,128)(2,1)S(1)}, u32[]{:S(2)}, u32[]{:S(2)}) collective-permute-start(bf16[2,256,256]{2,1,0:T(8,128)(2,1)S(1)} %bitcast.23), channel_id=1, source_target_pairs={{0,1},{1,0},{2,3},{3,2},{4,5},{5,4},{6,7},{7,6},{8,9},{9,8},{10,11... | collective-permute-start | bytes 786440 | tf_op jit(solution)/shard_map/ppermute | solution.py:24
  8.1 1.5 %mlp_own.1 = (f32[2,256,256]{2,1,0:T(8,128)S(1)}, f32[2,256,256]{2,1,0:T(8,128)S(1)}) custom-call(s32[3]{0:T(128)S(1)} %pad_add_fusion.meta.refs_0_, bf16[2,256,256]{2,1,0:T(8,128)(2,1)S(1)} %bitcast.24, bf16[2,256,256]{2,1,0:T(8,128)(2,1)S(1)} %bitcast.18, bf16[256,512]{1,0:T(8,128)(2,1)S(1)} %copy-done.3, bf16[512,256]{1,0:T(8,128)(2,1)S(1)} %copy-done.1), custom_call_target="tpu_custom_call" | custom-call | flops 536870912 | bytes 1048588 | tf_op jit(solution)/shard_map/mlp_own/pallas_call | solution.py:44
  9.6 1.5 %collective-permute-done.2.refs_1_.refs_2_ = bf16[256,512]{1,0:T(8,128)(2,1)S(1)} collective-permute-done((bf16[256,512]{1,0:T(8,128)(2,1)}, bf16[256,512]{1,0:T(8,128)(2,1)S(1)}, u32[]{:S(2)}, u32[]{:S(2)}) %collective-permute-start.2) | collective-permute-done | bytes 262176 | tf_op jit(solution)/shard_map/ppermute | solution.py:24
  11.0 5.6 %collective-permute-done.3.refs_2_.refs_3_ = bf16[512,256]{1,0:T(8,128)(2,1)S(1)} collective-permute-done((bf16[512,256]{1,0:T(8,128)(2,1)}, bf16[512,256]{1,0:T(8,128)(2,1)S(1)}, u32[]{:S(2)}, u32[]{:S(2)}) %collective-permute-start.3) | collective-permute-done | bytes 262176 | tf_op jit(solution)/shard_map/ppermute | solution.py:24
  16.7 1.2 mlp_post.1
  17.9 2.1 %collective-permute-start.1 = (bf16[2,256,256]{2,1,0:T(8,128)(2,1)S(1)}, bf16[2,256,256]{2,1,0:T(8,128)(2,1)S(1)}, u32[]{:S(2)}, u32[]{:S(2)}) collective-permute-start(bf16[2,256,256]{2,1,0:T(8,128)(2,1)S(1)} %bitcast.20), channel_id=1, source_target_pairs={{0,1},{1,0},{2,3},{3,2},{4,5},{5,4},{6,7},{7,6},{8,9},{9,8},{10,11... | collective-permute-start | bytes 786440 | tf_op jit(solution)/shard_map/ppermute | solution.py:24
  20.3 1.6 %collective-permute-start.6 = (bf16[2,256,256]{2,1,0:T(8,128)(2,1)S(1)}, bf16[2,256,256]{2,1,0:T(8,128)(2,1)S(1)}, u32[]{:S(2)}, u32[]{:S(2)}) collective-permute-start(bf16[2,256,256]{2,1,0:T(8,128)(2,1)S(1)} %get-tuple-element.65.refs_6_), channel_id=1, source_target_pairs={{0,4},{2,6},{4,0},{6,2},{8,12},{10,14},{12,8},{14,10},{16,20},{18,... | collective-permute-start | bytes 786440 | tf_op jit(solution)/shard_map/ppermute | solution.py:24
  22.5 1.2 mlp_pre.1.refs_4_.refs_2_
  23.7 2.7 %collective-permute-start.11 = (bf16[1,256,256]{2,1,0:T(8,128)(2,1)S(1)}, bf16[1,256,256]{2,1,0:T(8,128)(2,1)S(1)}, u32[]{:S(2)}, u32[]{:S(2)}) collective-permute-start(bf16[1,256,256]{2,1,0:T(8,128)(2,1)S(1)} %get-tuple-element.83), channel_id=1, source_target_pairs={{0,16},{2,18},{4,20},{6,22},{8,24},{10,26},{12,28},{14,30},{16,0},... | collective-permute-start | bytes 393224 | tf_op jit(solution)/shard_map/ppermute | solution.py:24
  26.4 1.6 %mlp_pre_other.1.refs_5_.refs_3_ = bf16[2,256,256]{2,1,0:T(8,128)(2,1)S(1)} custom-call(s32[3]{0:T(128)S(1)} %pad_add_fusion.meta.refs_0_, bf16[2,256,256]{2,1,0:T(8,128)(2,1)S(1)} %collective-permute-done.refs_1_.x_ref.refs_5_, bf16[256,512]{1,0:T(8,128)(2,1)S(1)} %copy-done.3, bf16[512,256]{1,0:T(8,128)(2,1)S(1)} %copy-done.1, ...), custom_call_target="tpu_custom_call" | custom-call | flops 536870912 | bytes 1310732 | tf_op jit(solution)/shard_map/mlp_pre_other/pallas_call | solution.py:44
  28.0 5.1 %pairs_own.1 = (f32[2,256,256]{2,1,0:T(8,128)S(1)}, f32[2,256,256]{2,1,0:T(8,128)S(1)}, bf16[2,512,256]{2,1,0:T(8,128)(2,1)S(1)}, bf16[2,256,512]{2,1,0:T(8,128)...) custom-call(s32[3]{0:T(128)S(1)} %pad_add_fusion.meta.refs_0_, ...), custom_call_target="tpu_custom_call" | custom-call | flops 10737418240 | bytes 1184012 | tf_op jit(solution)/shard_map/pairs_own/pallas_call | solution.py:44
  33.2 4.1 %collective-permute-start.13 = (bf16[1,256,256]{2,1,0:T(8,128)(2,1)S(1)}, bf16[1,256,256]{2,1,0:T(8,128)(2,1)S(1)}, u32[]{:S(2)}, u32[]{:S(2)}) collective-permute-start(bf16[1,256,256]{2,1,0:T(8,128)(2,1)S(1)} %get-tuple-element.83), channel_id=1, source_target_pairs={{0,20},{2,22},{4,16},{6,18},{8,28},{10,30},{12,24},{14,26},{16,4},... | collective-permute-start | bytes 393224 | tf_op jit(solution)/shard_map/ppermute | solution.py:24
  38.7 4.7 %pairs_near.1 = (f32[4,256,256]{2,1,0:T(8,128)S(1)}, f32[2,256,512]{2,1,0:T(8,128)S(1)}, f32[8,512]{1,0:T(8,128)S(1)}, f32[2,8,512]{2,1,0:T(8,128)S(1)}, f32[2,1,512]{2,1,0:T(1,128)S(1)}) custom-call(s32[3]{0:T(128)S(1)} %pad_add_fusion.meta.refs_0_, ...), custom_call_target="tpu_custom_call", output_to_operand_aliasing={{1}: (5, {}), {2}: (6, {}), {3}: (7, {}), {4}: (8, {})} | custom-call | flops 10737418240 | bytes 2679052 | tf_op jit(solution)/shard_map/pairs_near/pallas_call | solution.py:44
  44.2 4.7 %pairs_near_z.1 = (f32[4,256,256]{2,1,0:T(8,128)S(1)}, f32[2,256,512]{2,1,0:T(8,128)S(1)}, f32[8,512]{1,0:T(8,128)S(1)}, f32[2,8,512]{2,1,0:T(8,128)S(1)}, f32[2,1,512]{2,1,0:T(1,128)S(1)}) custom-call(s32[3]{0:T(128)S(1)} %pad_add_fusion.meta.refs_0_, ...), custom_call_target="tpu_custom_call", output_to_operand_aliasing={{1}: (5, {}), {2}: (6, {}), {3}: (7, {}), {4}: (8, {})} | custom-call | flops 10737418240 | bytes 2679052 | tf_op jit(solution)/shard_map/pairs_near_z/pallas_call | solution.py:44
  49.4 3.9 %pairs_far.1 = (f32[3,256,256]{2,1,0:T(8,128)S(1)}, f32[3,256,256]{2,1,0:T(8,128)S(1)}, f32[1032,256]{1,0:T(8,128)S(1)}) custom-call(s32[3]{0:T(128)S(1)} %pad_add_fusion.meta.refs_0_, s32[64]{0:T(128)S(1)} %reshape.16.refs_1_, s32[2,1,512]{2,1,0:T(1,128)S(1)} %broadcast_in_dim.3.refs_2_, bf16[2,512,256]{2,1,0:T(8,128)(2,1)S(1)} %get-tuple-element.66.refs_3_, ...), custom_call_target="tpu_custom_call" | custom-call | flops 8053063680 | bytes 2941196 | tf_op jit(solution)/shard_map/pairs_far/pallas_call | solution.py:44
  55.2 5.2 %collective-permute-start.19 = (bf16[2,256,256]{2,1,0:T(8,128)(2,1)S(1)}, bf16[2,256,256]{2,1,0:T(8,128)(2,1)S(1)}, u32[]{:S(2)}, u32[]{:S(2)}) collective-permute-start(bf16[2,256,256]{2,1,0:T(8,128)(2,1)S(1)} %get-tuple-element.97), channel_id=1, source_target_pairs={{0,4},{2,6},{4,0},{6,2},{8,12},{10,14},{12,8},{14,10},{16,20},{18,... | collective-permute-start | bytes 786440 | tf_op jit(solution)/shard_map/ppermute | solution.py:24
  61.1 9.6 %collective-permute-start.22 = (bf16[1,256,256]{2,1,0:T(8,128)(2,1)S(1)}, bf16[1,256,256]{2,1,0:T(8,128)(2,1)S(1)}, u32[]{:S(2)}, u32[]{:S(2)}) collective-permute-start(bf16[1,256,256]{2,1,0:T(8,128)(2,1)S(1)} %get-tuple-element.102), channel_id=1, source_target_pairs={{0,20},{2,22},{4,16},{6,18},{8,28},{10,30},{12,24},{14,26},{16,4},... | collective-permute-start | bytes 393224 | tf_op jit(solution)/shard_map/ppermute | solution.py:24
  71.9 4.1 %collective-permute-done.19.refs_3_ = bf16[2,256,256]{2,1,0:T(8,128)(2,1)S(1)} collective-permute-done((bf16[2,256,256]{2,1,0:T(8,128)(2,1)S(1)}, bf16[2,256,256]{2,1,0:T(8,128)(2,1)S(1)}, u32[]{:S(2)}, u32[]{:S(2)}) %collective-permute-start.19) | collective-permute-done | bytes 262176 | tf_op jit(solution)/shard_map/ppermute | solution.py:24
  76.1 1.6 %collective-permute-start.25 = (bf16[1,256,256]{2,1,0:T(8,128)(2,1)S(1)}, bf16[1,256,256]{2,1,0:T(8,128)(2,1)S(1)}, u32[]{:S(2)}, u32[]{:S(2)}) collective-permute-start(bf16[1,256,256]{2,1,0:T(8,128)(2,1)S(1)} %convert_element_type.3.refs_2_), channel_id=1, source_target_pairs={{0,1},{1,0},{2,3},{3,2},{4,5},{5,4},{6,7},{7,6},{8,9},{9,8},{10,11... | collective-permute-start | bytes 393224 | tf_op jit(solution)/shard_map/ppermute | solution.py:24
  77.7 2.5 %collective-permute-done.22.refs_2_ = bf16[1,256,256]{2,1,0:T(8,128)(2,1)S(1)} collective-permute-done((bf16[1,256,256]{2,1,0:T(8,128)(2,1)S(1)}, bf16[1,256,256]{2,1,0:T(8,128)(2,1)S(1)}, u32[]{:S(2)}, u32[]{:S(2)}) %collective-permute-start.22) | collective-permute-done | bytes 131104 | tf_op jit(solution)/shard_map/ppermute | solution.py:24
  80.2 1.6 %collective-permute-done.23.refs_3_ = bf16[1,256,256]{2,1,0:T(8,128)(2,1)S(1)} collective-permute-done((bf16[1,256,256]{2,1,0:T(8,128)(2,1)S(1)}, bf16[1,256,256]{2,1,0:T(8,128)(2,1)S(1)}, u32[]{:S(2)}, u32[]{:S(2)}) %collective-permute-start.23) | collective-permute-done | bytes 131104 | tf_op jit(solution)/shard_map/ppermute | solution.py:24
  81.9 1.5 %collective-permute-start.24 = (bf16[1,256,256]{2,1,0:T(8,128)(2,1)S(1)}, bf16[1,256,256]{2,1,0:T(8,128)(2,1)S(1)}, u32[]{:S(2)}, u32[]{:S(2)}) collective-permute-start(bf16[1,256,256]{2,1,0:T(8,128)(2,1)S(1)} %near_post.1.refs_0_), channel_id=1, source_target_pairs={{0,1},{1,0},{2,3},{3,2},{4,5},{5,4},{6,7},{7,6},{8,9},{9,8},{10,11... | collective-permute-start | bytes 393224 | tf_op jit(solution)/shard_map/ppermute | solution.py:24
  83.4 3.3 %hidden.1 = (bf16[2,2,512,256]{3,2,1,0:T(8,128)(2,1)S(1)}, f32[2,2,512,256]{3,2,1,0:T(8,128)S(1)}, bf16[2,2,512,256]{3,2,1,0:T(8,128)(2,1)S(1)}, f32[2,2,512,256]{3,2,1,0:T(8,128)S(1)}) custom-call(s32[3]{0:T(128)S(1)} %pad_add_fusion.meta.refs_0_, bf16[256,512]{1,0:T(8,128)(2,1)S(1)} %copy-done.3, bf16[2,256,256]{2,1,0:T(8,128)(2,1)S(1)} %bitcast.26, ...), custom_call_target="tpu_custom_call" | custom-call | flops 536870912 | bytes 1310732 | tf_op jit(solution)/shard_map/hidden/pallas_call | solution.py:44
  86.7 2.3 %pre_grads.1 = (f32[512,256]{1,0:T(8,128)S(1)}, f32[512,256]{1,0:T(8,128)S(1)}, f32[256,256]{1,0:T(8,128)S(1)}, f32[8,256]{1,0:T(8,128)S(1)}) custom-call(s32[3]{0:T(128)S(1)} %pad_add_fusion.meta.refs_0_, bf16[512,256]{1,0:T(8,128)(2,1)S(1)} %copy-done.1, bf16[256,256]{1,0:T(8,128)(2,1)S(1)} %copy-done.2, ...), custom_call_target="tpu_custom_call" | custom-call | flops 1073741824 | bytes 6701068 | tf_op jit(solution)/shard_map/pre_grads/pallas_call | solution.py:44
  89.0 2.1 %post_grads.1 = (f32[640,256]{1,0:T(8,128)S(1)}, f32[648,256]{1,0:T(8,128)S(1)}) custom-call(s32[3]{0:T(128)S(1)} %pad_add_fusion.meta.refs_0_, bf16[512,256]{1,0:T(8,128)(2,1)S(1)} %copy-done.1, bf16[2,2,512,256]{3,2,1,0:T(8,128)(2,1)S(1)} %get-tuple-element.59.active_ref, f32[2,2,512,256]{3,2,1,0:T(8,128)S(1)} %get-tuple-element.60.slope_ref, ...), custom_call_target="tpu_custom_call" | custom-call | flops 1073741824 | bytes 5775372 | tf_op jit(solution)/shard_map/post_grads/pallas_call | solution.py:44
  91.2 2.1 %collective-permute-done.26.other_ref = f32[648,256]{1,0:T(8,128)S(1)} collective-permute-done((f32[648,256]{1,0:T(8,128)S(1)}, f32[648,256]{1,0:T(8,128)S(1)}, u32[]{:S(2)}, u32[]{:S(2)}) %collective-permute-start.26) | collective-permute-done | bytes 663584 | tf_op jit(solution)/shard_map/ppermute | solution.py:24
  93.9 14.6 %all_to_all.22 = bf16[8,80,256]{2,1,0:T(8,128)(2,1)S(1)} all-to-all(bf16[8,80,256]{2,1,0:T(8,128)(2,1)S(1)} %bitcast.32), channel_id=1, replica_groups={{0,4,8,12,16,20,24,28},{2,6,10,14,18,22,26,30},{1,5,9,13,17,21,25,29},{..., dimensions={0} | all-to-all | bytes 655360 | tf_op jit(solution)/shard_map/all_to_all | solution.py:548
  109.2 14.8 %all_to_all.23 = s16[8,96,256]{2,1,0:T(8,128)(2,1)S(1)} all-to-all(s16[8,96,256]{2,1,0:T(8,128)(2,1)S(1)} %bitcast.30), channel_id=1, replica_groups={{0,4,8,12,16,20,24,28},{2,6,10,14,18,22,26,30},{1,5,9,13,17,21,25,29},{..., dimensions={0} | all-to-all | bytes 786432 | tf_op jit(solution)/shard_map/all_to_all | solution.py:548
  124.1 1.7 %collective-permute-done.27.other_ref = s16[768,256]{1,0:T(8,128)(2,1)S(1)} collective-permute-done((s16[768,256]{1,0:T(8,128)(2,1)S(1)}, s16[768,256]{1,0:T(8,128)(2,1)S(1)}, u32[]{:S(2)}, u32[]{:S(2)}) %collective-permute-start.27) | collective-permute-done | bytes 393248 | tf_op jit(solution)/shard_map/ppermute | solution.py:24
  125.8 2.0 %last.1 = (f32[256,512]{1,0:T(8,128)}, f32[512,256]{1,0:T(8,128)}, f32[256,256]{1,0:T(8,128)}, f32[8,128]{1,0:T(8,128)S(1)}) custom-call(s32[3]{0:T(128)S(1)} %pad_add_fusion.meta.refs_0_, s16[768,256]{1,0:T(8,128)(2,1)S(1)} %bitcast.29, s16[768,256]{1,0:T(8,128)(2,1)S(1)} %collective-permute-done.27.other_ref), custom_call_target="tpu_custom_call" | custom-call | bytes 786444 | tf_op jit(solution)/shard_map/last/pallas_call | solution.py:44
  (64 shorter events, 9.7 us)
Async XLA Ops:
  0.6 19.4 %copy-start = (s32[16,2,512]{2,1,0:T(2,128)S(1)}, s32[16,2,512]{2,1,0:T(2,128)}, u32[]{:S(2)}) copy-start(s32[16,2,512]{2,1,0:T(2,128)} %param.10) | copy-start | bytes 196612
  0.6 7.4 %copy-start.3 = (bf16[256,512]{1,0:T(8,128)(2,1)S(1)}, bf16[256,512]{1,0:T(8,128)(2,1)}, u32[]{:S(2)}) copy-start(bf16[256,512]{1,0:T(8,128)(2,1)} %refs_0_.1) | copy-start | bytes 786436
  0.7 10.4 %collective-permute-start.2 = (bf16[256,512]{1,0:T(8,128)(2,1)}, bf16[256,512]{1,0:T(8,128)(2,1)S(1)}, u32[]{:S(2)}, u32[]{:S(2)}) collective-permute-start(bf16[256,512]{1,0:T(8,128)(2,1)} %refs_0_.1), channel_id=1, source_target_pairs={{0,1},{1,0},{2,3},{3,2},{4,5},{5,4},{6,7},{7,6},{8,9},{9,8},{10,11... | collective-permute-start | bytes 786440 | tf_op jit(solution)/shard_map/ppermute | solution.py:24
  3.7 13.0 %collective-permute-start.3 = (bf16[512,256]{1,0:T(8,128)(2,1)}, bf16[512,256]{1,0:T(8,128)(2,1)S(1)}, u32[]{:S(2)}, u32[]{:S(2)}) collective-permute-start(bf16[512,256]{1,0:T(8,128)(2,1)} %w_out_ref.5), channel_id=1, source_target_pairs={{0,1},{1,0},{2,3},{3,2},{4,5},{5,4},{6,7},{7,6},{8,9},{9,8},{10,11... | collective-permute-start | bytes 786440 | tf_op jit(solution)/shard_map/ppermute | solution.py:24
  5.9 14.1 %copy-start.4 = (s32[16,2,2]{0,2,1:T(2,128)S(1)}, s32[16,2,2]{0,2,1:T(2,128)}, u32[]{:S(2)}) copy-start(s32[16,2,2]{0,2,1:T(2,128)} %param.11) | copy-start | bytes 772
  5.9 17.8 %collective-permute-start = (bf16[2,256,256]{2,1,0:T(8,128)(2,1)S(1)}, bf16[2,256,256]{2,1,0:T(8,128)(2,1)S(1)}, u32[]{:S(2)}, u32[]{:S(2)}) collective-permute-start(bf16[2,256,256]{2,1,0:T(8,128)(2,1)S(1)} %bitcast.23), channel_id=1, source_target_pairs={{0,1},{1,0},{2,3},{3,2},{4,5},{5,4},{6,7},{7,6},{8,9},{9,8},{10,11... | collective-permute-start | bytes 786440 | tf_op jit(solution)/shard_map/ppermute | solution.py:24
  17.8 10.2 %copy-start.2 = (bf16[256,256]{1,0:T(8,128)(2,1)S(1)}, bf16[256,256]{1,0:T(8,128)(2,1)}, u32[]{:S(2)}) copy-start(bf16[256,256]{1,0:T(8,128)(2,1)} %bil_ref.1) | copy-start | bytes 393220
  17.9 10.2 %collective-permute-start.4 = (bf16[2,256,256]{2,1,0:T(8,128)(2,1)S(1)}, bf16[2,256,256]{2,1,0:T(8,128)(2,1)S(1)}, u32[]{:S(2)}, u32[]{:S(2)}) collective-permute-start(bf16[2,256,256]{2,1,0:T(8,128)(2,1)S(1)} %get-tuple-element.65.refs_6_), channel_id=1, source_target_pairs={{0,2},{2,0},{4,6},{6,4},{8,10},{10,8},{12,14},{14,12},{16,18},{18,... | collective-permute-start | bytes 786440 | tf_op jit(solution)/shard_map/ppermute | solution.py:24
  17.9 19.3 %collective-permute-start.1 = (bf16[2,256,256]{2,1,0:T(8,128)(2,1)S(1)}, bf16[2,256,256]{2,1,0:T(8,128)(2,1)S(1)}, u32[]{:S(2)}, u32[]{:S(2)}) collective-permute-start(bf16[2,256,256]{2,1,0:T(8,128)(2,1)S(1)} %bitcast.20), channel_id=1, source_target_pairs={{0,1},{1,0},{2,3},{3,2},{4,5},{5,4},{6,7},{7,6},{8,9},{9,8},{10,11... | collective-permute-start | bytes 786440 | tf_op jit(solution)/shard_map/ppermute | solution.py:24
  20.3 17.8 %collective-permute-start.6 = (bf16[2,256,256]{2,1,0:T(8,128)(2,1)S(1)}, bf16[2,256,256]{2,1,0:T(8,128)(2,1)S(1)}, u32[]{:S(2)}, u32[]{:S(2)}) collective-permute-start(bf16[2,256,256]{2,1,0:T(8,128)(2,1)S(1)} %get-tuple-element.65.refs_6_), channel_id=1, source_target_pairs={{0,4},{2,6},{4,0},{6,2},{8,12},{10,14},{12,8},{14,10},{16,20},{18,... | collective-permute-start | bytes 786440 | tf_op jit(solution)/shard_map/ppermute | solution.py:24
  21.9 16.3 %collective-permute-start.5 = (bf16[2,256,256]{2,1,0:T(8,128)(2,1)S(1)}, bf16[2,256,256]{2,1,0:T(8,128)(2,1)S(1)}, u32[]{:S(2)}, u32[]{:S(2)}) collective-permute-start(bf16[2,256,256]{2,1,0:T(8,128)(2,1)S(1)} %get-tuple-element.65.refs_6_), channel_id=1, source_target_pairs={{4,8},{6,10},{8,4},{10,6},{20,24},{22,26},{24,20},{26,22},{5,9},{7... | collective-permute-start | bytes 786440 | tf_op jit(solution)/shard_map/ppermute | solution.py:24
  23.7 19.8 %collective-permute-start.11 = (bf16[1,256,256]{2,1,0:T(8,128)(2,1)S(1)}, bf16[1,256,256]{2,1,0:T(8,128)(2,1)S(1)}, u32[]{:S(2)}, u32[]{:S(2)}) collective-permute-start(bf16[1,256,256]{2,1,0:T(8,128)(2,1)S(1)} %get-tuple-element.83), channel_id=1, source_target_pairs={{0,16},{2,18},{4,20},{6,22},{8,24},{10,26},{12,28},{14,30},{16,0},... | collective-permute-start | bytes 393224 | tf_op jit(solution)/shard_map/ppermute | solution.py:24
  33.2 10.5 %collective-permute-start.13 = (bf16[1,256,256]{2,1,0:T(8,128)(2,1)S(1)}, bf16[1,256,256]{2,1,0:T(8,128)(2,1)S(1)}, u32[]{:S(2)}, u32[]{:S(2)}) collective-permute-start(bf16[1,256,256]{2,1,0:T(8,128)(2,1)S(1)} %get-tuple-element.83), channel_id=1, source_target_pairs={{0,20},{2,22},{4,16},{6,18},{8,28},{10,30},{12,24},{14,26},{16,4},... | collective-permute-start | bytes 393224 | tf_op jit(solution)/shard_map/ppermute | solution.py:24
  37.3 6.4 %collective-permute-start.9 = (bf16[1,256,256]{2,1,0:T(8,128)(2,1)S(1)}, bf16[1,256,256]{2,1,0:T(8,128)(2,1)S(1)}, u32[]{:S(2)}, u32[]{:S(2)}) collective-permute-start(bf16[1,256,256]{2,1,0:T(8,128)(2,1)S(1)} %get-tuple-element.83), channel_id=1, source_target_pairs={{4,24},{6,26},{8,20},{10,22},{20,8},{22,10},{24,4},{26,6},{5,25},{... | collective-permute-start | bytes 393224 | tf_op jit(solution)/shard_map/ppermute | solution.py:24
  38.1 6.0 %collective-permute-start.7 = (bf16[2,256,256]{2,1,0:T(8,128)(2,1)S(1)}, bf16[2,256,256]{2,1,0:T(8,128)(2,1)S(1)}, u32[]{:S(2)}, u32[]{:S(2)}) collective-permute-start(bf16[2,256,256]{2,1,0:T(8,128)(2,1)S(1)} %collective-permute-done.5.refs_9_), channel_id=1, source_target_pairs={{0,2},{2,0},{4,6},{6,4},{8,10},{10,8},{12,14},{14,12},{16,18},{18,... | collective-permute-start | bytes 786440 | tf_op jit(solution)/shard_map/ppermute | solution.py:24
  38.2 6.0 %collective-permute-start.8 = (bf16[2,256,256]{2,1,0:T(8,128)(2,1)S(1)}, bf16[2,256,256]{2,1,0:T(8,128)(2,1)S(1)}, u32[]{:S(2)}, u32[]{:S(2)}) collective-permute-start(bf16[2,256,256]{2,1,0:T(8,128)(2,1)S(1)} %collective-permute-done.6.refs_10_), channel_id=1, source_target_pairs={{0,2},{2,0},{4,6},{6,4},{8,10},{10,8},{12,14},{14,12},{16,18},{18,... | collective-permute-start | bytes 786440 | tf_op jit(solution)/shard_map/ppermute | solution.py:24
  43.5 5.9 %collective-permute-start.12 = (bf16[1,256,256]{2,1,0:T(8,128)(2,1)S(1)}, bf16[1,256,256]{2,1,0:T(8,128)(2,1)S(1)}, u32[]{:S(2)}, u32[]{:S(2)}) collective-permute-start(bf16[1,256,256]{2,1,0:T(8,128)(2,1)S(1)} %collective-permute-done.11.refs_11_), channel_id=1, source_target_pairs={{0,2},{2,0},{4,6},{6,4},{8,10},{10,8},{12,14},{14,12},{16,18},{18,... | collective-permute-start | bytes 393224 | tf_op jit(solution)/shard_map/ppermute | solution.py:24
  43.6 5.8 %collective-permute-start.10 = (bf16[1,256,256]{2,1,0:T(8,128)(2,1)S(1)}, bf16[1,256,256]{2,1,0:T(8,128)(2,1)S(1)}, u32[]{:S(2)}, u32[]{:S(2)}) collective-permute-start(bf16[1,256,256]{2,1,0:T(8,128)(2,1)S(1)} %collective-permute-done.9.refs_9_), channel_id=1, source_target_pairs={{0,2},{2,0},{4,6},{6,4},{8,10},{10,8},{12,14},{14,12},{16,18},{18,... | collective-permute-start | bytes 393224 | tf_op jit(solution)/shard_map/ppermute | solution.py:24
  44.1 5.3 %collective-permute-start.14 = (bf16[1,256,256]{2,1,0:T(8,128)(2,1)S(1)}, bf16[1,256,256]{2,1,0:T(8,128)(2,1)S(1)}, u32[]{:S(2)}, u32[]{:S(2)}) collective-permute-start(bf16[1,256,256]{2,1,0:T(8,128)(2,1)S(1)} %collective-permute-done.13.refs_13_), channel_id=1, source_target_pairs={{0,2},{2,0},{4,6},{6,4},{8,10},{10,8},{12,14},{14,12},{16,18},{18,... | collective-permute-start | bytes 393224 | tf_op jit(solution)/shard_map/ppermute | solution.py:24
  48.9 5.5 %collective-permute-start.17 = (f32[4,256,256]{2,1,0:T(8,128)S(1)}, f32[4,256,256]{2,1,0:T(8,128)S(1)}, u32[]{:S(2)}, u32[]{:S(2)}) collective-permute-start(f32[4,256,256]{2,1,0:T(8,128)S(1)} %get-tuple-element.95), channel_id=1, source_target_pairs={{0,2},{2,0},{4,6},{6,4},{8,10},{10,8},{12,14},{14,12},{16,18},{18,... | collective-permute-start | bytes 3145736 | tf_op jit(solution)/shard_map/ppermute | solution.py:24
  53.3 33.4 %collective-permute-start.15 = (f32[1032,256]{1,0:T(8,128)S(1)}, f32[1032,256]{1,0:T(8,128)S(1)}, u32[]{:S(2)}, u32[]{:S(2)}) collective-permute-start(f32[1032,256]{1,0:T(8,128)S(1)} %get-tuple-element.87.refs_0_), channel_id=1, source_target_pairs={{0,1},{1,0},{2,3},{3,2},{4,5},{5,4},{6,7},{7,6},{8,9},{9,8},{10,11... | collective-permute-start | bytes 3170312 | tf_op jit(solution)/shard_map/ppermute | solution.py:24
  53.9 6.5 %collective-permute-start.20 = (f32[3,256,256]{2,1,0:T(8,128)S(1)}, f32[3,256,256]{2,1,0:T(8,128)S(1)}, u32[]{:S(2)}, u32[]{:S(2)}) collective-permute-start(f32[3,256,256]{2,1,0:T(8,128)S(1)} %get-tuple-element.100), channel_id=1, source_target_pairs={{0,2},{2,0},{4,6},{6,4},{8,10},{10,8},{12,14},{14,12},{16,18},{18,... | collective-permute-start | bytes 2359304 | tf_op jit(solution)/shard_map/ppermute | solution.py:24
  53.9 16.8 %collective-permute-start.16 = (f32[2,256,256]{2,1,0:T(8,128)S(1)}, f32[2,256,256]{2,1,0:T(8,128)S(1)}, u32[]{:S(2)}, u32[]{:S(2)}) collective-permute-start(f32[2,256,256]{2,1,0:T(8,128)S(1)} %get-tuple-element.93), channel_id=1, source_target_pairs={{0,2},{2,0},{4,6},{6,4},{8,10},{10,8},{12,14},{14,12},{16,18},{18,... | collective-permute-start | bytes 1572872 | tf_op jit(solution)/shard_map/ppermute | solution.py:24
  54.5 6.6 %collective-permute-start.18 = (bf16[2,256,256]{2,1,0:T(8,128)(2,1)S(1)}, bf16[2,256,256]{2,1,0:T(8,128)(2,1)S(1)}, u32[]{:S(2)}, u32[]{:S(2)}) collective-permute-start(bf16[2,256,256]{2,1,0:T(8,128)(2,1)S(1)} %get-tuple-element.96), channel_id=1, source_target_pairs={{4,8},{6,10},{8,4},{10,6},{20,24},{22,26},{24,20},{26,22},{5,9},{7... | collective-permute-start | bytes 786440 | tf_op jit(solution)/shard_map/ppermute | solution.py:24
  55.2 20.8 %collective-permute-start.19 = (bf16[2,256,256]{2,1,0:T(8,128)(2,1)S(1)}, bf16[2,256,256]{2,1,0:T(8,128)(2,1)S(1)}, u32[]{:S(2)}, u32[]{:S(2)}) collective-permute-start(bf16[2,256,256]{2,1,0:T(8,128)(2,1)S(1)} %get-tuple-element.97), channel_id=1, source_target_pairs={{0,4},{2,6},{4,0},{6,2},{8,12},{10,14},{12,8},{14,10},{16,20},{18,... | collective-permute-start | bytes 786440 | tf_op jit(solution)/shard_map/ppermute | solution.py:24
  60.4 17.2 %collective-permute-start.21 = (bf16[1,256,256]{2,1,0:T(8,128)(2,1)S(1)}, bf16[1,256,256]{2,1,0:T(8,128)(2,1)S(1)}, u32[]{:S(2)}, u32[]{:S(2)}) collective-permute-start(bf16[1,256,256]{2,1,0:T(8,128)(2,1)S(1)} %get-tuple-element.101), channel_id=1, source_target_pairs={{4,24},{6,26},{8,20},{10,22},{20,8},{22,10},{24,4},{26,6},{5,25},{... | collective-permute-start | bytes 393224 | tf_op jit(solution)/shard_map/ppermute | solution.py:24
  61.1 19.1 %collective-permute-start.22 = (bf16[1,256,256]{2,1,0:T(8,128)(2,1)S(1)}, bf16[1,256,256]{2,1,0:T(8,128)(2,1)S(1)}, u32[]{:S(2)}, u32[]{:S(2)}) collective-permute-start(bf16[1,256,256]{2,1,0:T(8,128)(2,1)S(1)} %get-tuple-element.102), channel_id=1, source_target_pairs={{0,20},{2,22},{4,16},{6,18},{8,28},{10,30},{12,24},{14,26},{16,4},... | collective-permute-start | bytes 393224 | tf_op jit(solution)/shard_map/ppermute | solution.py:24
  70.7 11.1 %collective-permute-start.23 = (bf16[1,256,256]{2,1,0:T(8,128)(2,1)S(1)}, bf16[1,256,256]{2,1,0:T(8,128)(2,1)S(1)}, u32[]{:S(2)}, u32[]{:S(2)}) collective-permute-start(bf16[1,256,256]{2,1,0:T(8,128)(2,1)S(1)} %get-tuple-element.104), channel_id=1, source_target_pairs={{0,16},{2,18},{4,20},{6,22},{8,24},{10,26},{12,28},{14,30},{16,0},... | collective-permute-start | bytes 393224 | tf_op jit(solution)/shard_map/ppermute | solution.py:24
  76.1 12.9 %collective-permute-start.25 = (bf16[1,256,256]{2,1,0:T(8,128)(2,1)S(1)}, bf16[1,256,256]{2,1,0:T(8,128)(2,1)S(1)}, u32[]{:S(2)}, u32[]{:S(2)}) collective-permute-start(bf16[1,256,256]{2,1,0:T(8,128)(2,1)S(1)} %convert_element_type.3.refs_2_), channel_id=1, source_target_pairs={{0,1},{1,0},{2,3},{3,2},{4,5},{5,4},{6,7},{7,6},{8,9},{9,8},{10,11... | collective-permute-start | bytes 393224 | tf_op jit(solution)/shard_map/ppermute | solution.py:24
  81.9 7.2 %collective-permute-start.24 = (bf16[1,256,256]{2,1,0:T(8,128)(2,1)S(1)}, bf16[1,256,256]{2,1,0:T(8,128)(2,1)S(1)}, u32[]{:S(2)}, u32[]{:S(2)}) collective-permute-start(bf16[1,256,256]{2,1,0:T(8,128)(2,1)S(1)} %near_post.1.refs_0_), channel_id=1, source_target_pairs={{0,1},{1,0},{2,3},{3,2},{4,5},{5,4},{6,7},{7,6},{8,9},{9,8},{10,11... | collective-permute-start | bytes 393224 | tf_op jit(solution)/shard_map/ppermute | solution.py:24
  91.1 2.2 %collective-permute-start.26 = (f32[648,256]{1,0:T(8,128)S(1)}, f32[648,256]{1,0:T(8,128)S(1)}, u32[]{:S(2)}, u32[]{:S(2)}) collective-permute-start(f32[648,256]{1,0:T(8,128)S(1)} %get-tuple-element.107), channel_id=1, source_target_pairs={{0,2},{2,0},{4,6},{6,4},{8,10},{10,8},{12,14},{14,12},{16,18},{18,... | collective-permute-start | bytes 1990664 | tf_op jit(solution)/shard_map/ppermute | solution.py:24
  124.1 1.7 %collective-permute-start.27 = (s16[768,256]{1,0:T(8,128)(2,1)S(1)}, s16[768,256]{1,0:T(8,128)(2,1)S(1)}, u32[]{:S(2)}, u32[]{:S(2)}) collective-permute-start(s16[768,256]{1,0:T(8,128)(2,1)S(1)} %bitcast.28), channel_id=1, source_target_pairs={{0,2},{2,0},{4,6},{6,4},{8,10},{10,8},{12,14},{14,12},{16,18},{18,... | collective-permute-start | bytes 1179656 | tf_op jit(solution)/shard_map/ppermute | solution.py:24
  (1 other events, 7.4 us)

commit v3 on v2

--- a/solution.py
+++ b/solution.py
@@ -54,9 +54,9 @@
     )(*operands)
 
 
-def summed(arrays, places, kind, name):
+def summed(arrays, places, name):
     def kernel(*refs):
-        for (first, count), out in zip(places, refs[len(arrays) :], strict=True):
+        for (first, count, kind), out in zip(places, refs[len(arrays) :], strict=True):
             for t in range(count):
                 total = None
                 for ref in refs[: len(arrays)]:
@@ -66,7 +66,7 @@
                 out[t] = total.astype(kind)
 
     shape = arrays[0].shape[1:]
-    return call(kernel, name, [((count, *shape), kind) for unused, count in places], arrays)
+    return call(kernel, name, [((count, *shape), kind) for unused, count, kind in places], arrays)
 
 
 def sub_tile(xb, t):
@@ -158,15 +158,15 @@
 
 
 def post_kernel(groups, meta, w_out_ref, active_ref, slope_ref, in0, out0, bil0, loss0, *refs):
-    near_refs, far_refs, x_refs = refs[:groups], refs[groups : 2 * groups], refs[2 * groups : 3 * groups]
-    mine_ref, other_ref, whole = refs[3 * groups :]
+    back_refs, x_refs = refs[:groups], refs[groups : 2 * groups]
+    mine_ref, other_ref, whole = refs[2 * groups :]
     xb = meta[2]
     core = lax.rem(meta[0], 2)
     sums = (in0[...], out0[...])
     for t in range(2):
         u = sub_tile(xb, t)
         for g in range(groups):
-            back = (near_refs, far_refs)[t][g][0]
+            back = back_refs[g][t]
             sums = weight_part(back, x_refs[g][u], active_ref[g, u], slope_ref[g, u], w_out_ref[...], sums)
     hid = in0.shape[0]
     half = mine_ref.shape[0]
@@ -270,13 +270,15 @@
     toward = 1 - 2 * xb
     rows = post_refs[0].shape[1]
     width = post_refs[0].shape[2]
+    pre_counts = [counts[tile_here * 4 + sub_tile(xb, a) * 2] for a in (0, 1)]
     if first:
         scale = jnp.asarray(width ** (-0.5), bf16)
         for a in range(2):
             for g in range(groups):
-                part = dot(pre_refs[g][a], bil_ref[...]).astype(bf16)
-                place = pl.ds(pl.multiple_of(owner(meta, g, groups) * rows, rows), rows)
-                q_ref[a, place, :] = part
+                first_row = owner(meta, g, groups) * rows
+                site = first_row + lax.broadcasted_iota(jnp.int32, (rows, width), 0)
+                part = jnp.where(site < pre_counts[a], dot(pre_refs[g][a], bil_ref[...]), 0.0).astype(bf16)
+                q_ref[a, pl.ds(pl.multiple_of(first_row, rows), rows), :] = part
             qt_ref[a] = (q_ref[a] * scale).T
         acc[...] = jnp.zeros_like(acc)
         loss_ref[...] = jnp.zeros_like(loss_ref)
@@ -291,8 +293,7 @@
     j_col = lax.broadcasted_iota(jnp.int32, (rows, 128), 0)
     i_row = lax.broadcasted_iota(jnp.int32, (1, site_rows), 1)
     step = rows // (8 if rows >= 128 else 4)
-    i_ok = [i_row < counts[tile_here * 4 + sub_tile(xb, a) * 2] for a in (0, 1)]
-    i_bias = [jnp.where(ok, 0.0, OFF).astype(f32) for ok in i_ok]
+    i_ok = [i_row < count for count in pre_counts]
     if foreign:
         nz = sum(1 for dy, unused in slots if dy == 0)
         chunks = [[(n, 0) for n in range(k, k + nz)] for k in range(0, len(slots), nz)]
@@ -328,7 +329,7 @@
                 found_ref[a] += jnp.where(key >= 0, 1.0, 0.0)
                 targets.append(j_own == key)
             target = jnp.concatenate(targets, 0)
-            s = dot(post, qt_ref[a]) + j_bias + i_bias[a]
+            s = dot(post, qt_ref[a]) + j_bias
             e = jnp.exp(-jnp.abs(s))
             w = 1.0 + e
             r = pl.reciprocal(w, approx=True)
@@ -350,7 +351,7 @@
                     hit = found if hit is None else hit + found
                 loss = above + jnp.where(small < 1e-3, small, jnp.log(product))
                 piece = loss if piece is None else piece + loss
-            loss_ref[...] += jnp.sum(piece.reshape(step // 8, 8, site_rows), 0)
+            loss_ref[...] += jnp.where(i_ok[a], jnp.sum(piece.reshape(step // 8, 8, site_rows), 0), 0.0)
             hit_ref[a] += jnp.sum(hit.reshape(step // 8, 8, site_rows), 0)
         for k, (n, t) in enumerate(chunk):
             dy, z_slot = slots[n]
@@ -359,7 +360,8 @@
     if last:
         total = jnp.sum(loss_ref[...])
         for a in range(2):
-            out_ref[a * site_rows : (a + 1) * site_rows] = (acc[a] * out_scale).T
+            ok = lax.broadcasted_iota(jnp.int32, (site_rows, width), 0) < pre_counts[a]
+            out_ref[a * site_rows : (a + 1) * site_rows] = jnp.where(ok, (acc[a] * out_scale).T, 0.0)
             score = jnp.sum(hit_ref[a], 0, keepdims=True)
             soft = jnp.log1p(jnp.exp(-jnp.abs(score)))
             missed = heavy * (jnp.maximum(-score, 0.0) + soft) - (jnp.maximum(score, 0.0) + soft)
@@ -505,12 +507,14 @@
         return [moved(g, "tile", back_z(slot)) for slot, g in zip(z_slots[1:], grads, strict=True)]
 
     own_parts = grads_own[:1] + back_from_z(grads_own[1:])
-    near_sums = summed(grads_near + back_from_z(grads_near_z), [(0, 2), (2, 2)], bf16, "near_sums")
+    near_sums = summed(grads_near + back_from_z(grads_near_z), [(0, 2, bf16), (2, 2, bf16)], "near_sums")
     near_back = [moved(total, "tile", along_y(dy)) for total, dy in zip(near_sums, (-1, 1), strict=True)]
     query_parts = over_mlp(query_part)
-    far_sums = summed(grads_far[:1] + back_from_z(grads_far[1:]), [(0, 1), (1, 1), (2, 1)], bf16, "far_sums")
-    far_back = [moved(far_sums[0], "tile", both(-1)), moved(far_sums[2], "tile", both(1))]
-    far_back.append(moved(after(far_sums[1], near_back[0]), "tile", side))
+    side_b, side_0, side_a = summed(
+        grads_far[:1] + back_from_z(grads_far[1:]), [(0, 1, bf16), (1, 1, f32), (2, 1, bf16)], "far_sums"
+    )
+    side_parts = [side_0, moved(side_a, "tile", along_y(1)), moved(side_b, "tile", along_y(-1))]
+    side_back = moved(summed(side_parts, [(0, 1, bf16)], "side_sum")[0], "tile", side)
     part_t = (groups, 2, hid, row_part)
     active_0, slope_0, active_1, slope_1 = call(
         functools.partial(hidden_kernel, groups),
@@ -527,15 +531,13 @@
         flops * groups,
         [pltpu.VMEM((2, site_rows, width), bf16)] * 2,
     )
-    near_post, far_post = summed(own_parts + near_back, [(0, 1), (1, 1)], f32, "post_sums")
-    far_post = over_mlp(far_post.astype(bf16))
-    near_post = over_mlp(summed([near_post] + far_back, [(0, 1)], bf16, "near_post")[0])
+    post_back = over_mlp(summed(own_parts + near_back + [side_back], [(0, 2, bf16)], "post_sum")[0])
     half_rows = (2 * hid + width) // 2
     mine, other = call(
         functools.partial(post_kernel, groups),
         "post_grads",
         [((half_rows, width), f32), ((half_rows + 8, width), f32)],
-        [meta, w_out, active_1, slope_1, in_0, out_0, bil_0, loss, *near_post, *far_post, *x1s],
+        [meta, w_out, active_1, slope_1, in_0, out_0, bil_0, loss, *post_back, *x1s],
         flops * groups,
         [pltpu.VMEM((2 * half_rows, width), f32)],
     )

time: 129 us -> 126 us (0.977)
  starting transfers between devices: 40.4 us -> 29.4 us
  waiting for transfers between devices: 19.2 us -> 26.3 us
  blocking collectives: 29.4 us -> 31.4 us
    ppermute x28 -> x27, starting transfers between devices: 40.4 us -> 29.4 us  [moved(): return lax.ppermute(array, axis, pairs)]
    ppermute x28 -> x27, waiting for transfers between devices: 19.2 us -> 26.3 us  [moved(): return lax.ppermute(array, axis, pairs)]
    all_to_all x2, blocking collectives: 29.4 us -> 31.4 us  [to_chips(): lax.all_to_all(array, 'tile', 0, 0, tiled=True, axis_index_groups=same_core)]
  transfers between devices with their start and end apart: 28 -> 27, of which waited for: 7 -> 10; matrix products, arithmetic and copies ran while one was open for 2% -> 2% of each run, Pallas kernels for 23% -> 23%
where the time goes in v3:
time: 126 us
  Pallas kernels  35 us (28%)
  blocking collectives  31.4 us (25%)
  starting transfers between devices  29.4 us (23%)
  waiting for transfers between devices  26.3 us (21%)
  local copies, waits for them, and re-layouts  2.94 us (2%)
    pallas_call x18, Pallas kernels, call(): pl.pallas_call(kernel, out_shape=[jax.ShapeDtypeStruct(shape, kind) for s...  35 us
    all_to_all x2, blocking collectives, to_chips(): lax.all_to_all(array, 'tile', 0, 0, tiled=True, axis_index_groups=same_core)  31.4 us
    ppermute x27, starting transfers between devices, moved(): return lax.ppermute(array, axis, pairs)  29.4 us
    ppermute x27, waiting for transfers between devices, moved(): return lax.ppermute(array, axis, pairs)  26.3 us
  transfers between devices with their start and end apart: 27, of which 10 were waited for; matrix products, arithmetic and copies ran while one was open for 2% of the time, Pallas kernels for 23%

profile of v3, /device:TPU:0, one launch (start us, length us, event | category | flops | bytes accessed | tf_op | source)
XLA Modules:
  0.0 126.1 jit_solution(11223688875574170591)
XLA Ops:
  0.7 3.0 %collective-permute-start.2 = (bf16[256,512]{1,0:T(8,128)(2,1)}, bf16[256,512]{1,0:T(8,128)(2,1)S(1)}, u32[]{:S(2)}, u32[]{:S(2)}) collective-permute-start(bf16[256,512]{1,0:T(8,128)(2,1)} %refs_0_.1), channel_id=1, source_target_pairs={{0,1},{1,0},{2,3},{3,2},{4,5},{5,4},{6,7},{7,6},{8,9},{9,8},{10,11... | collective-permute-start | bytes 786440 | tf_op jit(solution)/shard_map/ppermute | solution.py:24
  3.8 2.1 %fusion = (bf16[1,256,2,1,256]{4,3,2,1,0:T(2,128)(2,1)S(1)}, bf16[1,256,2,1,256]{4,3,2,1,0:T(2,128)(2,1)S(1)}) fusion(bf16[1,256,2,2,256]{4,3,2,1,0:T(2,128)(2,1)} %param.6), kind=kLoop, calls=%fused_computation.4 | loop fusion | bytes 1048576 | tf_op jit(solution)/shard_map/slice | solution.py:452
  5.9 2.0 %collective-permute-start = (bf16[2,256,256]{2,1,0:T(8,128)(2,1)S(1)}, bf16[2,256,256]{2,1,0:T(8,128)(2,1)S(1)}, u32[]{:S(2)}, u32[]{:S(2)}) collective-permute-start(bf16[2,256,256]{2,1,0:T(8,128)(2,1)S(1)} %bitcast.23), channel_id=1, source_target_pairs={{0,1},{1,0},{2,3},{3,2},{4,5},{5,4},{6,7},{7,6},{8,9},{9,8},{10,11... | collective-permute-start | bytes 786440 | tf_op jit(solution)/shard_map/ppermute | solution.py:24
  8.1 1.5 %mlp_own.1 = (f32[2,256,256]{2,1,0:T(8,128)S(1)}, f32[2,256,256]{2,1,0:T(8,128)S(1)}) custom-call(s32[3]{0:T(128)S(1)} %pad_add_fusion.meta.refs_0_, bf16[2,256,256]{2,1,0:T(8,128)(2,1)S(1)} %bitcast.24, bf16[2,256,256]{2,1,0:T(8,128)(2,1)S(1)} %bitcast.18, bf16[256,512]{1,0:T(8,128)(2,1)S(1)} %copy-done.3, bf16[512,256]{1,0:T(8,128)(2,1)S(1)} %copy-done.1), custom_call_target="tpu_custom_call" | custom-call | flops 536870912 | bytes 1048588 | tf_op jit(solution)/shard_map/mlp_own/pallas_call | solution.py:44
  9.6 1.5 %collective-permute-done.2.refs_1_.refs_2_ = bf16[256,512]{1,0:T(8,128)(2,1)S(1)} collective-permute-done((bf16[256,512]{1,0:T(8,128)(2,1)}, bf16[256,512]{1,0:T(8,128)(2,1)S(1)}, u32[]{:S(2)}, u32[]{:S(2)}) %collective-permute-start.2) | collective-permute-done | bytes 262176 | tf_op jit(solution)/shard_map/ppermute | solution.py:24
  11.0 5.6 %collective-permute-done.3.refs_2_.refs_3_ = bf16[512,256]{1,0:T(8,128)(2,1)S(1)} collective-permute-done((bf16[512,256]{1,0:T(8,128)(2,1)}, bf16[512,256]{1,0:T(8,128)(2,1)S(1)}, u32[]{:S(2)}, u32[]{:S(2)}) %collective-permute-start.3) | collective-permute-done | bytes 262176 | tf_op jit(solution)/shard_map/ppermute | solution.py:24
  16.7 1.2 mlp_post.1
  17.9 2.1 %collective-permute-start.1 = (bf16[2,256,256]{2,1,0:T(8,128)(2,1)S(1)}, bf16[2,256,256]{2,1,0:T(8,128)(2,1)S(1)}, u32[]{:S(2)}, u32[]{:S(2)}) collective-permute-start(bf16[2,256,256]{2,1,0:T(8,128)(2,1)S(1)} %bitcast.20), channel_id=1, source_target_pairs={{0,1},{1,0},{2,3},{3,2},{4,5},{5,4},{6,7},{7,6},{8,9},{9,8},{10,11... | collective-permute-start | bytes 786440 | tf_op jit(solution)/shard_map/ppermute | solution.py:24
  20.3 1.6 %collective-permute-start.6 = (bf16[2,256,256]{2,1,0:T(8,128)(2,1)S(1)}, bf16[2,256,256]{2,1,0:T(8,128)(2,1)S(1)}, u32[]{:S(2)}, u32[]{:S(2)}) collective-permute-start(bf16[2,256,256]{2,1,0:T(8,128)(2,1)S(1)} %get-tuple-element.62.refs_6_), channel_id=1, source_target_pairs={{0,4},{2,6},{4,0},{6,2},{8,12},{10,14},{12,8},{14,10},{16,20},{18,... | collective-permute-start | bytes 786440 | tf_op jit(solution)/shard_map/ppermute | solution.py:24
  23.7 2.7 %collective-permute-start.11 = (bf16[1,256,256]{2,1,0:T(8,128)(2,1)S(1)}, bf16[1,256,256]{2,1,0:T(8,128)(2,1)S(1)}, u32[]{:S(2)}, u32[]{:S(2)}) collective-permute-start(bf16[1,256,256]{2,1,0:T(8,128)(2,1)S(1)} %get-tuple-element.80), channel_id=1, source_target_pairs={{0,16},{2,18},{4,20},{6,22},{8,24},{10,26},{12,28},{14,30},{16,0},... | collective-permute-start | bytes 393224 | tf_op jit(solution)/shard_map/ppermute | solution.py:24
  26.4 1.6 %mlp_pre_other.1.refs_5_.refs_3_ = bf16[2,256,256]{2,1,0:T(8,128)(2,1)S(1)} custom-call(s32[3]{0:T(128)S(1)} %pad_add_fusion.meta.refs_0_, bf16[2,256,256]{2,1,0:T(8,128)(2,1)S(1)} %collective-permute-done.refs_1_.x_ref.refs_5_, bf16[256,512]{1,0:T(8,128)(2,1)S(1)} %copy-done.3, bf16[512,256]{1,0:T(8,128)(2,1)S(1)} %copy-done.1, ...), custom_call_target="tpu_custom_call" | custom-call | flops 536870912 | bytes 1310732 | tf_op jit(solution)/shard_map/mlp_pre_other/pallas_call | solution.py:44
  28.0 5.0 %pairs_own.1 = (f32[2,256,256]{2,1,0:T(8,128)S(1)}, f32[2,256,256]{2,1,0:T(8,128)S(1)}, bf16[2,512,256]{2,1,0:T(8,128)(2,1)S(1)}, bf16[2,256,512]{2,1,0:T(8,128)...) custom-call(s32[3]{0:T(128)S(1)} %pad_add_fusion.meta.refs_0_, ...), custom_call_target="tpu_custom_call" | custom-call | flops 10737418240 | bytes 1184012 | tf_op jit(solution)/shard_map/pairs_own/pallas_call | solution.py:44
  33.1 4.1 %collective-permute-start.13 = (bf16[1,256,256]{2,1,0:T(8,128)(2,1)S(1)}, bf16[1,256,256]{2,1,0:T(8,128)(2,1)S(1)}, u32[]{:S(2)}, u32[]{:S(2)}) collective-permute-start(bf16[1,256,256]{2,1,0:T(8,128)(2,1)S(1)} %get-tuple-element.80), channel_id=1, source_target_pairs={{0,20},{2,22},{4,16},{6,18},{8,28},{10,30},{12,24},{14,26},{16,4},... | collective-permute-start | bytes 393224 | tf_op jit(solution)/shard_map/ppermute | solution.py:24
  38.6 4.6 %pairs_near.1 = (f32[4,256,256]{2,1,0:T(8,128)S(1)}, f32[2,256,512]{2,1,0:T(8,128)S(1)}, f32[8,512]{1,0:T(8,128)S(1)}, f32[2,8,512]{2,1,0:T(8,128)S(1)}, f32[2,1,512]{2,1,0:T(1,128)S(1)}) custom-call(s32[3]{0:T(128)S(1)} %pad_add_fusion.meta.refs_0_, ...), custom_call_target="tpu_custom_call", output_to_operand_aliasing={{1}: (5, {}), {2}: (6, {}), {3}: (7, {}), {4}: (8, {})} | custom-call | flops 10737418240 | bytes 2679052 | tf_op jit(solution)/shard_map/pairs_near/pallas_call | solution.py:44
  44.0 4.6 %pairs_near_z.1 = (f32[4,256,256]{2,1,0:T(8,128)S(1)}, f32[2,256,512]{2,1,0:T(8,128)S(1)}, f32[8,512]{1,0:T(8,128)S(1)}, f32[2,8,512]{2,1,0:T(8,128)S(1)}, f32[2,1,512]{2,1,0:T(1,128)S(1)}) custom-call(s32[3]{0:T(128)S(1)} %pad_add_fusion.meta.refs_0_, ...), custom_call_target="tpu_custom_call", output_to_operand_aliasing={{1}: (5, {}), {2}: (6, {}), {3}: (7, {}), {4}: (8, {})} | custom-call | flops 10737418240 | bytes 2679052 | tf_op jit(solution)/shard_map/pairs_near_z/pallas_call | solution.py:44
  49.1 3.9 %pairs_far.1 = (f32[3,256,256]{2,1,0:T(8,128)S(1)}, f32[3,256,256]{2,1,0:T(8,128)S(1)}, f32[1032,256]{1,0:T(8,128)S(1)}) custom-call(s32[3]{0:T(128)S(1)} %pad_add_fusion.meta.refs_0_, s32[64]{0:T(128)S(1)} %reshape.16.refs_1_, s32[2,1,512]{2,1,0:T(1,128)S(1)} %broadcast_in_dim.3.refs_2_, bf16[2,512,256]{2,1,0:T(8,128)(2,1)S(1)} %get-tuple-element.63.refs_3_, ...), custom_call_target="tpu_custom_call" | custom-call | flops 8053063680 | bytes 2941196 | tf_op jit(solution)/shard_map/pairs_far/pallas_call | solution.py:44
  53.8 1.5 %collective-permute-done.20.refs_1_ = f32[3,256,256]{2,1,0:T(8,128)S(1)} collective-permute-done((f32[3,256,256]{2,1,0:T(8,128)S(1)}, f32[3,256,256]{2,1,0:T(8,128)S(1)}, u32[]{:S(2)}, u32[]{:S(2)}) %collective-permute-start.20) | collective-permute-done | bytes 786464 | tf_op jit(solution)/shard_map/ppermute | solution.py:24
  55.4 3.7 %collective-permute-start.21 = (bf16[1,256,256]{2,1,0:T(8,128)(2,1)S(1)}, bf16[1,256,256]{2,1,0:T(8,128)(2,1)S(1)}, u32[]{:S(2)}, u32[]{:S(2)}) collective-permute-start(bf16[1,256,256]{2,1,0:T(8,128)(2,1)S(1)} %get-tuple-element.98), channel_id=1, source_target_pairs={{0,4},{2,6},{4,0},{6,2},{8,12},{10,14},{12,8},{14,10},{16,20},{18,... | collective-permute-start | bytes 393224 | tf_op jit(solution)/shard_map/ppermute | solution.py:24
  60.6 2.6 %collective-permute-done.21.refs_1_ = bf16[1,256,256]{2,1,0:T(8,128)(2,1)S(1)} collective-permute-done((bf16[1,256,256]{2,1,0:T(8,128)(2,1)S(1)}, bf16[1,256,256]{2,1,0:T(8,128)(2,1)S(1)}, u32[]{:S(2)}, u32[]{:S(2)}) %collective-permute-start.21) | collective-permute-done | bytes 131104 | tf_op jit(solution)/shard_map/ppermute | solution.py:24
  63.1 2.9 %collective-permute-start.19 = (bf16[2,256,256]{2,1,0:T(8,128)(2,1)S(1)}, bf16[2,256,256]{2,1,0:T(8,128)(2,1)S(1)}, u32[]{:S(2)}, u32[]{:S(2)}) collective-permute-start(bf16[2,256,256]{2,1,0:T(8,128)(2,1)S(1)} %get-tuple-element.94), channel_id=1, source_target_pairs={{0,4},{2,6},{4,0},{6,2},{8,12},{10,14},{12,8},{14,10},{16,20},{18,... | collective-permute-start | bytes 786440 | tf_op jit(solution)/shard_map/ppermute | solution.py:24
  66.1 1.2 collective-permute-start.23
  67.3 4.7 %collective-permute-done.23.refs_4_ = bf16[1,256,256]{2,1,0:T(8,128)(2,1)S(1)} collective-permute-done((bf16[1,256,256]{2,1,0:T(8,128)(2,1)S(1)}, bf16[1,256,256]{2,1,0:T(8,128)(2,1)S(1)}, u32[]{:S(2)}, u32[]{:S(2)}) %collective-permute-start.23) | collective-permute-done | bytes 131104 | tf_op jit(solution)/shard_map/ppermute | solution.py:24
  72.1 4.3 %collective-permute-done.19.refs_3_ = bf16[2,256,256]{2,1,0:T(8,128)(2,1)S(1)} collective-permute-done((bf16[2,256,256]{2,1,0:T(8,128)(2,1)S(1)}, bf16[2,256,256]{2,1,0:T(8,128)(2,1)S(1)}, u32[]{:S(2)}, u32[]{:S(2)}) %collective-permute-start.19) | collective-permute-done | bytes 262176 | tf_op jit(solution)/shard_map/ppermute | solution.py:24
  77.1 3.3 %hidden.1 = (bf16[2,2,512,256]{3,2,1,0:T(8,128)(2,1)S(1)}, f32[2,2,512,256]{3,2,1,0:T(8,128)S(1)}, bf16[2,2,512,256]{3,2,1,0:T(8,128)(2,1)S(1)}, f32[2,2,512,256]{3,2,1,0:T(8,128)S(1)}) custom-call(s32[3]{0:T(128)S(1)} %pad_add_fusion.meta.refs_0_, bf16[256,512]{1,0:T(8,128)(2,1)S(1)} %copy-done.3, bf16[2,256,256]{2,1,0:T(8,128)(2,1)S(1)} %bitcast.26, ...), custom_call_target="tpu_custom_call" | custom-call | flops 536870912 | bytes 1310732 | tf_op jit(solution)/shard_map/hidden/pallas_call | solution.py:44
  80.4 2.3 %pre_grads.1 = (f32[512,256]{1,0:T(8,128)S(1)}, f32[512,256]{1,0:T(8,128)S(1)}, f32[256,256]{1,0:T(8,128)S(1)}, f32[8,256]{1,0:T(8,128)S(1)}) custom-call(s32[3]{0:T(128)S(1)} %pad_add_fusion.meta.refs_0_, bf16[512,256]{1,0:T(8,128)(2,1)S(1)} %copy-done.1, bf16[256,256]{1,0:T(8,128)(2,1)S(1)} %copy-done.2, ...), custom_call_target="tpu_custom_call" | custom-call | flops 1073741824 | bytes 6701068 | tf_op jit(solution)/shard_map/pre_grads/pallas_call | solution.py:44
  82.7 2.1 %collective-permute-done.24.refs_1_ = bf16[2,256,256]{2,1,0:T(8,128)(2,1)S(1)} collective-permute-done((bf16[2,256,256]{2,1,0:T(8,128)(2,1)S(1)}, bf16[2,256,256]{2,1,0:T(8,128)(2,1)S(1)}, u32[]{:S(2)}, u32[]{:S(2)}) %collective-permute-start.24) | collective-permute-done | bytes 262176 | tf_op jit(solution)/shard_map/ppermute | solution.py:24
  84.8 2.1 %post_grads.1 = (f32[640,256]{1,0:T(8,128)S(1)}, f32[648,256]{1,0:T(8,128)S(1)}) custom-call(s32[3]{0:T(128)S(1)} %pad_add_fusion.meta.refs_0_, bf16[512,256]{1,0:T(8,128)(2,1)S(1)} %copy-done.1, bf16[2,2,512,256]{3,2,1,0:T(8,128)(2,1)S(1)} %get-tuple-element.56.active_ref, f32[2,2,512,256]{3,2,1,0:T(8,128)S(1)} %get-tuple-element.57.slope_ref, ...), custom_call_target="tpu_custom_call" | custom-call | flops 1073741824 | bytes 5775372 | tf_op jit(solution)/shard_map/post_grads/pallas_call | solution.py:44
  87.0 2.1 %collective-permute-done.25.other_ref = f32[648,256]{1,0:T(8,128)S(1)} collective-permute-done((f32[648,256]{1,0:T(8,128)S(1)}, f32[648,256]{1,0:T(8,128)S(1)}, u32[]{:S(2)}, u32[]{:S(2)}) %collective-permute-start.25) | collective-permute-done | bytes 663584 | tf_op jit(solution)/shard_map/ppermute | solution.py:24
  89.7 16.6 %all_to_all.22 = bf16[8,80,256]{2,1,0:T(8,128)(2,1)S(1)} all-to-all(bf16[8,80,256]{2,1,0:T(8,128)(2,1)S(1)} %bitcast.32), channel_id=1, replica_groups={{0,4,8,12,16,20,24,28},{2,6,10,14,18,22,26,30},{1,5,9,13,17,21,25,29},{..., dimensions={0} | all-to-all | bytes 655360 | tf_op jit(solution)/shard_map/all_to_all | solution.py:550
  107.1 14.8 %all_to_all.23 = s16[8,96,256]{2,1,0:T(8,128)(2,1)S(1)} all-to-all(s16[8,96,256]{2,1,0:T(8,128)(2,1)S(1)} %bitcast.30), channel_id=1, replica_groups={{0,4,8,12,16,20,24,28},{2,6,10,14,18,22,26,30},{1,5,9,13,17,21,25,29},{..., dimensions={0} | all-to-all | bytes 786432 | tf_op jit(solution)/shard_map/all_to_all | solution.py:550
  121.9 1.7 %collective-permute-done.26.other_ref = s16[768,256]{1,0:T(8,128)(2,1)S(1)} collective-permute-done((s16[768,256]{1,0:T(8,128)(2,1)S(1)}, s16[768,256]{1,0:T(8,128)(2,1)S(1)}, u32[]{:S(2)}, u32[]{:S(2)}) %collective-permute-start.26) | collective-permute-done | bytes 393248 | tf_op jit(solution)/shard_map/ppermute | solution.py:24
  123.6 2.0 %last.1 = (f32[256,512]{1,0:T(8,128)}, f32[512,256]{1,0:T(8,128)}, f32[256,256]{1,0:T(8,128)}, f32[8,128]{1,0:T(8,128)S(1)}) custom-call(s32[3]{0:T(128)S(1)} %pad_add_fusion.meta.refs_0_, s16[768,256]{1,0:T(8,128)(2,1)S(1)} %bitcast.29, s16[768,256]{1,0:T(8,128)(2,1)S(1)} %collective-permute-done.26.other_ref), custom_call_target="tpu_custom_call" | custom-call | bytes 786444 | tf_op jit(solution)/shard_map/last/pallas_call | solution.py:44
  (61 shorter events, 10.0 us)
Async XLA Ops:
  0.6 19.4 %copy-start = (s32[16,2,512]{2,1,0:T(2,128)S(1)}, s32[16,2,512]{2,1,0:T(2,128)}, u32[]{:S(2)}) copy-start(s32[16,2,512]{2,1,0:T(2,128)} %param.10) | copy-start | bytes 196612
  0.6 7.4 %copy-start.3 = (bf16[256,512]{1,0:T(8,128)(2,1)S(1)}, bf16[256,512]{1,0:T(8,128)(2,1)}, u32[]{:S(2)}) copy-start(bf16[256,512]{1,0:T(8,128)(2,1)} %refs_0_.1) | copy-start | bytes 786436
  0.7 7.4 %copy-start.1 = (bf16[512,256]{1,0:T(8,128)(2,1)S(1)}, bf16[512,256]{1,0:T(8,128)(2,1)}, u32[]{:S(2)}) copy-start(bf16[512,256]{1,0:T(8,128)(2,1)} %w_out_ref.5) | copy-start | bytes 786436
  0.7 10.4 %collective-permute-start.2 = (bf16[256,512]{1,0:T(8,128)(2,1)}, bf16[256,512]{1,0:T(8,128)(2,1)S(1)}, u32[]{:S(2)}, u32[]{:S(2)}) collective-permute-start(bf16[256,512]{1,0:T(8,128)(2,1)} %refs_0_.1), channel_id=1, source_target_pairs={{0,1},{1,0},{2,3},{3,2},{4,5},{5,4},{6,7},{7,6},{8,9},{9,8},{10,11... | collective-permute-start | bytes 786440 | tf_op jit(solution)/shard_map/ppermute | solution.py:24
  3.7 13.0 %collective-permute-start.3 = (bf16[512,256]{1,0:T(8,128)(2,1)}, bf16[512,256]{1,0:T(8,128)(2,1)S(1)}, u32[]{:S(2)}, u32[]{:S(2)}) collective-permute-start(bf16[512,256]{1,0:T(8,128)(2,1)} %w_out_ref.5), channel_id=1, source_target_pairs={{0,1},{1,0},{2,3},{3,2},{4,5},{5,4},{6,7},{7,6},{8,9},{9,8},{10,11... | collective-permute-start | bytes 786440 | tf_op jit(solution)/shard_map/ppermute | solution.py:24
  5.9 14.1 %copy-start.4 = (s32[16,2,2]{0,2,1:T(2,128)S(1)}, s32[16,2,2]{0,2,1:T(2,128)}, u32[]{:S(2)}) copy-start(s32[16,2,2]{0,2,1:T(2,128)} %param.11) | copy-start | bytes 772
  5.9 17.8 %collective-permute-start = (bf16[2,256,256]{2,1,0:T(8,128)(2,1)S(1)}, bf16[2,256,256]{2,1,0:T(8,128)(2,1)S(1)}, u32[]{:S(2)}, u32[]{:S(2)}) collective-permute-start(bf16[2,256,256]{2,1,0:T(8,128)(2,1)S(1)} %bitcast.23), channel_id=1, source_target_pairs={{0,1},{1,0},{2,3},{3,2},{4,5},{5,4},{6,7},{7,6},{8,9},{9,8},{10,11... | collective-permute-start | bytes 786440 | tf_op jit(solution)/shard_map/ppermute | solution.py:24
  17.8 10.2 %copy-start.2 = (bf16[256,256]{1,0:T(8,128)(2,1)S(1)}, bf16[256,256]{1,0:T(8,128)(2,1)}, u32[]{:S(2)}) copy-start(bf16[256,256]{1,0:T(8,128)(2,1)} %bil_ref.1) | copy-start | bytes 393220
  17.9 10.2 %collective-permute-start.4 = (bf16[2,256,256]{2,1,0:T(8,128)(2,1)S(1)}, bf16[2,256,256]{2,1,0:T(8,128)(2,1)S(1)}, u32[]{:S(2)}, u32[]{:S(2)}) collective-permute-start(bf16[2,256,256]{2,1,0:T(8,128)(2,1)S(1)} %get-tuple-element.62.refs_6_), channel_id=1, source_target_pairs={{0,2},{2,0},{4,6},{6,4},{8,10},{10,8},{12,14},{14,12},{16,18},{18,... | collective-permute-start | bytes 786440 | tf_op jit(solution)/shard_map/ppermute | solution.py:24
  17.9 19.2 %collective-permute-start.1 = (bf16[2,256,256]{2,1,0:T(8,128)(2,1)S(1)}, bf16[2,256,256]{2,1,0:T(8,128)(2,1)S(1)}, u32[]{:S(2)}, u32[]{:S(2)}) collective-permute-start(bf16[2,256,256]{2,1,0:T(8,128)(2,1)S(1)} %bitcast.20), channel_id=1, source_target_pairs={{0,1},{1,0},{2,3},{3,2},{4,5},{5,4},{6,7},{7,6},{8,9},{9,8},{10,11... | collective-permute-start | bytes 786440 | tf_op jit(solution)/shard_map/ppermute | solution.py:24
  20.3 17.7 %collective-permute-start.6 = (bf16[2,256,256]{2,1,0:T(8,128)(2,1)S(1)}, bf16[2,256,256]{2,1,0:T(8,128)(2,1)S(1)}, u32[]{:S(2)}, u32[]{:S(2)}) collective-permute-start(bf16[2,256,256]{2,1,0:T(8,128)(2,1)S(1)} %get-tuple-element.62.refs_6_), channel_id=1, source_target_pairs={{0,4},{2,6},{4,0},{6,2},{8,12},{10,14},{12,8},{14,10},{16,20},{18,... | collective-permute-start | bytes 786440 | tf_op jit(solution)/shard_map/ppermute | solution.py:24
  21.9 16.2 %collective-permute-start.5 = (bf16[2,256,256]{2,1,0:T(8,128)(2,1)S(1)}, bf16[2,256,256]{2,1,0:T(8,128)(2,1)S(1)}, u32[]{:S(2)}, u32[]{:S(2)}) collective-permute-start(bf16[2,256,256]{2,1,0:T(8,128)(2,1)S(1)} %get-tuple-element.62.refs_6_), channel_id=1, source_target_pairs={{4,8},{6,10},{8,4},{10,6},{20,24},{22,26},{24,20},{26,22},{5,9},{7... | collective-permute-start | bytes 786440 | tf_op jit(solution)/shard_map/ppermute | solution.py:24
  23.7 19.5 %collective-permute-start.11 = (bf16[1,256,256]{2,1,0:T(8,128)(2,1)S(1)}, bf16[1,256,256]{2,1,0:T(8,128)(2,1)S(1)}, u32[]{:S(2)}, u32[]{:S(2)}) collective-permute-start(bf16[1,256,256]{2,1,0:T(8,128)(2,1)S(1)} %get-tuple-element.80), channel_id=1, source_target_pairs={{0,16},{2,18},{4,20},{6,22},{8,24},{10,26},{12,28},{14,30},{16,0},... | collective-permute-start | bytes 393224 | tf_op jit(solution)/shard_map/ppermute | solution.py:24
  33.1 10.4 %collective-permute-start.13 = (bf16[1,256,256]{2,1,0:T(8,128)(2,1)S(1)}, bf16[1,256,256]{2,1,0:T(8,128)(2,1)S(1)}, u32[]{:S(2)}, u32[]{:S(2)}) collective-permute-start(bf16[1,256,256]{2,1,0:T(8,128)(2,1)S(1)} %get-tuple-element.80), channel_id=1, source_target_pairs={{0,20},{2,22},{4,16},{6,18},{8,28},{10,30},{12,24},{14,26},{16,4},... | collective-permute-start | bytes 393224 | tf_op jit(solution)/shard_map/ppermute | solution.py:24
  37.2 6.3 %collective-permute-start.9 = (bf16[1,256,256]{2,1,0:T(8,128)(2,1)S(1)}, bf16[1,256,256]{2,1,0:T(8,128)(2,1)S(1)}, u32[]{:S(2)}, u32[]{:S(2)}) collective-permute-start(bf16[1,256,256]{2,1,0:T(8,128)(2,1)S(1)} %get-tuple-element.80), channel_id=1, source_target_pairs={{4,24},{6,26},{8,20},{10,22},{20,8},{22,10},{24,4},{26,6},{5,25},{... | collective-permute-start | bytes 393224 | tf_op jit(solution)/shard_map/ppermute | solution.py:24
  38.0 5.9 %collective-permute-start.7 = (bf16[2,256,256]{2,1,0:T(8,128)(2,1)S(1)}, bf16[2,256,256]{2,1,0:T(8,128)(2,1)S(1)}, u32[]{:S(2)}, u32[]{:S(2)}) collective-permute-start(bf16[2,256,256]{2,1,0:T(8,128)(2,1)S(1)} %collective-permute-done.5.refs_9_), channel_id=1, source_target_pairs={{0,2},{2,0},{4,6},{6,4},{8,10},{10,8},{12,14},{14,12},{16,18},{18,... | collective-permute-start | bytes 786440 | tf_op jit(solution)/shard_map/ppermute | solution.py:24
  38.1 5.9 %collective-permute-start.8 = (bf16[2,256,256]{2,1,0:T(8,128)(2,1)S(1)}, bf16[2,256,256]{2,1,0:T(8,128)(2,1)S(1)}, u32[]{:S(2)}, u32[]{:S(2)}) collective-permute-start(bf16[2,256,256]{2,1,0:T(8,128)(2,1)S(1)} %collective-permute-done.6.refs_10_), channel_id=1, source_target_pairs={{0,2},{2,0},{4,6},{6,4},{8,10},{10,8},{12,14},{14,12},{16,18},{18,... | collective-permute-start | bytes 786440 | tf_op jit(solution)/shard_map/ppermute | solution.py:24
  43.3 5.8 %collective-permute-start.12 = (bf16[1,256,256]{2,1,0:T(8,128)(2,1)S(1)}, bf16[1,256,256]{2,1,0:T(8,128)(2,1)S(1)}, u32[]{:S(2)}, u32[]{:S(2)}) collective-permute-start(bf16[1,256,256]{2,1,0:T(8,128)(2,1)S(1)} %collective-permute-done.11.refs_11_), channel_id=1, source_target_pairs={{0,2},{2,0},{4,6},{6,4},{8,10},{10,8},{12,14},{14,12},{16,18},{18,... | collective-permute-start | bytes 393224 | tf_op jit(solution)/shard_map/ppermute | solution.py:24
  43.5 5.6 %collective-permute-start.10 = (bf16[1,256,256]{2,1,0:T(8,128)(2,1)S(1)}, bf16[1,256,256]{2,1,0:T(8,128)(2,1)S(1)}, u32[]{:S(2)}, u32[]{:S(2)}) collective-permute-start(bf16[1,256,256]{2,1,0:T(8,128)(2,1)S(1)} %collective-permute-done.9.refs_9_), channel_id=1, source_target_pairs={{0,2},{2,0},{4,6},{6,4},{8,10},{10,8},{12,14},{14,12},{16,18},{18,... | collective-permute-start | bytes 393224 | tf_op jit(solution)/shard_map/ppermute | solution.py:24
  43.9 5.2 %collective-permute-start.14 = (bf16[1,256,256]{2,1,0:T(8,128)(2,1)S(1)}, bf16[1,256,256]{2,1,0:T(8,128)(2,1)S(1)}, u32[]{:S(2)}, u32[]{:S(2)}) collective-permute-start(bf16[1,256,256]{2,1,0:T(8,128)(2,1)S(1)} %collective-permute-done.13.refs_13_), channel_id=1, source_target_pairs={{0,2},{2,0},{4,6},{6,4},{8,10},{10,8},{12,14},{14,12},{16,18},{18,... | collective-permute-start | bytes 393224 | tf_op jit(solution)/shard_map/ppermute | solution.py:24
  48.6 11.1 %collective-permute-start.17 = (f32[4,256,256]{2,1,0:T(8,128)S(1)}, f32[4,256,256]{2,1,0:T(8,128)S(1)}, u32[]{:S(2)}, u32[]{:S(2)}) collective-permute-start(f32[4,256,256]{2,1,0:T(8,128)S(1)} %get-tuple-element.92), channel_id=1, source_target_pairs={{0,2},{2,0},{4,6},{6,4},{8,10},{10,8},{12,14},{14,12},{16,18},{18,... | collective-permute-start | bytes 3145736 | tf_op jit(solution)/shard_map/ppermute | solution.py:24
  53.0 2.4 %collective-permute-start.20 = (f32[3,256,256]{2,1,0:T(8,128)S(1)}, f32[3,256,256]{2,1,0:T(8,128)S(1)}, u32[]{:S(2)}, u32[]{:S(2)}) collective-permute-start(f32[3,256,256]{2,1,0:T(8,128)S(1)} %get-tuple-element.96), channel_id=1, source_target_pairs={{0,2},{2,0},{4,6},{6,4},{8,10},{10,8},{12,14},{14,12},{16,18},{18,... | collective-permute-start | bytes 2359304 | tf_op jit(solution)/shard_map/ppermute | solution.py:24
  53.2 27.3 %collective-permute-start.15 = (f32[1032,256]{1,0:T(8,128)S(1)}, f32[1032,256]{1,0:T(8,128)S(1)}, u32[]{:S(2)}, u32[]{:S(2)}) collective-permute-start(f32[1032,256]{1,0:T(8,128)S(1)} %get-tuple-element.84.refs_0_), channel_id=1, source_target_pairs={{0,1},{1,0},{2,3},{3,2},{4,5},{5,4},{6,7},{7,6},{8,9},{9,8},{10,11... | collective-permute-start | bytes 3170312 | tf_op jit(solution)/shard_map/ppermute | solution.py:24
  53.7 13.7 %collective-permute-start.16 = (f32[2,256,256]{2,1,0:T(8,128)S(1)}, f32[2,256,256]{2,1,0:T(8,128)S(1)}, u32[]{:S(2)}, u32[]{:S(2)}) collective-permute-start(f32[2,256,256]{2,1,0:T(8,128)S(1)} %get-tuple-element.90), channel_id=1, source_target_pairs={{0,2},{2,0},{4,6},{6,4},{8,10},{10,8},{12,14},{14,12},{16,18},{18,... | collective-permute-start | bytes 1572872 | tf_op jit(solution)/shard_map/ppermute | solution.py:24
  55.4 7.7 %collective-permute-start.21 = (bf16[1,256,256]{2,1,0:T(8,128)(2,1)S(1)}, bf16[1,256,256]{2,1,0:T(8,128)(2,1)S(1)}, u32[]{:S(2)}, u32[]{:S(2)}) collective-permute-start(bf16[1,256,256]{2,1,0:T(8,128)(2,1)S(1)} %get-tuple-element.98), channel_id=1, source_target_pairs={{0,4},{2,6},{4,0},{6,2},{8,12},{10,14},{12,8},{14,10},{16,20},{18,... | collective-permute-start | bytes 393224 | tf_op jit(solution)/shard_map/ppermute | solution.py:24
  59.1 7.0 %collective-permute-start.22 = (bf16[1,256,256]{2,1,0:T(8,128)(2,1)S(1)}, bf16[1,256,256]{2,1,0:T(8,128)(2,1)S(1)}, u32[]{:S(2)}, u32[]{:S(2)}) collective-permute-start(bf16[1,256,256]{2,1,0:T(8,128)(2,1)S(1)} %get-tuple-element.99), channel_id=1, source_target_pairs={{4,8},{6,10},{8,4},{10,6},{20,24},{22,26},{24,20},{26,22},{5,9},{7... | collective-permute-start | bytes 393224 | tf_op jit(solution)/shard_map/ppermute | solution.py:24
  59.9 12.2 %collective-permute-start.18 = (bf16[2,256,256]{2,1,0:T(8,128)(2,1)S(1)}, bf16[2,256,256]{2,1,0:T(8,128)(2,1)S(1)}, u32[]{:S(2)}, u32[]{:S(2)}) collective-permute-start(bf16[2,256,256]{2,1,0:T(8,128)(2,1)S(1)} %get-tuple-element.93), channel_id=1, source_target_pairs={{4,8},{6,10},{8,4},{10,6},{20,24},{22,26},{24,20},{26,22},{5,9},{7... | collective-permute-start | bytes 786440 | tf_op jit(solution)/shard_map/ppermute | solution.py:24
  63.1 13.3 %collective-permute-start.19 = (bf16[2,256,256]{2,1,0:T(8,128)(2,1)S(1)}, bf16[2,256,256]{2,1,0:T(8,128)(2,1)S(1)}, u32[]{:S(2)}, u32[]{:S(2)}) collective-permute-start(bf16[2,256,256]{2,1,0:T(8,128)(2,1)S(1)} %get-tuple-element.94), channel_id=1, source_target_pairs={{0,4},{2,6},{4,0},{6,2},{8,12},{10,14},{12,8},{14,10},{16,20},{18,... | collective-permute-start | bytes 786440 | tf_op jit(solution)/shard_map/ppermute | solution.py:24
  66.1 6.0 %collective-permute-start.23 = (bf16[1,256,256]{2,1,0:T(8,128)(2,1)S(1)}, bf16[1,256,256]{2,1,0:T(8,128)(2,1)S(1)}, u32[]{:S(2)}, u32[]{:S(2)}) collective-permute-start(bf16[1,256,256]{2,1,0:T(8,128)(2,1)S(1)} %side_sum.1), channel_id=1, source_target_pairs={{0,16},{2,18},{4,20},{6,22},{8,24},{10,26},{12,28},{14,30},{16,0},... | collective-permute-start | bytes 393224 | tf_op jit(solution)/shard_map/ppermute | solution.py:24
  76.5 8.3 %collective-permute-start.24 = (bf16[2,256,256]{2,1,0:T(8,128)(2,1)S(1)}, bf16[2,256,256]{2,1,0:T(8,128)(2,1)S(1)}, u32[]{:S(2)}, u32[]{:S(2)}) collective-permute-start(bf16[2,256,256]{2,1,0:T(8,128)(2,1)S(1)} %post_sum.1.refs_0_), channel_id=1, source_target_pairs={{0,1},{1,0},{2,3},{3,2},{4,5},{5,4},{6,7},{7,6},{8,9},{9,8},{10,11... | collective-permute-start | bytes 786440 | tf_op jit(solution)/shard_map/ppermute | solution.py:24
  86.9 2.2 %collective-permute-start.25 = (f32[648,256]{1,0:T(8,128)S(1)}, f32[648,256]{1,0:T(8,128)S(1)}, u32[]{:S(2)}, u32[]{:S(2)}) collective-permute-start(f32[648,256]{1,0:T(8,128)S(1)} %get-tuple-element.101), channel_id=1, source_target_pairs={{0,2},{2,0},{4,6},{6,4},{8,10},{10,8},{12,14},{14,12},{16,18},{18,... | collective-permute-start | bytes 1990664 | tf_op jit(solution)/shard_map/ppermute | solution.py:24
  121.9 1.7 %collective-permute-start.26 = (s16[768,256]{1,0:T(8,128)(2,1)S(1)}, s16[768,256]{1,0:T(8,128)(2,1)S(1)}, u32[]{:S(2)}, u32[]{:S(2)}) collective-permute-start(s16[768,256]{1,0:T(8,128)(2,1)S(1)} %bitcast.28), channel_id=1, source_target_pairs={{0,2},{2,0},{4,6},{6,4},{8,10},{10,8},{12,14},{14,12},{16,18},{18,... | collective-permute-start | bytes 1179656 | tf_op jit(solution)/shard_map/ppermute | solution.py:24

commit v4 on v3

--- a/solution.py
+++ b/solution.py
@@ -292,7 +292,7 @@
     j_own = lax.broadcasted_iota(jnp.int32, (rows, site_rows), 0)
     j_col = lax.broadcasted_iota(jnp.int32, (rows, 128), 0)
     i_row = lax.broadcasted_iota(jnp.int32, (1, site_rows), 1)
-    step = rows // (8 if rows >= 128 else 4)
+    step = rows // (32 if rows >= 128 else 4)
     i_ok = [i_row < count for count in pre_counts]
     if foreign:
         nz = sum(1 for dy, unused in slots if dy == 0)
@@ -330,7 +330,7 @@
                 targets.append(j_own == key)
             target = jnp.concatenate(targets, 0)
             s = dot(post, qt_ref[a]) + j_bias
-            e = jnp.exp(-jnp.abs(s))
+            e = jnp.exp2(jnp.abs(s) * -1.4426950408889634)
             w = 1.0 + e
             r = pl.reciprocal(w, approx=True)
             chance = jnp.where(s >= 0.0, r, e * r)

time: 126 us -> 126 us (level)
  no operation moved by 1% of the time
where the time goes in v4:
time: 126 us; the launch traced here: 125 us
  Pallas kernels  34.1 us (27%)
  blocking collectives  31.4 us (25%)
  starting transfers between devices  29.6 us (23%)
  waiting for transfers between devices  26.2 us (21%)
  local copies, waits for them, and re-layouts  2.94 us (2%)
    pallas_call x18, Pallas kernels, call(): pl.pallas_call(kernel, out_shape=[jax.ShapeDtypeStruct(shape, kind) for s...  34.1 us
    all_to_all x2, blocking collectives, to_chips(): lax.all_to_all(array, 'tile', 0, 0, tiled=True, axis_index_groups=same_core)  31.4 us
    ppermute x27, starting transfers between devices, moved(): return lax.ppermute(array, axis, pairs)  29.6 us
    ppermute x27, waiting for transfers between devices, moved(): return lax.ppermute(array, axis, pairs)  26.2 us
  transfers between devices with their start and end apart: 27, of which 10 were waited for; matrix products, arithmetic and copies ran while one was open for 2% of the time, Pallas kernels for 23%

profile of v4, /device:TPU:0, one launch (start us, length us, event | category | flops | bytes accessed | tf_op | source)
XLA Modules:
  0.0 125.2 jit_solution(3047313021855164876)
XLA Ops:
  0.7 3.0 %collective-permute-start.2 = (bf16[256,512]{1,0:T(8,128)(2,1)}, bf16[256,512]{1,0:T(8,128)(2,1)S(1)}, u32[]{:S(2)}, u32[]{:S(2)}) collective-permute-start(bf16[256,512]{1,0:T(8,128)(2,1)} %refs_0_.1), channel_id=1, source_target_pairs={{0,1},{1,0},{2,3},{3,2},{4,5},{5,4},{6,7},{7,6},{8,9},{9,8},{10,11... | collective-permute-start | bytes 786440 | tf_op jit(solution)/shard_map/ppermute | solution.py:24
  3.8 2.1 %fusion = (bf16[1,256,2,1,256]{4,3,2,1,0:T(2,128)(2,1)S(1)}, bf16[1,256,2,1,256]{4,3,2,1,0:T(2,128)(2,1)S(1)}) fusion(bf16[1,256,2,2,256]{4,3,2,1,0:T(2,128)(2,1)} %param.6), kind=kLoop, calls=%fused_computation.4 | loop fusion | bytes 1048576 | tf_op jit(solution)/shard_map/slice | solution.py:452
  5.9 2.0 %collective-permute-start = (bf16[2,256,256]{2,1,0:T(8,128)(2,1)S(1)}, bf16[2,256,256]{2,1,0:T(8,128)(2,1)S(1)}, u32[]{:S(2)}, u32[]{:S(2)}) collective-permute-start(bf16[2,256,256]{2,1,0:T(8,128)(2,1)S(1)} %bitcast.23), channel_id=1, source_target_pairs={{0,1},{1,0},{2,3},{3,2},{4,5},{5,4},{6,7},{7,6},{8,9},{9,8},{10,11... | collective-permute-start | bytes 786440 | tf_op jit(solution)/shard_map/ppermute | solution.py:24
  8.1 1.5 %mlp_own.1 = (f32[2,256,256]{2,1,0:T(8,128)S(1)}, f32[2,256,256]{2,1,0:T(8,128)S(1)}) custom-call(s32[3]{0:T(128)S(1)} %pad_add_fusion.meta.refs_0_, bf16[2,256,256]{2,1,0:T(8,128)(2,1)S(1)} %bitcast.24, bf16[2,256,256]{2,1,0:T(8,128)(2,1)S(1)} %bitcast.18, bf16[256,512]{1,0:T(8,128)(2,1)S(1)} %copy-done.3, bf16[512,256]{1,0:T(8,128)(2,1)S(1)} %copy-done.1), custom_call_target="tpu_custom_call" | custom-call | flops 536870912 | bytes 1048588 | tf_op jit(solution)/shard_map/mlp_own/pallas_call | solution.py:44
  9.6 1.5 %collective-permute-done.2.refs_1_.refs_2_ = bf16[256,512]{1,0:T(8,128)(2,1)S(1)} collective-permute-done((bf16[256,512]{1,0:T(8,128)(2,1)}, bf16[256,512]{1,0:T(8,128)(2,1)S(1)}, u32[]{:S(2)}, u32[]{:S(2)}) %collective-permute-start.2) | collective-permute-done | bytes 262176 | tf_op jit(solution)/shard_map/ppermute | solution.py:24
  11.0 5.6 %collective-permute-done.3.refs_2_.refs_3_ = bf16[512,256]{1,0:T(8,128)(2,1)S(1)} collective-permute-done((bf16[512,256]{1,0:T(8,128)(2,1)}, bf16[512,256]{1,0:T(8,128)(2,1)S(1)}, u32[]{:S(2)}, u32[]{:S(2)}) %collective-permute-start.3) | collective-permute-done | bytes 262176 | tf_op jit(solution)/shard_map/ppermute | solution.py:24
  16.7 1.2 mlp_post.1
  17.9 2.1 %collective-permute-start.1 = (bf16[2,256,256]{2,1,0:T(8,128)(2,1)S(1)}, bf16[2,256,256]{2,1,0:T(8,128)(2,1)S(1)}, u32[]{:S(2)}, u32[]{:S(2)}) collective-permute-start(bf16[2,256,256]{2,1,0:T(8,128)(2,1)S(1)} %bitcast.20), channel_id=1, source_target_pairs={{0,1},{1,0},{2,3},{3,2},{4,5},{5,4},{6,7},{7,6},{8,9},{9,8},{10,11... | collective-permute-start | bytes 786440 | tf_op jit(solution)/shard_map/ppermute | solution.py:24
  20.3 1.6 %collective-permute-start.6 = (bf16[2,256,256]{2,1,0:T(8,128)(2,1)S(1)}, bf16[2,256,256]{2,1,0:T(8,128)(2,1)S(1)}, u32[]{:S(2)}, u32[]{:S(2)}) collective-permute-start(bf16[2,256,256]{2,1,0:T(8,128)(2,1)S(1)} %get-tuple-element.62.refs_6_), channel_id=1, source_target_pairs={{0,4},{2,6},{4,0},{6,2},{8,12},{10,14},{12,8},{14,10},{16,20},{18,... | collective-permute-start | bytes 786440 | tf_op jit(solution)/shard_map/ppermute | solution.py:24
  22.5 1.2 mlp_pre.1.refs_4_.refs_2_
  23.7 2.7 %collective-permute-start.11 = (bf16[1,256,256]{2,1,0:T(8,128)(2,1)S(1)}, bf16[1,256,256]{2,1,0:T(8,128)(2,1)S(1)}, u32[]{:S(2)}, u32[]{:S(2)}) collective-permute-start(bf16[1,256,256]{2,1,0:T(8,128)(2,1)S(1)} %get-tuple-element.80), channel_id=1, source_target_pairs={{0,16},{2,18},{4,20},{6,22},{8,24},{10,26},{12,28},{14,30},{16,0},... | collective-permute-start | bytes 393224 | tf_op jit(solution)/shard_map/ppermute | solution.py:24
  26.4 1.6 %mlp_pre_other.1.refs_5_.refs_3_ = bf16[2,256,256]{2,1,0:T(8,128)(2,1)S(1)} custom-call(s32[3]{0:T(128)S(1)} %pad_add_fusion.meta.refs_0_, bf16[2,256,256]{2,1,0:T(8,128)(2,1)S(1)} %collective-permute-done.refs_1_.x_ref.refs_5_, bf16[256,512]{1,0:T(8,128)(2,1)S(1)} %copy-done.3, bf16[512,256]{1,0:T(8,128)(2,1)S(1)} %copy-done.1, ...), custom_call_target="tpu_custom_call" | custom-call | flops 536870912 | bytes 1310732 | tf_op jit(solution)/shard_map/mlp_pre_other/pallas_call | solution.py:44
  28.0 4.8 %pairs_own.1 = (f32[2,256,256]{2,1,0:T(8,128)S(1)}, f32[2,256,256]{2,1,0:T(8,128)S(1)}, bf16[2,512,256]{2,1,0:T(8,128)(2,1)S(1)}, bf16[2,256,512]{2,1,0:T(8,128)...) custom-call(s32[3]{0:T(128)S(1)} %pad_add_fusion.meta.refs_0_, ...), custom_call_target="tpu_custom_call" | custom-call | flops 10737418240 | bytes 1184012 | tf_op jit(solution)/shard_map/pairs_own/pallas_call | solution.py:44
  32.8 4.1 %collective-permute-start.13 = (bf16[1,256,256]{2,1,0:T(8,128)(2,1)S(1)}, bf16[1,256,256]{2,1,0:T(8,128)(2,1)S(1)}, u32[]{:S(2)}, u32[]{:S(2)}) collective-permute-start(bf16[1,256,256]{2,1,0:T(8,128)(2,1)S(1)} %get-tuple-element.80), channel_id=1, source_target_pairs={{0,20},{2,22},{4,16},{6,18},{8,28},{10,30},{12,24},{14,26},{16,4},... | collective-permute-start | bytes 393224 | tf_op jit(solution)/shard_map/ppermute | solution.py:24
  38.4 4.4 %pairs_near.1 = (f32[4,256,256]{2,1,0:T(8,128)S(1)}, f32[2,256,512]{2,1,0:T(8,128)S(1)}, f32[8,512]{1,0:T(8,128)S(1)}, f32[2,8,512]{2,1,0:T(8,128)S(1)}, f32[2,1,512]{2,1,0:T(1,128)S(1)}) custom-call(s32[3]{0:T(128)S(1)} %pad_add_fusion.meta.refs_0_, ...), custom_call_target="tpu_custom_call", output_to_operand_aliasing={{1}: (5, {}), {2}: (6, {}), {3}: (7, {}), {4}: (8, {})} | custom-call | flops 10737418240 | bytes 2679052 | tf_op jit(solution)/shard_map/pairs_near/pallas_call | solution.py:44
  43.7 4.4 %pairs_near_z.1 = (f32[4,256,256]{2,1,0:T(8,128)S(1)}, f32[2,256,512]{2,1,0:T(8,128)S(1)}, f32[8,512]{1,0:T(8,128)S(1)}, f32[2,8,512]{2,1,0:T(8,128)S(1)}, f32[2,1,512]{2,1,0:T(1,128)S(1)}) custom-call(s32[3]{0:T(128)S(1)} %pad_add_fusion.meta.refs_0_, ...), custom_call_target="tpu_custom_call", output_to_operand_aliasing={{1}: (5, {}), {2}: (6, {}), {3}: (7, {}), {4}: (8, {})} | custom-call | flops 10737418240 | bytes 2679052 | tf_op jit(solution)/shard_map/pairs_near_z/pallas_call | solution.py:44
  48.3 3.7 %pairs_far.1 = (f32[3,256,256]{2,1,0:T(8,128)S(1)}, f32[3,256,256]{2,1,0:T(8,128)S(1)}, f32[1032,256]{1,0:T(8,128)S(1)}) custom-call(s32[3]{0:T(128)S(1)} %pad_add_fusion.meta.refs_0_, s32[64]{0:T(128)S(1)} %reshape.16.refs_1_, s32[2,1,512]{2,1,0:T(1,128)S(1)} %broadcast_in_dim.3.refs_2_, bf16[2,512,256]{2,1,0:T(8,128)(2,1)S(1)} %get-tuple-element.63.refs_3_, ...), custom_call_target="tpu_custom_call" | custom-call | flops 8053063680 | bytes 2941196 | tf_op jit(solution)/shard_map/pairs_far/pallas_call | solution.py:44
  53.0 1.4 %collective-permute-done.20.refs_1_ = f32[3,256,256]{2,1,0:T(8,128)S(1)} collective-permute-done((f32[3,256,256]{2,1,0:T(8,128)S(1)}, f32[3,256,256]{2,1,0:T(8,128)S(1)}, u32[]{:S(2)}, u32[]{:S(2)}) %collective-permute-start.20) | collective-permute-done | bytes 786464 | tf_op jit(solution)/shard_map/ppermute | solution.py:24
  54.5 3.7 %collective-permute-start.21 = (bf16[1,256,256]{2,1,0:T(8,128)(2,1)S(1)}, bf16[1,256,256]{2,1,0:T(8,128)(2,1)S(1)}, u32[]{:S(2)}, u32[]{:S(2)}) collective-permute-start(bf16[1,256,256]{2,1,0:T(8,128)(2,1)S(1)} %get-tuple-element.98), channel_id=1, source_target_pairs={{0,4},{2,6},{4,0},{6,2},{8,12},{10,14},{12,8},{14,10},{16,20},{18,... | collective-permute-start | bytes 393224 | tf_op jit(solution)/shard_map/ppermute | solution.py:24
  59.9 2.3 %collective-permute-done.21.refs_1_ = bf16[1,256,256]{2,1,0:T(8,128)(2,1)S(1)} collective-permute-done((bf16[1,256,256]{2,1,0:T(8,128)(2,1)S(1)}, bf16[1,256,256]{2,1,0:T(8,128)(2,1)S(1)}, u32[]{:S(2)}, u32[]{:S(2)}) %collective-permute-start.21) | collective-permute-done | bytes 131104 | tf_op jit(solution)/shard_map/ppermute | solution.py:24
  62.2 3.2 %collective-permute-start.19 = (bf16[2,256,256]{2,1,0:T(8,128)(2,1)S(1)}, bf16[2,256,256]{2,1,0:T(8,128)(2,1)S(1)}, u32[]{:S(2)}, u32[]{:S(2)}) collective-permute-start(bf16[2,256,256]{2,1,0:T(8,128)(2,1)S(1)} %get-tuple-element.94), channel_id=1, source_target_pairs={{0,4},{2,6},{4,0},{6,2},{8,12},{10,14},{12,8},{14,10},{16,20},{18,... | collective-permute-start | bytes 786440 | tf_op jit(solution)/shard_map/ppermute | solution.py:24
  66.4 5.0 %collective-permute-done.23.refs_4_ = bf16[1,256,256]{2,1,0:T(8,128)(2,1)S(1)} collective-permute-done((bf16[1,256,256]{2,1,0:T(8,128)(2,1)S(1)}, bf16[1,256,256]{2,1,0:T(8,128)(2,1)S(1)}, u32[]{:S(2)}, u32[]{:S(2)}) %collective-permute-start.23) | collective-permute-done | bytes 131104 | tf_op jit(solution)/shard_map/ppermute | solution.py:24
  71.4 4.1 %collective-permute-done.19.refs_3_ = bf16[2,256,256]{2,1,0:T(8,128)(2,1)S(1)} collective-permute-done((bf16[2,256,256]{2,1,0:T(8,128)(2,1)S(1)}, bf16[2,256,256]{2,1,0:T(8,128)(2,1)S(1)}, u32[]{:S(2)}, u32[]{:S(2)}) %collective-permute-start.19) | collective-permute-done | bytes 262176 | tf_op jit(solution)/shard_map/ppermute | solution.py:24
  76.2 3.3 %hidden.1 = (bf16[2,2,512,256]{3,2,1,0:T(8,128)(2,1)S(1)}, f32[2,2,512,256]{3,2,1,0:T(8,128)S(1)}, bf16[2,2,512,256]{3,2,1,0:T(8,128)(2,1)S(1)}, f32[2,2,512,256]{3,2,1,0:T(8,128)S(1)}) custom-call(s32[3]{0:T(128)S(1)} %pad_add_fusion.meta.refs_0_, bf16[256,512]{1,0:T(8,128)(2,1)S(1)} %copy-done.3, bf16[2,256,256]{2,1,0:T(8,128)(2,1)S(1)} %bitcast.26, ...), custom_call_target="tpu_custom_call" | custom-call | flops 536870912 | bytes 1310732 | tf_op jit(solution)/shard_map/hidden/pallas_call | solution.py:44
  79.6 2.3 %pre_grads.1 = (f32[512,256]{1,0:T(8,128)S(1)}, f32[512,256]{1,0:T(8,128)S(1)}, f32[256,256]{1,0:T(8,128)S(1)}, f32[8,256]{1,0:T(8,128)S(1)}) custom-call(s32[3]{0:T(128)S(1)} %pad_add_fusion.meta.refs_0_, bf16[512,256]{1,0:T(8,128)(2,1)S(1)} %copy-done.1, bf16[256,256]{1,0:T(8,128)(2,1)S(1)} %copy-done.2, ...), custom_call_target="tpu_custom_call" | custom-call | flops 1073741824 | bytes 6701068 | tf_op jit(solution)/shard_map/pre_grads/pallas_call | solution.py:44
  81.8 2.1 %collective-permute-done.24.refs_1_ = bf16[2,256,256]{2,1,0:T(8,128)(2,1)S(1)} collective-permute-done((bf16[2,256,256]{2,1,0:T(8,128)(2,1)S(1)}, bf16[2,256,256]{2,1,0:T(8,128)(2,1)S(1)}, u32[]{:S(2)}, u32[]{:S(2)}) %collective-permute-start.24) | collective-permute-done | bytes 262176 | tf_op jit(solution)/shard_map/ppermute | solution.py:24
  83.9 2.1 %post_grads.1 = (f32[640,256]{1,0:T(8,128)S(1)}, f32[648,256]{1,0:T(8,128)S(1)}) custom-call(s32[3]{0:T(128)S(1)} %pad_add_fusion.meta.refs_0_, bf16[512,256]{1,0:T(8,128)(2,1)S(1)} %copy-done.1, bf16[2,2,512,256]{3,2,1,0:T(8,128)(2,1)S(1)} %get-tuple-element.56.active_ref, f32[2,2,512,256]{3,2,1,0:T(8,128)S(1)} %get-tuple-element.57.slope_ref, ...), custom_call_target="tpu_custom_call" | custom-call | flops 1073741824 | bytes 5775372 | tf_op jit(solution)/shard_map/post_grads/pallas_call | solution.py:44
  86.1 2.1 %collective-permute-done.25.other_ref = f32[648,256]{1,0:T(8,128)S(1)} collective-permute-done((f32[648,256]{1,0:T(8,128)S(1)}, f32[648,256]{1,0:T(8,128)S(1)}, u32[]{:S(2)}, u32[]{:S(2)}) %collective-permute-start.25) | collective-permute-done | bytes 663584 | tf_op jit(solution)/shard_map/ppermute | solution.py:24
  88.8 16.6 %all_to_all.22 = bf16[8,80,256]{2,1,0:T(8,128)(2,1)S(1)} all-to-all(bf16[8,80,256]{2,1,0:T(8,128)(2,1)S(1)} %bitcast.32), channel_id=1, replica_groups={{0,4,8,12,16,20,24,28},{2,6,10,14,18,22,26,30},{1,5,9,13,17,21,25,29},{..., dimensions={0} | all-to-all | bytes 655360 | tf_op jit(solution)/shard_map/all_to_all | solution.py:550
  106.2 14.8 %all_to_all.23 = s16[8,96,256]{2,1,0:T(8,128)(2,1)S(1)} all-to-all(s16[8,96,256]{2,1,0:T(8,128)(2,1)S(1)} %bitcast.30), channel_id=1, replica_groups={{0,4,8,12,16,20,24,28},{2,6,10,14,18,22,26,30},{1,5,9,13,17,21,25,29},{..., dimensions={0} | all-to-all | bytes 786432 | tf_op jit(solution)/shard_map/all_to_all | solution.py:550
  121.0 1.7 %collective-permute-done.26.other_ref = s16[768,256]{1,0:T(8,128)(2,1)S(1)} collective-permute-done((s16[768,256]{1,0:T(8,128)(2,1)S(1)}, s16[768,256]{1,0:T(8,128)(2,1)S(1)}, u32[]{:S(2)}, u32[]{:S(2)}) %collective-permute-start.26) | collective-permute-done | bytes 393248 | tf_op jit(solution)/shard_map/ppermute | solution.py:24
  122.7 2.0 %last.1 = (f32[256,512]{1,0:T(8,128)}, f32[512,256]{1,0:T(8,128)}, f32[256,256]{1,0:T(8,128)}, f32[8,128]{1,0:T(8,128)S(1)}) custom-call(s32[3]{0:T(128)S(1)} %pad_add_fusion.meta.refs_0_, s16[768,256]{1,0:T(8,128)(2,1)S(1)} %bitcast.29, s16[768,256]{1,0:T(8,128)(2,1)S(1)} %collective-permute-done.26.other_ref), custom_call_target="tpu_custom_call" | custom-call | bytes 786444 | tf_op jit(solution)/shard_map/last/pallas_call | solution.py:44
  (61 shorter events, 10.2 us)
Async XLA Ops:
  0.6 19.4 %copy-start = (s32[16,2,512]{2,1,0:T(2,128)S(1)}, s32[16,2,512]{2,1,0:T(2,128)}, u32[]{:S(2)}) copy-start(s32[16,2,512]{2,1,0:T(2,128)} %param.10) | copy-start | bytes 196612
  0.6 7.4 %copy-start.3 = (bf16[256,512]{1,0:T(8,128)(2,1)S(1)}, bf16[256,512]{1,0:T(8,128)(2,1)}, u32[]{:S(2)}) copy-start(bf16[256,512]{1,0:T(8,128)(2,1)} %refs_0_.1) | copy-start | bytes 786436
  0.7 7.4 %copy-start.1 = (bf16[512,256]{1,0:T(8,128)(2,1)S(1)}, bf16[512,256]{1,0:T(8,128)(2,1)}, u32[]{:S(2)}) copy-start(bf16[512,256]{1,0:T(8,128)(2,1)} %w_out_ref.5) | copy-start | bytes 786436
  0.7 10.4 %collective-permute-start.2 = (bf16[256,512]{1,0:T(8,128)(2,1)}, bf16[256,512]{1,0:T(8,128)(2,1)S(1)}, u32[]{:S(2)}, u32[]{:S(2)}) collective-permute-start(bf16[256,512]{1,0:T(8,128)(2,1)} %refs_0_.1), channel_id=1, source_target_pairs={{0,1},{1,0},{2,3},{3,2},{4,5},{5,4},{6,7},{7,6},{8,9},{9,8},{10,11... | collective-permute-start | bytes 786440 | tf_op jit(solution)/shard_map/ppermute | solution.py:24
  3.7 13.0 %collective-permute-start.3 = (bf16[512,256]{1,0:T(8,128)(2,1)}, bf16[512,256]{1,0:T(8,128)(2,1)S(1)}, u32[]{:S(2)}, u32[]{:S(2)}) collective-permute-start(bf16[512,256]{1,0:T(8,128)(2,1)} %w_out_ref.5), channel_id=1, source_target_pairs={{0,1},{1,0},{2,3},{3,2},{4,5},{5,4},{6,7},{7,6},{8,9},{9,8},{10,11... | collective-permute-start | bytes 786440 | tf_op jit(solution)/shard_map/ppermute | solution.py:24
  5.9 14.1 %copy-start.4 = (s32[16,2,2]{0,2,1:T(2,128)S(1)}, s32[16,2,2]{0,2,1:T(2,128)}, u32[]{:S(2)}) copy-start(s32[16,2,2]{0,2,1:T(2,128)} %param.11) | copy-start | bytes 772
  5.9 17.8 %collective-permute-start = (bf16[2,256,256]{2,1,0:T(8,128)(2,1)S(1)}, bf16[2,256,256]{2,1,0:T(8,128)(2,1)S(1)}, u32[]{:S(2)}, u32[]{:S(2)}) collective-permute-start(bf16[2,256,256]{2,1,0:T(8,128)(2,1)S(1)} %bitcast.23), channel_id=1, source_target_pairs={{0,1},{1,0},{2,3},{3,2},{4,5},{5,4},{6,7},{7,6},{8,9},{9,8},{10,11... | collective-permute-start | bytes 786440 | tf_op jit(solution)/shard_map/ppermute | solution.py:24
  17.8 10.2 %copy-start.2 = (bf16[256,256]{1,0:T(8,128)(2,1)S(1)}, bf16[256,256]{1,0:T(8,128)(2,1)}, u32[]{:S(2)}) copy-start(bf16[256,256]{1,0:T(8,128)(2,1)} %bil_ref.1) | copy-start | bytes 393220
  17.9 10.2 %collective-permute-start.4 = (bf16[2,256,256]{2,1,0:T(8,128)(2,1)S(1)}, bf16[2,256,256]{2,1,0:T(8,128)(2,1)S(1)}, u32[]{:S(2)}, u32[]{:S(2)}) collective-permute-start(bf16[2,256,256]{2,1,0:T(8,128)(2,1)S(1)} %get-tuple-element.62.refs_6_), channel_id=1, source_target_pairs={{0,2},{2,0},{4,6},{6,4},{8,10},{10,8},{12,14},{14,12},{16,18},{18,... | collective-permute-start | bytes 786440 | tf_op jit(solution)/shard_map/ppermute | solution.py:24
  17.9 19.0 %collective-permute-start.1 = (bf16[2,256,256]{2,1,0:T(8,128)(2,1)S(1)}, bf16[2,256,256]{2,1,0:T(8,128)(2,1)S(1)}, u32[]{:S(2)}, u32[]{:S(2)}) collective-permute-start(bf16[2,256,256]{2,1,0:T(8,128)(2,1)S(1)} %bitcast.20), channel_id=1, source_target_pairs={{0,1},{1,0},{2,3},{3,2},{4,5},{5,4},{6,7},{7,6},{8,9},{9,8},{10,11... | collective-permute-start | bytes 786440 | tf_op jit(solution)/shard_map/ppermute | solution.py:24
  20.3 17.5 %collective-permute-start.6 = (bf16[2,256,256]{2,1,0:T(8,128)(2,1)S(1)}, bf16[2,256,256]{2,1,0:T(8,128)(2,1)S(1)}, u32[]{:S(2)}, u32[]{:S(2)}) collective-permute-start(bf16[2,256,256]{2,1,0:T(8,128)(2,1)S(1)} %get-tuple-element.62.refs_6_), channel_id=1, source_target_pairs={{0,4},{2,6},{4,0},{6,2},{8,12},{10,14},{12,8},{14,10},{16,20},{18,... | collective-permute-start | bytes 786440 | tf_op jit(solution)/shard_map/ppermute | solution.py:24
  21.9 15.9 %collective-permute-start.5 = (bf16[2,256,256]{2,1,0:T(8,128)(2,1)S(1)}, bf16[2,256,256]{2,1,0:T(8,128)(2,1)S(1)}, u32[]{:S(2)}, u32[]{:S(2)}) collective-permute-start(bf16[2,256,256]{2,1,0:T(8,128)(2,1)S(1)} %get-tuple-element.62.refs_6_), channel_id=1, source_target_pairs={{4,8},{6,10},{8,4},{10,6},{20,24},{22,26},{24,20},{26,22},{5,9},{7... | collective-permute-start | bytes 786440 | tf_op jit(solution)/shard_map/ppermute | solution.py:24
  23.7 19.1 %collective-permute-start.11 = (bf16[1,256,256]{2,1,0:T(8,128)(2,1)S(1)}, bf16[1,256,256]{2,1,0:T(8,128)(2,1)S(1)}, u32[]{:S(2)}, u32[]{:S(2)}) collective-permute-start(bf16[1,256,256]{2,1,0:T(8,128)(2,1)S(1)} %get-tuple-element.80), channel_id=1, source_target_pairs={{0,16},{2,18},{4,20},{6,22},{8,24},{10,26},{12,28},{14,30},{16,0},... | collective-permute-start | bytes 393224 | tf_op jit(solution)/shard_map/ppermute | solution.py:24
  32.8 10.4 %collective-permute-start.13 = (bf16[1,256,256]{2,1,0:T(8,128)(2,1)S(1)}, bf16[1,256,256]{2,1,0:T(8,128)(2,1)S(1)}, u32[]{:S(2)}, u32[]{:S(2)}) collective-permute-start(bf16[1,256,256]{2,1,0:T(8,128)(2,1)S(1)} %get-tuple-element.80), channel_id=1, source_target_pairs={{0,20},{2,22},{4,16},{6,18},{8,28},{10,30},{12,24},{14,26},{16,4},... | collective-permute-start | bytes 393224 | tf_op jit(solution)/shard_map/ppermute | solution.py:24
  36.9 6.3 %collective-permute-start.9 = (bf16[1,256,256]{2,1,0:T(8,128)(2,1)S(1)}, bf16[1,256,256]{2,1,0:T(8,128)(2,1)S(1)}, u32[]{:S(2)}, u32[]{:S(2)}) collective-permute-start(bf16[1,256,256]{2,1,0:T(8,128)(2,1)S(1)} %get-tuple-element.80), channel_id=1, source_target_pairs={{4,24},{6,26},{8,20},{10,22},{20,8},{22,10},{24,4},{26,6},{5,25},{... | collective-permute-start | bytes 393224 | tf_op jit(solution)/shard_map/ppermute | solution.py:24
  37.8 5.9 %collective-permute-start.7 = (bf16[2,256,256]{2,1,0:T(8,128)(2,1)S(1)}, bf16[2,256,256]{2,1,0:T(8,128)(2,1)S(1)}, u32[]{:S(2)}, u32[]{:S(2)}) collective-permute-start(bf16[2,256,256]{2,1,0:T(8,128)(2,1)S(1)} %collective-permute-done.5.refs_9_), channel_id=1, source_target_pairs={{0,2},{2,0},{4,6},{6,4},{8,10},{10,8},{12,14},{14,12},{16,18},{18,... | collective-permute-start | bytes 786440 | tf_op jit(solution)/shard_map/ppermute | solution.py:24
  37.9 5.8 %collective-permute-start.8 = (bf16[2,256,256]{2,1,0:T(8,128)(2,1)S(1)}, bf16[2,256,256]{2,1,0:T(8,128)(2,1)S(1)}, u32[]{:S(2)}, u32[]{:S(2)}) collective-permute-start(bf16[2,256,256]{2,1,0:T(8,128)(2,1)S(1)} %collective-permute-done.6.refs_10_), channel_id=1, source_target_pairs={{0,2},{2,0},{4,6},{6,4},{8,10},{10,8},{12,14},{14,12},{16,18},{18,... | collective-permute-start | bytes 786440 | tf_op jit(solution)/shard_map/ppermute | solution.py:24
  42.8 5.5 %collective-permute-start.12 = (bf16[1,256,256]{2,1,0:T(8,128)(2,1)S(1)}, bf16[1,256,256]{2,1,0:T(8,128)(2,1)S(1)}, u32[]{:S(2)}, u32[]{:S(2)}) collective-permute-start(bf16[1,256,256]{2,1,0:T(8,128)(2,1)S(1)} %collective-permute-done.11.refs_11_), channel_id=1, source_target_pairs={{0,2},{2,0},{4,6},{6,4},{8,10},{10,8},{12,14},{14,12},{16,18},{18,... | collective-permute-start | bytes 393224 | tf_op jit(solution)/shard_map/ppermute | solution.py:24
  43.2 5.1 %collective-permute-start.10 = (bf16[1,256,256]{2,1,0:T(8,128)(2,1)S(1)}, bf16[1,256,256]{2,1,0:T(8,128)(2,1)S(1)}, u32[]{:S(2)}, u32[]{:S(2)}) collective-permute-start(bf16[1,256,256]{2,1,0:T(8,128)(2,1)S(1)} %collective-permute-done.9.refs_9_), channel_id=1, source_target_pairs={{0,2},{2,0},{4,6},{6,4},{8,10},{10,8},{12,14},{14,12},{16,18},{18,... | collective-permute-start | bytes 393224 | tf_op jit(solution)/shard_map/ppermute | solution.py:24
  43.4 5.0 %collective-permute-start.14 = (bf16[1,256,256]{2,1,0:T(8,128)(2,1)S(1)}, bf16[1,256,256]{2,1,0:T(8,128)(2,1)S(1)}, u32[]{:S(2)}, u32[]{:S(2)}) collective-permute-start(bf16[1,256,256]{2,1,0:T(8,128)(2,1)S(1)} %collective-permute-done.13.refs_13_), channel_id=1, source_target_pairs={{0,2},{2,0},{4,6},{6,4},{8,10},{10,8},{12,14},{14,12},{16,18},{18,... | collective-permute-start | bytes 393224 | tf_op jit(solution)/shard_map/ppermute | solution.py:24
  48.1 10.8 %collective-permute-start.17 = (f32[4,256,256]{2,1,0:T(8,128)S(1)}, f32[4,256,256]{2,1,0:T(8,128)S(1)}, u32[]{:S(2)}, u32[]{:S(2)}) collective-permute-start(f32[4,256,256]{2,1,0:T(8,128)S(1)} %get-tuple-element.92), channel_id=1, source_target_pairs={{0,2},{2,0},{4,6},{6,4},{8,10},{10,8},{12,14},{14,12},{16,18},{18,... | collective-permute-start | bytes 3145736 | tf_op jit(solution)/shard_map/ppermute | solution.py:24
  52.1 2.4 %collective-permute-start.20 = (f32[3,256,256]{2,1,0:T(8,128)S(1)}, f32[3,256,256]{2,1,0:T(8,128)S(1)}, u32[]{:S(2)}, u32[]{:S(2)}) collective-permute-start(f32[3,256,256]{2,1,0:T(8,128)S(1)} %get-tuple-element.96), channel_id=1, source_target_pairs={{0,2},{2,0},{4,6},{6,4},{8,10},{10,8},{12,14},{14,12},{16,18},{18,... | collective-permute-start | bytes 2359304 | tf_op jit(solution)/shard_map/ppermute | solution.py:24
  52.5 27.1 %collective-permute-start.15 = (f32[1032,256]{1,0:T(8,128)S(1)}, f32[1032,256]{1,0:T(8,128)S(1)}, u32[]{:S(2)}, u32[]{:S(2)}) collective-permute-start(f32[1032,256]{1,0:T(8,128)S(1)} %get-tuple-element.84.refs_0_), channel_id=1, source_target_pairs={{0,1},{1,0},{2,3},{3,2},{4,5},{5,4},{6,7},{7,6},{8,9},{9,8},{10,11... | collective-permute-start | bytes 3170312 | tf_op jit(solution)/shard_map/ppermute | solution.py:24
  53.0 13.4 %collective-permute-start.16 = (f32[2,256,256]{2,1,0:T(8,128)S(1)}, f32[2,256,256]{2,1,0:T(8,128)S(1)}, u32[]{:S(2)}, u32[]{:S(2)}) collective-permute-start(f32[2,256,256]{2,1,0:T(8,128)S(1)} %get-tuple-element.90), channel_id=1, source_target_pairs={{0,2},{2,0},{4,6},{6,4},{8,10},{10,8},{12,14},{14,12},{16,18},{18,... | collective-permute-start | bytes 1572872 | tf_op jit(solution)/shard_map/ppermute | solution.py:24
  54.5 7.7 %collective-permute-start.21 = (bf16[1,256,256]{2,1,0:T(8,128)(2,1)S(1)}, bf16[1,256,256]{2,1,0:T(8,128)(2,1)S(1)}, u32[]{:S(2)}, u32[]{:S(2)}) collective-permute-start(bf16[1,256,256]{2,1,0:T(8,128)(2,1)S(1)} %get-tuple-element.98), channel_id=1, source_target_pairs={{0,4},{2,6},{4,0},{6,2},{8,12},{10,14},{12,8},{14,10},{16,20},{18,... | collective-permute-start | bytes 393224 | tf_op jit(solution)/shard_map/ppermute | solution.py:24
  58.2 7.2 %collective-permute-start.22 = (bf16[1,256,256]{2,1,0:T(8,128)(2,1)S(1)}, bf16[1,256,256]{2,1,0:T(8,128)(2,1)S(1)}, u32[]{:S(2)}, u32[]{:S(2)}) collective-permute-start(bf16[1,256,256]{2,1,0:T(8,128)(2,1)S(1)} %get-tuple-element.99), channel_id=1, source_target_pairs={{4,8},{6,10},{8,4},{10,6},{20,24},{22,26},{24,20},{26,22},{5,9},{7... | collective-permute-start | bytes 393224 | tf_op jit(solution)/shard_map/ppermute | solution.py:24
  59.0 12.4 %collective-permute-start.18 = (bf16[2,256,256]{2,1,0:T(8,128)(2,1)S(1)}, bf16[2,256,256]{2,1,0:T(8,128)(2,1)S(1)}, u32[]{:S(2)}, u32[]{:S(2)}) collective-permute-start(bf16[2,256,256]{2,1,0:T(8,128)(2,1)S(1)} %get-tuple-element.93), channel_id=1, source_target_pairs={{4,8},{6,10},{8,4},{10,6},{20,24},{22,26},{24,20},{26,22},{5,9},{7... | collective-permute-start | bytes 786440 | tf_op jit(solution)/shard_map/ppermute | solution.py:24
  62.2 13.3 %collective-permute-start.19 = (bf16[2,256,256]{2,1,0:T(8,128)(2,1)S(1)}, bf16[2,256,256]{2,1,0:T(8,128)(2,1)S(1)}, u32[]{:S(2)}, u32[]{:S(2)}) collective-permute-start(bf16[2,256,256]{2,1,0:T(8,128)(2,1)S(1)} %get-tuple-element.94), channel_id=1, source_target_pairs={{0,4},{2,6},{4,0},{6,2},{8,12},{10,14},{12,8},{14,10},{16,20},{18,... | collective-permute-start | bytes 786440 | tf_op jit(solution)/shard_map/ppermute | solution.py:24
  65.4 6.0 %collective-permute-start.23 = (bf16[1,256,256]{2,1,0:T(8,128)(2,1)S(1)}, bf16[1,256,256]{2,1,0:T(8,128)(2,1)S(1)}, u32[]{:S(2)}, u32[]{:S(2)}) collective-permute-start(bf16[1,256,256]{2,1,0:T(8,128)(2,1)S(1)} %side_sum.1), channel_id=1, source_target_pairs={{0,16},{2,18},{4,20},{6,22},{8,24},{10,26},{12,28},{14,30},{16,0},... | collective-permute-start | bytes 393224 | tf_op jit(solution)/shard_map/ppermute | solution.py:24
  75.6 8.3 %collective-permute-start.24 = (bf16[2,256,256]{2,1,0:T(8,128)(2,1)S(1)}, bf16[2,256,256]{2,1,0:T(8,128)(2,1)S(1)}, u32[]{:S(2)}, u32[]{:S(2)}) collective-permute-start(bf16[2,256,256]{2,1,0:T(8,128)(2,1)S(1)} %post_sum.1.refs_0_), channel_id=1, source_target_pairs={{0,1},{1,0},{2,3},{3,2},{4,5},{5,4},{6,7},{7,6},{8,9},{9,8},{10,11... | collective-permute-start | bytes 786440 | tf_op jit(solution)/shard_map/ppermute | solution.py:24
  86.0 2.2 %collective-permute-start.25 = (f32[648,256]{1,0:T(8,128)S(1)}, f32[648,256]{1,0:T(8,128)S(1)}, u32[]{:S(2)}, u32[]{:S(2)}) collective-permute-start(f32[648,256]{1,0:T(8,128)S(1)} %get-tuple-element.101), channel_id=1, source_target_pairs={{0,2},{2,0},{4,6},{6,4},{8,10},{10,8},{12,14},{14,12},{16,18},{18,... | collective-permute-start | bytes 1990664 | tf_op jit(solution)/shard_map/ppermute | solution.py:24
  121.0 1.7 %collective-permute-start.26 = (s16[768,256]{1,0:T(8,128)(2,1)S(1)}, s16[768,256]{1,0:T(8,128)(2,1)S(1)}, u32[]{:S(2)}, u32[]{:S(2)}) collective-permute-start(s16[768,256]{1,0:T(8,128)(2,1)S(1)} %bitcast.28), channel_id=1, source_target_pairs={{0,2},{2,0},{4,6},{6,4},{8,10},{10,8},{12,14},{14,12},{16,18},{18,... | collective-permute-start | bytes 1179656 | tf_op jit(solution)/shard_map/ppermute | solution.py:24
